TPU v7x, 32 devices: a whole 2x2x4 slice. The times are simulated.
32 devices in a mesh: chan: 8 (over y, x, core), nbr: 4 (over z).
Axes of the slice: x: 2, y: 2, z: 4, core: 2. Of those that a mesh axis runs over, the one named last changes fastest.
Arguments:
- records: float32 [640, 28, 1280], P('chan', 'nbr'), may hold values from -112 to 112, as said below
- gap_mask: int32 [640, 28], P('chan', 'nbr'), may hold values from 0 to 1, as said below
- pair_list: int32 [8, 2, 8, 64], P('chan'), may hold values from 0 to 639, as said below
- pair_counts: int32 [8, 8], P('chan'), may hold values from 32 to 64, as said below
Outputs:
- correlations: float32 [8, 8, 64, 1024], P('chan', None, 'nbr')
Inputs may be any that keep to these rules, and one draw needn't show every extreme that they name: `records`: random floats of an unknown law; no structure is promised. `gap_mask`: entries are 0 or 1; some channels are silent in every segment. `pair_list`: the source channel lies in block b, and the receiver channel is 1 to 80 channels beyond it, below 640. Slots at or beyond the live count hold pairs of the same kind that no output uses. `pair_counts`: for one owner block, every source block fills all 64 slots.
All inputs are finite; a program needn't handle non-finite values.
Results may differ from a plain program's by a relative error of at most 0.0045.
Values may be sent and summed in bfloat16 or wider, within the bound.
No kernel may reach another device: no remote copies, remote signals or barrier semaphores. Data moves between devices by JAX's collectives and lax.ppermute only.
A program may use at most 192 MiB of HBM per device.

v0:
```python
import math

import jax
import jax.numpy as jnp
from jax import lax
from jax.sharding import PartitionSpec as P

NF = 256
NLAG = 1024


def passed_along(array, axis, by):
    length = lax.axis_size(axis)
    pairs = [(i, i + by) for i in range(length) if 0 <= i + by < length]
    return lax.ppermute(array, axis, pairs)


def passband_taper(bin_count):
    position = jnp.arange(bin_count, dtype=jnp.float32) + 1.0
    window = jnp.sin(math.pi * position / (bin_count + 1.0))
    return jnp.concatenate([window, window])


def forward_table(window_span, bin_count):
    clock_readings = jnp.arange(window_span, dtype=jnp.int32)
    probe_hertz = jnp.arange(bin_count, dtype=jnp.int32) + 1
    cycle_radians = (clock_readings[:, None] * probe_hertz[None, :] % window_span).astype(
        jnp.float32
    ) * (2.0 * math.pi / window_span)
    return jnp.concatenate([jnp.cos(cycle_radians), -jnp.sin(cycle_radians)], axis=1)


def inverse_table(bin_count, delay_total, window_span):
    probe_hertz = jnp.arange(bin_count, dtype=jnp.int32) + 1
    offsets = jnp.arange(delay_total, dtype=jnp.int32) - delay_total // 2
    cycle_radians = (probe_hertz[:, None] * offsets[None, :] % window_span).astype(jnp.float32) * (
        2.0 * math.pi / window_span
    )
    return jnp.concatenate([jnp.cos(cycle_radians), -jnp.sin(cycle_radians)], axis=0)


def to_lags(spectra, inverse):
    shape = spectra.shape
    flat = spectra.reshape(-1, shape[-1])
    traces = jnp.dot(
        flat, inverse, precision=lax.Precision.HIGHEST, preferred_element_type=jnp.float32
    )
    return traces.reshape(shape[:-1] + (inverse.shape[1],))


def local(records, gap_mask, pair_list, pair_counts):
    row_count, seg_count, window_span = records.shape
    block_count = pair_counts.shape[1]
    slot_count = pair_list.shape[3]
    spectrum = jnp.dot(
        records.reshape(row_count * seg_count, window_span),
        forward_table(window_span, NF),
        precision=lax.Precision.HIGHEST,
        preferred_element_type=jnp.float32,
    )
    energy = jnp.mean(spectrum * spectrum, axis=-1, keepdims=True)
    active = gap_mask.astype(jnp.float32).reshape(row_count * seg_count, 1)
    whitened = (spectrum * (active / jnp.sqrt(energy + 1e-05)) * passband_taper(NF)).astype(
        jnp.bfloat16
    )
    whitened = whitened.reshape(row_count, seg_count, 2 * NF)
    gap_marks = gap_mask.astype(jnp.bfloat16)
    next_white, next_marks = passed_along((whitened, gap_marks), "chan", -1)
    joined_white = jnp.concatenate([whitened, next_white], axis=0)
    joined_marks = jnp.concatenate([gap_marks, next_marks], axis=0).astype(jnp.float32)
    anchor = lax.axis_index("chan") * row_count
    source = (pair_list[0, 0] - anchor).reshape(-1)
    receiver = (pair_list[0, 1] - anchor).reshape(-1)
    slot_index = jnp.arange(slot_count, dtype=jnp.int32)
    usable = (slot_index[None, :] < pair_counts[0][:, None]).astype(jnp.float32).reshape(-1)
    source_rows = whitened[source].astype(jnp.float32)
    target_rows = joined_white[receiver].astype(jnp.float32)
    source_real, source_imag = (source_rows[..., :NF], source_rows[..., NF:])
    target_real, target_imag = (target_rows[..., :NF], target_rows[..., NF:])
    cross_real = jnp.sum(source_real * target_real + source_imag * target_imag, axis=1)
    cross_imag = jnp.sum(source_imag * target_real - source_real * target_imag, axis=1)
    cross = (jnp.concatenate([cross_real, cross_imag], axis=-1) * usable[:, None]).reshape(
        block_count, slot_count, 2 * NF
    )
    local_marks = gap_mask.astype(jnp.float32)
    intersection = (jnp.sum(local_marks[source] * joined_marks[receiver], axis=1) * usable).reshape(
        block_count, slot_count
    )
    inverse = inverse_table(NF, NLAG, window_span)
    partial_lags = to_lags(cross, inverse)
    summed, counted = (
        lax.psum_scatter(partial_lags, "nbr", scatter_dimension=1, tiled=True),
        lax.psum_scatter(intersection, "nbr", scatter_dimension=1, tiled=True),
    )
    traces = summed / jnp.maximum(counted, 1.0)[..., None]
    arrived = lax.all_to_all(traces, "chan", split_axis=0, concat_axis=0, tiled=True)
    return arrived[None]


def solution(mesh):
    return jax.shard_map(
        local,
        mesh=mesh,
        in_specs=(
            P("chan", "nbr", None),
            P("chan", "nbr"),
            P("chan", None, None, None),
            P("chan", None),
        ),
        out_specs=P("chan", None, "nbr", None),
        check_vma=False,
    )
```

profile of v0, /device:TPU:1, one launch (start us, length us, event | category | flops | bytes accessed | tf_op | source)
XLA Modules:
  0.0 138.2 jit_solution(9734129035887745050)
XLA Ops:
  6.6 6.5 %fusion.12 = (f32[1280,256]{1,0:T(8,128)}, f32[1280,256]{1,0:T(8,128)}) fusion(s32[256]{0:T(256)S(1)} %iota_add_fusion.1), kind=kLoop, calls=%fused_computation.23 | loop fusion | flops 3276800 | bytes 2622464 | tf_op jit(solution)/shard_map/cos | solution.py:30
  13.1 3.5 %copy.10 = f32[80,7,1280]{2,1,0:T(8,128)S(1)} copy(f32[80,7,1280]{2,0,1:T(8,128)} %param.4) | data formatting | bytes 5734400 | tf_op args[0]
  16.6 1.8 %reshape.110 = f32[560,1280]{1,0:T(8,128)} reshape(f32[80,7,1280]{2,1,0:T(8,128)S(1)} %copy.10) | data formatting | bytes 5734400 | tf_op jit(solution)/shard_map/reshape | solution.py:56
  18.4 0.1 copy.11
  18.5 0.1 reshape.111
  18.7 7.4 %multiply_reduce_fusion = (f32[560]{0:T(1024)S(1)}, f32[512,560]{0,1:T(8,128)S(1)}) fusion(f32[560,1280]{1,0:T(8,128)} %reshape.110, f32[1280,256]{1,0:T(8,128)} %get-tuple-element.12, f32[1280,256]{1,0:T(8,128)} %get-tuple-element.11), kind=kOutput, calls=%fused_computation.26 | convolution fusion | flops 4405247488 | bytes 6637760 | tf_op jit(solution)/shard_map/dot_general | solution.py:55
  26.1 0.2 fusion.22
  26.3 0.2 reshape.112
  26.5 1.0 copy.12
  27.5 2.0 %collective-permute-start = (bf16[80,7,512]{2,0,1:T(8,128)(2,1)}, bf16[80,7,512]{2,0,1:T(8,128)(2,1)S(1)}, u32[]{:S(2)}, u32[]{:S(2)}) collective-permute-start(bf16[80,7,512]{2,0,1:T(8,128)(2,1)} %copy.12), channel_id=1, source_target_pairs={{4,0},{8,4},{12,8},{16,12},{20,16},{24,20},{28,24},{5,1},{9,5},{13... | collective-permute-start | bytes 1720328 | tf_op jit(solution)/shard_map/ppermute | solution.py:15
  29.5 2.1 %collective-permute-start.1 = (bf16[80,7]{0,1:T(8,128)(2,1)S(1)}, bf16[80,7]{0,1:T(8,128)(2,1)S(1)}, u32[]{:S(2)}, u32[]{:S(2)}) collective-permute-start(bf16[80,7]{0,1:T(8,128)(2,1)S(1)} %convert_element_type.53), channel_id=1, source_target_pairs={{4,0},{8,4},{12,8},{16,12},{20,16},{24,20},{28,24},{5,1},{9,5},{13... | collective-permute-start | bytes 3368 | tf_op jit(solution)/shard_map/ppermute | solution.py:15
  31.8 5.3 %fusion.20 = (f32[256,1024]{1,0:T(8,128)S(1)}, f32[256,1024]{1,0:T(8,128)}) fusion(s32[1024]{0:T(1024)S(1)} %iota_add_fusion, s32[256]{0:T(256)S(1)} %iota_add_fusion.1), kind=kLoop, calls=%fused_computation.36 | loop fusion | flops 2621440 | bytes 2102272 | tf_op jit(solution)/shard_map/cos | solution.py:39
  37.2 3.5 %gather_fusion = bf16[512,7,512]{2,1,0:T(8,128)(2,1)} fusion(bf16[80,7,512]{2,1,0:T(8,128)(2,1)S(1)} %reshape.112, s32[1024]{0:T(1024)S(1)} %pad_clamp_fusion.1), kind=kCustom, calls=%fused_computation | custom fusion | bytes 7342080 | tf_op jit(solution)/shard_map/gather | solution.py:76
  40.7 1.0 gather_fusion.2
  41.7 6.6 %convert_element_type.48 = f32[512,7,512]{2,1,0:T(8,128)} convert(bf16[512,7,512]{2,1,0:T(8,128)(2,1)} %gather_fusion) | non-fusion elementwise | flops 1835008 | bytes 11010048 | tf_op jit(solution)/shard_map/convert_element_type | solution.py:76
  48.5 0.1 copy.14
  48.6 1.0 gather_fusion.3
  49.6 0.1 multiply_reduce_fusion.1
  49.8 0.1 reduce_sum.42
  49.9 0.7 copy.15
  50.7 0.3 copy.13
  51.1 0.3 pad_maximum_fusion
  51.3 3.5 %gather_fusion.1 = bf16[512,7,512]{2,1,0:T(8,128)(2,1)} fusion(bf16[160,7,512]{2,1,0:T(8,128)(2,1)S(1)} %pad_maximum_fusion, s32[1024]{0:T(1024)S(1)} %pad_clamp_fusion), kind=kCustom, calls=%fused_computation.1 | custom fusion | bytes 7342080 | tf_op jit(solution)/shard_map/gather | solution.py:77
  54.8 3.4 %convert_element_type.49 = f32[512,7,512]{2,1,0:T(8,128)S(1)} convert(bf16[512,7,512]{2,1,0:T(8,128)(2,1)} %gather_fusion.1) | non-fusion elementwise | flops 1835008 | bytes 11010048 | tf_op jit(solution)/shard_map/convert_element_type | solution.py:77
  58.2 5.7 %add_reduce_fusion = (f32[512,256]{1,0:T(8,128)S(1)}, f32[512,256]{1,0:T(8,128)S(1)}) fusion(f32[512,7,512]{2,1,0:T(8,128)S(1)} %convert_element_type.49, f32[512,7,512]{2,1,0:T(8,128)} %convert_element_type.48), kind=kLoop, calls=%fused_computation.5 | loop fusion | flops 7077888 | bytes 15728640 | tf_op jit(solution)/shard_map/reduce_sum | solution.py:80
  63.9 4.9 %fusion.4 = f32[512,1024]{1,0:T(8,128)} fusion(f32[256,1024]{1,0:T(8,128)S(1)} %copy-done, f32[256,1024]{1,0:T(8,128)S(1)} %get-tuple-element.9, f32[512,256]{1,0:T(8,128)S(1)} %get-tuple-element.6, f32[512,256]{1,0:T(8,128)S(1)} %get-tuple-element.5, f32[512]{0:T(512)S(1)} %reshape.114), kind=kOutput, calls=%fused_computation.10 | convolution fusion | flops 3222274048 | bytes 5244928 | tf_op jit(solution)/shard_map/dot_general | solution.py:45
  68.8 1.3 reduce-scatter.7.cloned.1.call-done
  70.2 0.8 copy.16
  70.9 45.8 %reduce-scatter.5.cloned.1.call-done = f32[8,16,1024]{2,1,0:T(8,128)} async-done(((f32[8,64,1024]{2,1,0:T(8,128)}), f32[8,16,1024]{2,1,0:T(8,128)}) %reduce-scatter.5.cloned.1.call-update) | async-done | bytes 524304 | tf_op jit(solution)/shard_map/reduce_scatter | solution.py:92
  116.7 1.1 broadcast_divide_fusion
  117.8 12.7 %all_to_all.5 = f32[8,16,1024]{2,1,0:T(8,128)S(1)} all-to-all(f32[8,16,1024]{2,1,0:T(8,128)S(1)} %broadcast_divide_fusion), channel_id=1, replica_groups=mesh['chan'=8,'nbr'=4] {'chan'}, dimensions={0} | all-to-all | bytes 1048576 | tf_op jit(solution)/shard_map/all_to_all | solution.py:96
  130.6 0.8 copy.18
  (33 shorter events, 0.7 us)
Async XLA Ops:
  6.5 63.6 %reduce-scatter.7.cloned.1.call-start = ((), (), s32[]{:S(2)}) async-start(), calls=%async_computation.4 | async-start | bytes 40960
  16.6 1.8 %copy-start.1 = (s32[80,7]{0,1:T(8,128)S(1)}, s32[80,7]{0,1:T(8,128)}, u32[]{:S(2)}) copy-start(s32[80,7]{0,1:T(8,128)} %param.5) | copy-start | bytes 6724
  26.1 5.5 %copy-start.2 = (s32[1,2,8,64]{3,2,1,0:T(8,128)S(1)}, s32[1,2,8,64]{3,2,1,0:T(8,128)}, u32[]{:S(2)}) copy-start(s32[1,2,8,64]{3,2,1,0:T(8,128)} %param.6) | copy-start | bytes 12292
  26.3 10.8 %copy-start.3 = (s32[1,8]{1,0:T(1,128)S(1)}, s32[1,8]{1,0:T(1,128)}, u32[]{:S(2)}) copy-start(s32[1,8]{1,0:T(1,128)} %param.7) | copy-start | bytes 100
  27.5 23.2 %collective-permute-start = (bf16[80,7,512]{2,0,1:T(8,128)(2,1)}, bf16[80,7,512]{2,0,1:T(8,128)(2,1)S(1)}, u32[]{:S(2)}, u32[]{:S(2)}) collective-permute-start(bf16[80,7,512]{2,0,1:T(8,128)(2,1)} %copy.12), channel_id=1, source_target_pairs={{4,0},{8,4},{12,8},{16,12},{20,16},{24,20},{28,24},{5,1},{9,5},{13... | collective-permute-start | bytes 1720328 | tf_op jit(solution)/shard_map/ppermute | solution.py:15
  29.5 18.9 %collective-permute-start.1 = (bf16[80,7]{0,1:T(8,128)(2,1)S(1)}, bf16[80,7]{0,1:T(8,128)(2,1)S(1)}, u32[]{:S(2)}, u32[]{:S(2)}) collective-permute-start(bf16[80,7]{0,1:T(8,128)(2,1)S(1)} %convert_element_type.53), channel_id=1, source_target_pairs={{4,0},{8,4},{12,8},{16,12},{20,16},{24,20},{28,24},{5,1},{9,5},{13... | collective-permute-start | bytes 3368 | tf_op jit(solution)/shard_map/ppermute | solution.py:15
  50.7 66.0 %reduce-scatter.5.cloned.1.call-start = ((), (), s32[]{:S(2)}) async-start(), calls=%async_computation.3 | async-start | bytes 2621440 | tf_op jit(solution)/shard_map/reduce_scatter | solution.py:92
  58.2 5.7 %copy-start = (f32[256,1024]{1,0:T(8,128)S(1)}, f32[256,1024]{1,0:T(8,128)}, u32[]{:S(2)}) copy-start(f32[256,1024]{1,0:T(8,128)} %get-tuple-element.10) | copy-start | bytes 3145732
Sparse Core Ops, SparseCore 0:
  50.8 19.3 reduce-scatter.6
  72.6 44.0 reduce-scatter.4
where the time goes:
time: 140 us; the launch traced here: 138 us
  waiting for transfers between devices  47.1 us (34%)
  other arithmetic  29.5 us (21%)
  local copies, waits for them, and re-layouts  18.8 us (13%)
  between operations  13.6 us (10%)
  blocking collectives  12.7 us (9%)
  matrix products  12.3 us (9%)
  starting transfers between devices  4.1 us (3%)
    reduce_scatter x1, waiting for transfers between devices, local(): lax.psum_scatter(partial_lags, 'nbr', scatter_dimension=1, tiled=True)  45.8 us
    all_to_all x1, blocking collectives, local(): lax.all_to_all(traces, 'chan', split_axis=0, concat_axis=0, tiled=True)  12.7 us
    dot_general x1, matrix products, local(): jnp.dot(records.reshape(row_count * seg_count, window_span), forward_tabl...  7.41 us
    convert_element_type x1, other arithmetic, local(): source_rows = whitened[source].astype(jnp.float32)  6.61 us
    cos x1, other arithmetic, forward_table(): jnp.cos(cycle_radians)  6.5 us
    unnamed x13, local copies, waits for them, and re-layouts  5.88 us
    reduce_sum x1, other arithmetic, local(): jnp.sum(source_real * target_real + source_imag * target_imag, axis=1)  5.66 us
    cos x1, other arithmetic, inverse_table(): jnp.cos(cycle_radians)  5.32 us
  transfers between devices with their start and end apart: 4, of which 2 were waited for; matrix products, arithmetic and copies ran while one was open for 27% of the time, Pallas kernels for 0%

commit v1 on v0

v1 whole, which is shorter than its diff:
```python
import functools
import math

import jax
import jax.numpy as jnp
import ml_dtypes
import numpy as np
from jax import lax
from jax.experimental import pallas as pl
from jax.experimental.pallas import tpu as pltpu
from jax.sharding import PartitionSpec as P

NF = 256
NLAG = 1024
LANES = 128
BF = jnp.bfloat16
F32 = jnp.float32
VMEM = pl.BlockSpec(memory_space=pltpu.VMEM)
SMEM = pl.BlockSpec(memory_space=pltpu.SMEM)

BINS = np.concatenate([np.arange(2, NF + 1, 2), np.arange(1, NF + 1, 2)])


def two_parts(table):
    high = table.astype(ml_dtypes.bfloat16)
    return high, (table - high.astype(np.float64)).astype(ml_dtypes.bfloat16)


def forward_tables(span):
    clock = np.arange(span // 2)[:, None]
    parts = []
    for bins in (BINS[: NF // 2], BINS[NF // 2 :]):
        angle = (clock * bins[None, :] % span) * (2.0 * math.pi / span)
        parts += two_parts(np.concatenate([np.cos(angle), -np.sin(angle)], axis=1))
    return np.concatenate(parts, axis=1)


def inverse_tables(span):
    lag = np.arange(NLAG)[None, :] - NLAG // 2
    angle = (BINS[:, None] * lag % span) * (2.0 * math.pi / span)
    return two_parts(np.concatenate([np.cos(angle), -np.sin(angle)], axis=0))


def taper():
    window = np.sin(math.pi * BINS / (NF + 1.0))
    return np.concatenate([window, window])[None, :].astype(np.float32)


def halves(value):
    high = value.astype(BF)
    return high, (value - high.astype(F32)).astype(BF)


def dot(a, b):
    return jnp.dot(a, b, preferred_element_type=F32)


def as_column(row):
    size = row.shape[1]
    shape = (size, size)
    same = lax.broadcasted_iota(jnp.int32, shape, 0) == lax.broadcasted_iota(jnp.int32, shape, 1)
    return jnp.sum(jnp.where(same, row, 0.0), axis=1, keepdims=True)


def whiten_kernel(x_ref, mark_ref, table_ref, taper_ref, out_ref):
    segs, rows, span = x_ref.shape
    half, quad = span // 2, NF // 2
    flags = jnp.concatenate(
        [as_column(mark_ref[s : s + 1, :].astype(F32)) for s in range(segs)], axis=0
    )
    low = x_ref[:, :, :half].reshape(segs * rows, half)
    high = x_ref[:, :, half:].reshape(segs * rows, half)
    found = []
    for i, folded in enumerate((low + high, low - high)):
        coarse, fine = halves(folded)
        table = table_ref[:, 2 * i * NF : (2 * i + 1) * NF]
        rest = table_ref[:, (2 * i + 1) * NF : (2 * i + 2) * NF]
        found.append(dot(coarse, table) + dot(fine, table) + dot(coarse, rest))
    even, odd = found
    energy = jnp.sum(even * even + odd * odd, axis=1, keepdims=True) * (0.5 / NF)
    factor = flags / jnp.sqrt(energy + 1e-05)
    for place, part in enumerate((even[:, :quad], odd[:, :quad], even[:, quad:], odd[:, quad:])):
        columns = slice(place * quad, (place + 1) * quad)
        white = (part * factor * taper_ref[:, columns]).astype(BF)
        out_ref[:, :, columns] = white.reshape(segs, rows, quad)


def pairs_kernel(
    step, white_ref, next_ref, mark_ref, next_mark_ref, list_ref, count_ref, out_ref, source, receiver
):
    segs, rows, width = white_ref.shape
    owners, slots = list_ref.shape[2:]
    dests, _, _ = out_ref.shape
    per = owners * slots // dests
    anchor = lax.axis_index("chan") * rows
    for o in range(owners):
        live = lax.broadcasted_iota(jnp.int32, (1, slots), 1) < count_ref[0, o]
        first = jnp.where(live, list_ref[0, 0, o : o + 1, :] - anchor, -1).astype(F32)
        second = (list_ref[0, 1, o : o + 1, :] - anchor).astype(F32)
        spots = lax.broadcasted_iota(jnp.int32, (slots, rows), 1).astype(F32)
        where = slice(o * slots, (o + 1) * slots)
        source[where, :] = (spots == as_column(first)).astype(BF)
        column = as_column(second)
        receiver[0, where, :] = (spots == column).astype(BF)
        receiver[1, where, :] = (spots == column - rows).astype(BF)
    marks = mark_ref[...].astype(BF)
    next_marks = next_mark_ref[...].astype(BF)
    across = (((1,), (1,)), ((), ()))

    def body(i, carry):
        at = pl.ds(pl.multiple_of(i * step, step), step)
        src, own, nxt = source[at, :], receiver[0, at, :], receiver[1, at, :]
        real = jnp.zeros((step, NF), F32)
        imag = jnp.zeros((step, NF), F32)
        for s in range(segs):
            a = dot(src, white_ref[s])
            b = dot(own, white_ref[s]) + dot(nxt, next_ref[s])
            real += a[:, :NF] * b[:, :NF] + a[:, NF:] * b[:, NF:]
            imag += a[:, NF:] * b[:, :NF] - a[:, :NF] * b[:, NF:]
        both = lax.dot_general(src, marks, across, preferred_element_type=F32) * (
            lax.dot_general(own, marks, across, preferred_element_type=F32)
            + lax.dot_general(nxt, next_marks, across, preferred_element_type=F32)
        )
        shared = jnp.sum(both, axis=1, keepdims=True)
        to = pl.ds(i * (step // per), step // per)
        for block in range(2 * NF // LANES):
            part = (real, imag)[block // 2][:, (block % 2) * LANES : (block % 2 + 1) * LANES]
            out_ref[to, block * per : (block + 1) * per, :] = part.astype(BF).reshape(-1, per, LANES)
        shared = jnp.broadcast_to(shared, (step, LANES)).reshape(-1, per, LANES)
        tail = shared[:, :8, :]
        lane = lax.broadcasted_iota(jnp.int32, tail.shape, 2)
        for k in range(1, per // 8):
            tail = jnp.where(lane >= k * 8 * LANES // per, shared[:, 8 * k : 8 * k + 8, :], tail)
        out_ref[to, 2 * NF // LANES * per :, :] = tail.astype(BF)
        return carry

    lax.fori_loop(0, owners * slots // step, body, 0)


def lags_kernel(parts, per, x_ref, high_ref, low_ref, out_ref):
    dests, length, _ = x_ref.shape
    blocks = 2 * NF // LANES
    total = jnp.sum(x_ref[...].astype(F32).reshape(dests // parts, parts, length, LANES), axis=1)
    scale = 1.0 / jnp.maximum(total[:, blocks * per :, :], 1.0)
    scale = jnp.concatenate(
        [scale[:, :, k * 8 * LANES // per :][:, :, :1] for k in range(per // 8)], axis=1
    )
    stacked = jnp.concatenate(
        [
            (total[:, k * per : (k + 1) * per, :] * scale).reshape(-1, LANES)
            for k in range(blocks)
        ],
        axis=1,
    )
    coarse, fine = halves(stacked)
    traces = dot(coarse, high_ref[...]) + dot(fine, high_ref[...]) + dot(coarse, low_ref[...])
    out_ref[...] = traces.reshape(out_ref.shape)


def call(kernel, shape, args, specs, scratch=(), mib=24):
    return pl.pallas_call(
        kernel,
        out_shape=shape,
        in_specs=specs,
        out_specs=VMEM,
        scratch_shapes=list(scratch),
        compiler_params=pltpu.CompilerParams(vmem_limit_bytes=mib << 20),
    )(*args)


def local(records, gap_mask, pair_list, pair_counts):
    rows, segs, span = records.shape
    owners, slots = pair_list.shape[2:]
    chan, nbr = lax.axis_size("chan"), lax.axis_size("nbr")
    per = slots // nbr
    pairs = owners * slots
    back = [(i, i - 1) for i in range(1, chan)]
    marks = gap_mask.T
    white = call(
        whiten_kernel,
        jax.ShapeDtypeStruct((segs, rows, 2 * NF), BF),
        (jnp.transpose(records, (1, 0, 2)), marks, jnp.asarray(forward_tables(span)), jnp.asarray(taper())),
        [VMEM] * 4,
    )
    next_white = lax.ppermute(white, "chan", back)
    next_marks = lax.ppermute(marks, "chan", back)
    cross = call(
        functools.partial(pairs_kernel, min(256, pairs)),
        jax.ShapeDtypeStruct((chan * nbr, 2 * NF // LANES * per + 8, LANES), BF),
        (white, next_white, marks, next_marks, pair_list, pair_counts),
        [VMEM] * 5 + [SMEM],
        [pltpu.VMEM((pairs, rows), BF), pltpu.VMEM((2, pairs, rows), BF)],
    )
    arrived = lax.all_to_all(cross, ("chan", "nbr"), split_axis=0, concat_axis=0, tiled=True)
    high, low = inverse_tables(span)
    traces = call(
        functools.partial(lags_kernel, nbr, per),
        jax.ShapeDtypeStruct((chan, per, NLAG), F32),
        (arrived, jnp.asarray(high), jnp.asarray(low)),
        [VMEM] * 3,
        mib=32,
    )
    return traces[None]


def solution(mesh):
    return jax.shard_map(
        local,
        mesh=mesh,
        in_specs=(
            P("chan", "nbr", None),
            P("chan", "nbr"),
            P("chan", None, None, None),
            P("chan", None),
        ),
        out_specs=P("chan", None, "nbr", None),
        check_vma=False,
    )
```

time: 140 us -> 46.9 us (0.33); the launches traced: 138 us -> 46.6 us
  waiting for transfers between devices: 47.1 us -> 8.04 us
  other arithmetic: 29.5 us -> 0 us
  local copies, waits for them, and re-layouts: 18.8 us -> 4.52 us
  between operations: 13.6 us -> 0.04 us
  matrix products: 12.3 us -> 0 us
  blocking collectives: 12.7 us -> 22.1 us
  Pallas kernels: 0 us -> 8.01 us
    reduce_scatter x1 -> x0, waiting for transfers between devices: 45.8 us -> none  [local(): lax.psum_scatter(partial_lags, 'nbr', scatter_dimension=1, tiled=True)]
    dot_general x2 -> x0, matrix products: 12.3 us -> none  [the longest x1 7.41 us: local(): jnp.dot(records.reshape(row_count * seg_count, window_span), forward_tabl...]
    cos x2 -> x0, other arithmetic: 11.8 us -> none  [the longest x1 6.5 us: forward_table(): jnp.cos(cycle_radians)]
    convert_element_type x7 -> x0, other arithmetic: 10.3 us -> none  [the longest x1 6.61 us: local(): source_rows = whitened[source].astype(jnp.float32)]
    all_to_all x1, blocking collectives: 12.7 us -> 22.1 us  [local(): lax.all_to_all(cross, ('chan', 'nbr'), split_axis=0, concat_axis=0, tiled...]
    gather x4 -> x0, local copies, waits for them, and re-layouts: 9.03 us -> none  [the longest x1 3.48 us: local(): target_rows = joined_white[receiver].astype(jnp.float32)]
    ppermute x2, waiting for transfers between devices: 0.01 us -> 8.04 us  [the longest x1 8.04 us: local(): next_marks = lax.ppermute(marks, 'chan', back)]
    pallas_call x0 -> x3, Pallas kernels: none -> 8.01 us  [call(): pl.pallas_call(kernel, out_shape=shape, in_specs=specs, out_specs=VMEM, s...]
  transfers between devices with their start and end apart: 4 -> 2, of which waited for: 2 -> 1; matrix products, arithmetic and copies ran while one was open for 27% -> 0% of each run, Pallas kernels for 0% -> 0%
where the time goes in v1:
time: 46.9 us; the launch traced here: 46.6 us
  blocking collectives  22.1 us (47%)
  waiting for transfers between devices  8.04 us (17%)
  Pallas kernels  8.01 us (17%)
  local copies, waits for them, and re-layouts  4.52 us (10%)
  starting transfers between devices  3.88 us (8%)
    all_to_all x1, blocking collectives, local(): lax.all_to_all(cross, ('chan', 'nbr'), split_axis=0, concat_axis=0, tiled...  22.1 us
    ppermute x1, waiting for transfers between devices, local(): next_marks = lax.ppermute(marks, 'chan', back)  8.04 us
    pallas_call x3, Pallas kernels, call(): pl.pallas_call(kernel, out_shape=shape, in_specs=specs, out_specs=VMEM, s...  8.01 us
    unnamed x16, local copies, waits for them, and re-layouts  4.52 us
    ppermute x1, starting transfers between devices, local(): next_white = lax.ppermute(white, 'chan', back)  1.96 us
    ppermute x1, starting transfers between devices, local(): next_marks = lax.ppermute(marks, 'chan', back)  1.92 us
  transfers between devices with their start and end apart: 2, of which 1 were waited for; matrix products, arithmetic and copies ran while one was open for 0% of the time, Pallas kernels for 0%

profile of v1, /device:TPU:1, one launch (start us, length us, event | category | flops | bytes accessed | tf_op | source)
XLA Modules:
  0.0 46.6 jit_solution(11120581839970094040)
XLA Ops:
  0.0 0.0 copy-start.7
  0.0 0.0 copy-start
  0.0 1.8 %copy-done = f32[80,7,1280]{2,0,1:T(8,128)S(1)} copy-done((f32[80,7,1280]{2,0,1:T(8,128)S(1)}, f32[80,7,1280]{2,0,1:T(8,128)}, u32[]{:S(2)}) %copy-start) | copy-done | bytes 2867224
  1.8 0.0 copy-start.1
  1.8 1.3 %copy-done.1 = bf16[640,1024]{1,0:T(8,128)(2,1)S(1)} copy-done((bf16[640,1024]{1,0:T(8,128)(2,1)S(1)}, bf16[640,1024]{1,0:T(8,128)(2,1)}, u32[]{:S(2)}) %copy-start.1) | copy-done | bytes 1310744
  3.1 0.0 copy-start.4
  3.1 0.7 %copy-done.4 = s32[80,7]{0,1:T(8,128)S(1)} copy-done((s32[80,7]{0,1:T(8,128)S(1)}, s32[80,7]{0,1:T(8,128)}, u32[]{:S(2)}) %copy-start.4) | copy-done | bytes 2264
  3.8 0.0 copy-start.6
  3.8 0.7 %copy-done.6 = f32[1,512]{1,0:T(1,128)S(1)} copy-done((f32[1,512]{1,0:T(1,128)S(1)}, f32[1,512]{1,0:T(1,128)}, u32[]{:S(2)}) %copy-start.6) | copy-done | bytes 2072
  4.5 0.0 copy-start.5
  4.5 0.0 copy-start.2
  4.5 0.0 copy-start.3
  4.5 2.0 %shard_map.82.white_ref = bf16[7,80,512]{2,1,0:T(8,128)(2,1)S(1)} custom-call(f32[7,80,1280]{2,1,0:T(8,128)S(1)} %bitcast.3, s32[7,80]{1,0:T(8,128)S(1)} %bitcast.4, bf16[640,1024]{1,0:T(8,128)(2,1)S(1)} %copy-done.1, f32[1,512]{1,0:T(1,128)S(1)} %copy-done.6), custom_call_target="tpu_custom_call" | custom-call | tf_op jit(solution)/shard_map/pallas_call | solution.py:161
  6.5 2.0 %collective-permute-start = (bf16[7,80,512]{2,1,0:T(8,128)(2,1)S(1)}, bf16[7,80,512]{2,1,0:T(8,128)(2,1)S(1)}, u32[]{:S(2)}, u32[]{:S(2)}) collective-permute-start(bf16[7,80,512]{2,1,0:T(8,128)(2,1)S(1)} %shard_map.82.white_ref), channel_id=1, source_target_pairs={{4,0},{8,4},{12,8},{16,12},{20,16},{24,20},{28,24},{5,1},{9,5},{13... | collective-permute-start | bytes 1720328 | tf_op jit(solution)/shard_map/ppermute | solution.py:185
  8.5 1.9 %collective-permute-start.1 = (s32[7,80]{1,0:T(8,128)S(1)}, s32[7,80]{1,0:T(8,128)S(1)}, u32[]{:S(2)}, u32[]{:S(2)}) collective-permute-start(s32[7,80]{1,0:T(8,128)S(1)} %bitcast.5), channel_id=1, source_target_pairs={{4,0},{8,4},{12,8},{16,12},{20,16},{24,20},{28,24},{5,1},{9,5},{13... | collective-permute-start | bytes 6728 | tf_op jit(solution)/shard_map/ppermute | solution.py:186
  10.4 8.0 %collective-permute-done.1.next_mark_ref = s32[7,80]{1,0:T(8,128)S(1)} collective-permute-done((s32[7,80]{1,0:T(8,128)S(1)}, s32[7,80]{1,0:T(8,128)S(1)}, u32[]{:S(2)}, u32[]{:S(2)}) %collective-permute-start.1) | collective-permute-done | bytes 2272 | tf_op jit(solution)/shard_map/ppermute | solution.py:186
  18.5 0.0 collective-permute-done.next_ref
  18.5 0.0 copy-done.7
  18.5 0.0 copy-done.5
  18.5 4.5 %shard_map.83 = bf16[32,72,128]{2,1,0:T(8,128)(2,1)S(1)} custom-call(bf16[7,80,512]{2,1,0:T(8,128)(2,1)S(1)} %shard_map.82.white_ref, bf16[7,80,512]{2,1,0:T(8,128)(2,1)S(1)} %collective-permute-done.next_ref, s32[7,80]{1,0:T(8,128)S(1)} %bitcast.6, s32[7,80]{1,0:T(8,128)S(1)} %collective-permute-done.1.next_mark_ref, s32[1,2,8,64]{3,2,1,0:T(8,128)S(1)} %copy-done.5, ...), custom_call_target="tpu_custom_call" | custom-call | tf_op jit(solution)/shard_map/pallas_call | solution.py:161
  23.0 22.1 %all_to_all.5.x_ref = bf16[32,72,128]{2,1,0:T(8,128)(2,1)S(1)} all-to-all(bf16[32,72,128]{2,1,0:T(8,128)(2,1)S(1)} %shard_map.83), channel_id=1, replica_groups=mesh['chan'=8,'nbr'=4] {'chan','nbr'}, dimensions={0} | all-to-all | bytes 1179648 | tf_op jit(solution)/shard_map/all_to_all | solution.py:194
  45.1 0.0 copy-done.2
  45.1 0.0 copy-done.3
  45.1 1.5 %shard_map.84 = f32[8,16,1024]{2,1,0:T(8,128)} custom-call(bf16[32,72,128]{2,1,0:T(8,128)(2,1)S(1)} %all_to_all.5.x_ref, bf16[512,1024]{1,0:T(8,128)(2,1)S(1)} %copy-done.3, bf16[512,1024]{1,0:T(8,128)(2,1)S(1)} %copy-done.2), custom_call_target="tpu_custom_call" | custom-call | tf_op jit(solution)/shard_map/pallas_call | solution.py:161
Async XLA Ops:
  0.0 18.5 %copy-start.7 = (s32[1,8]{1,0:T(1,128)S(1)}, s32[1,8]{1,0:T(1,128)}, u32[]{:S(2)}) copy-start(s32[1,8]{1,0:T(1,128)} %count_ref.1) | copy-start | bytes 100
  0.0 1.8 %copy-start = (f32[80,7,1280]{2,0,1:T(8,128)S(1)}, f32[80,7,1280]{2,0,1:T(8,128)}, u32[]{:S(2)}) copy-start(f32[80,7,1280]{2,0,1:T(8,128)} %param.8) | copy-start | bytes 8601604
  1.8 1.3 %copy-start.1 = (bf16[640,1024]{1,0:T(8,128)(2,1)S(1)}, bf16[640,1024]{1,0:T(8,128)(2,1)}, u32[]{:S(2)}) copy-start(bf16[640,1024]{1,0:T(8,128)(2,1)} %constant.8.clone.table_ref) | copy-start | bytes 3932164
  3.1 0.7 %copy-start.4 = (s32[80,7]{0,1:T(8,128)S(1)}, s32[80,7]{0,1:T(8,128)}, u32[]{:S(2)}) copy-start(s32[80,7]{0,1:T(8,128)} %param.9) | copy-start | bytes 6724
  3.8 0.7 %copy-start.6 = (f32[1,512]{1,0:T(1,128)S(1)}, f32[1,512]{1,0:T(1,128)}, u32[]{:S(2)}) copy-start(f32[1,512]{1,0:T(1,128)} %constant.9.clone.taper_ref) | copy-start | bytes 6148
  4.5 13.9 %copy-start.5 = (s32[1,2,8,64]{3,2,1,0:T(8,128)S(1)}, s32[1,2,8,64]{3,2,1,0:T(8,128)}, u32[]{:S(2)}) copy-start(s32[1,2,8,64]{3,2,1,0:T(8,128)} %list_ref.1) | copy-start | bytes 12292
  4.5 40.6 %copy-start.2 = (bf16[512,1024]{1,0:T(8,128)(2,1)S(1)}, bf16[512,1024]{1,0:T(8,128)(2,1)}, u32[]{:S(2)}) copy-start(bf16[512,1024]{1,0:T(8,128)(2,1)} %constant.11.clone.low_ref) | copy-start | bytes 3145732
  4.5 40.6 %copy-start.3 = (bf16[512,1024]{1,0:T(8,128)(2,1)S(1)}, bf16[512,1024]{1,0:T(8,128)(2,1)}, u32[]{:S(2)}) copy-start(bf16[512,1024]{1,0:T(8,128)(2,1)} %constant.10.clone.high_ref) | copy-start | bytes 3145732
  6.5 11.9 %collective-permute-start = (bf16[7,80,512]{2,1,0:T(8,128)(2,1)S(1)}, bf16[7,80,512]{2,1,0:T(8,128)(2,1)S(1)}, u32[]{:S(2)}, u32[]{:S(2)}) collective-permute-start(bf16[7,80,512]{2,1,0:T(8,128)(2,1)S(1)} %shard_map.82.white_ref), channel_id=1, source_target_pairs={{4,0},{8,4},{12,8},{16,12},{20,16},{24,20},{28,24},{5,1},{9,5},{13... | collective-permute-start | bytes 1720328 | tf_op jit(solution)/shard_map/ppermute | solution.py:185
  8.5 10.0 %collective-permute-start.1 = (s32[7,80]{1,0:T(8,128)S(1)}, s32[7,80]{1,0:T(8,128)S(1)}, u32[]{:S(2)}, u32[]{:S(2)}) collective-permute-start(s32[7,80]{1,0:T(8,128)S(1)} %bitcast.5), channel_id=1, source_target_pairs={{4,0},{8,4},{12,8},{16,12},{20,16},{24,20},{28,24},{5,1},{9,5},{13... | collective-permute-start | bytes 6728 | tf_op jit(solution)/shard_map/ppermute | solution.py:186

commit v2 on v1

v2 whole, which is shorter than its diff:
```python
import functools
import math

import jax
import jax.numpy as jnp
import ml_dtypes
import numpy as np
from jax import lax
from jax.experimental import pallas as pl
from jax.experimental.pallas import tpu as pltpu
from jax.sharding import PartitionSpec as P

NF = 256
NLAG = 1024
LANES = 128
BF = jnp.bfloat16
F32 = jnp.float32
VMEM = pl.BlockSpec(memory_space=pltpu.VMEM)
HBM = pl.BlockSpec(memory_space=pltpu.HBM)
SMEM = pl.BlockSpec(memory_space=pltpu.SMEM)

EVEN, ODD = np.arange(2, NF + 1, 2), np.arange(1, NF + 1, 2)
FIRST = 3
STEP = 128


def two_parts(table):
    high = table.astype(ml_dtypes.bfloat16)
    return high, (table - high.astype(np.float64)).astype(ml_dtypes.bfloat16)


def forward_tables(span):
    clock = np.arange(span // 2)[:, None]
    parts = []
    for bins in (EVEN, ODD):
        angle = (clock * bins[None, :] % span) * (2.0 * math.pi / span)
        parts += two_parts(np.concatenate([np.cos(angle), -np.sin(angle)], axis=1))
    return np.stack(parts)


def inverse_tables(span):
    lag = np.arange(NLAG)[None, :] - NLAG // 2
    rows = []
    for bins in (EVEN, ODD):
        angle = (bins[:, None] * lag % span) * (2.0 * math.pi / span)
        rows += [np.cos(angle), -np.sin(angle)]
    return two_parts(np.concatenate(rows, axis=0))


def taper():
    window = np.sin(math.pi * np.concatenate([EVEN, EVEN, ODD, ODD]) / (NF + 1.0))
    return window[None, :].astype(np.float32)


def halves(value):
    high = value.astype(BF)
    return high, (value - high.astype(F32)).astype(BF)


def dot(a, b):
    return jnp.dot(a, b, preferred_element_type=F32)


def dot_across(a, b):
    return lax.dot_general(a, b, (((1,), (1,)), ((), ())), preferred_element_type=F32)


def as_column(row):
    size = row.shape[1]
    shape = (size, size)
    same = lax.broadcasted_iota(jnp.int32, shape, 0) == lax.broadcasted_iota(jnp.int32, shape, 1)
    return jnp.sum(jnp.where(same, row, 0.0), axis=1, keepdims=True)


def whiten(x_ref, flags, table_ref, taper_ref, out_ref, ready):
    segs, rows, span = x_ref.shape
    half = span // 2
    low = x_ref[:, :, :half].reshape(segs * rows, half)
    high = x_ref[:, :, half:].reshape(segs * rows, half)
    found = []
    for i, folded in enumerate((low + high, low - high)):
        coarse, fine = halves(folded)
        ready(i)
        found.append(
            dot(coarse, table_ref[2 * i]) + dot(fine, table_ref[2 * i]) + dot(coarse, table_ref[2 * i + 1])
        )
    even, odd = found
    energy = jnp.sum(even * even + odd * odd, axis=1, keepdims=True) * (0.5 / NF)
    factor = flags / jnp.sqrt(energy + 1e-05)
    for i, part in enumerate(found):
        columns = slice(i * NF, (i + 1) * NF)
        white = (part * factor * taper_ref[:, columns]).astype(BF)
        out_ref[:, :, columns] = white.reshape(segs, rows, NF)


def flag_columns(mark_ref, segs):
    return jnp.concatenate([as_column(mark_ref[s : s + 1, :].astype(F32)) for s in segs], axis=0)


def first_kernel(x_hbm, mark_hbm, table_hbm, taper_hbm, out_ref, rest_ref, mark_ref, table_ref, taper_ref, x, sem):
    count, total = x.shape[0], x_hbm.shape[0]
    copies = [
        pltpu.make_async_copy(mark_hbm, mark_ref, sem.at[0]),
        pltpu.make_async_copy(taper_hbm, taper_ref, sem.at[1]),
        pltpu.make_async_copy(x_hbm.at[pl.ds(0, count)], x, sem.at[2]),
        pltpu.make_async_copy(table_hbm.at[pl.ds(0, 2)], table_ref.at[pl.ds(0, 2)], sem.at[3]),
        pltpu.make_async_copy(table_hbm.at[pl.ds(2, 2)], table_ref.at[pl.ds(2, 2)], sem.at[4]),
        pltpu.make_async_copy(x_hbm.at[pl.ds(count, total - count)], rest_ref, sem.at[5]),
    ]
    for copy in copies:
        copy.start()
    for copy in copies[:3]:
        copy.wait()
    flags = flag_columns(mark_ref, range(count))
    whiten(x, flags, table_ref, taper_ref, out_ref, lambda i: copies[3 + i].wait())
    copies[5].wait()


def second_kernel(x_ref, mark_ref, table_ref, taper_ref, out_ref, mark_out):
    mark_out[...] = mark_ref[...]
    total = mark_ref.shape[0]
    flags = flag_columns(mark_ref, range(total - x_ref.shape[0], total))
    whiten(x_ref, flags, table_ref, taper_ref, out_ref, lambda i: None)


def add_products(real, imag, a, b):
    quad = NF // 2
    ar, ai, br, bi = a[:, :quad], a[:, quad:], b[:, :quad], b[:, quad:]
    return real + (ar * br + ai * bi), imag + (ai * br - ar * bi)


def sources_kernel(
    step, early_ref, late_ref, mark_ref, list_ref, count_ref,
    source_ref, sum_ref, next_ref, source_mark_ref, own_mark_ref, first, own,
):
    rows = early_ref.shape[1]
    owners, slots = list_ref.shape[2:]
    quad = NF // 2
    anchor = lax.axis_index("chan") * rows
    spots = lax.broadcasted_iota(jnp.int32, (slots, rows), 1).astype(F32)
    for o in range(owners):
        live = lax.broadcasted_iota(jnp.int32, (1, slots), 1) < count_ref[0, o]
        where = slice(o * slots, (o + 1) * slots)
        column = as_column(jnp.where(live, list_ref[0, 0, o : o + 1, :] - anchor, -1).astype(F32))
        first[where, :] = (spots == column).astype(BF)
        column = as_column((list_ref[0, 1, o : o + 1, :] - anchor).astype(F32))
        own[where, :] = (spots == column).astype(BF)
        next_ref[where, :] = (spots == column - rows).astype(BF)
    marks = mark_ref[...].astype(BF)

    def body(i, carry):
        at = pl.ds(pl.multiple_of(i * step, step), step)
        a_hot, b_hot = first[at, :], own[at, :]
        source_mark_ref[at, :] = dot_across(a_hot, marks)
        own_mark_ref[at, :] = dot_across(b_hot, marks)
        for h in range(2):
            columns = slice(h * NF, (h + 1) * NF)
            real = imag = jnp.zeros((step, quad), F32)
            seg = 0
            for ref in (early_ref, late_ref):
                for s in range(ref.shape[0]):
                    a = dot(a_hot, ref[s, :, columns])
                    source_ref[seg, at, columns] = a.astype(BF)
                    real, imag = add_products(real, imag, a, dot(b_hot, ref[s, :, columns]))
                    seg += 1
            sum_ref[at, h * NF : h * NF + quad] = real
            sum_ref[at, h * NF + quad : (h + 1) * NF] = imag
        return carry

    lax.fori_loop(0, owners * slots // step, body, 0)


def add_segments(at, base, white_ref, source_ref, hot, sums):
    quad = NF // 2
    result = []
    for h in range(2):
        columns = slice(h * NF, (h + 1) * NF)
        real, imag = sums[at, h * NF : h * NF + quad], sums[at, h * NF + quad : (h + 1) * NF]
        for s in range(white_ref.shape[0]):
            a = source_ref[base + s, at, columns].astype(F32)
            real, imag = add_products(real, imag, a, dot(hot, white_ref[s, :, columns]))
        result += [real, imag]
    return result


def early_kernel(step, white_ref, source_ref, next_ref, sum_ref, out_ref):
    quad = NF // 2

    def body(i, carry):
        at = pl.ds(pl.multiple_of(i * step, step), step)
        for k, part in enumerate(add_segments(at, 0, white_ref, source_ref, next_ref[at, :], sum_ref)):
            out_ref[at, k * quad : (k + 1) * quad] = part
        return carry

    lax.fori_loop(0, sum_ref.shape[0] // step, body, 0)


def late_kernel(
    step, base, white_ref, source_ref, next_ref, sum_ref, source_mark_ref, own_mark_ref, next_mark_ref, out_ref
):
    pairs = sum_ref.shape[0]
    per = pairs // out_ref.shape[0]
    next_marks = next_mark_ref[...].astype(BF)

    def body(i, carry):
        at = pl.ds(pl.multiple_of(i * step, step), step)
        to = pl.ds(i * (step // per), step // per)
        hot = next_ref[at, :]
        for k, part in enumerate(add_segments(at, base, white_ref, source_ref, hot, sum_ref)):
            out_ref[to, k * per : (k + 1) * per, :] = part.astype(BF).reshape(-1, per, LANES)
        both = source_mark_ref[at, :] * (own_mark_ref[at, :] + dot_across(hot, next_marks))
        shared = jnp.broadcast_to(jnp.sum(both, axis=1, keepdims=True), (step, LANES)).reshape(-1, per, LANES)
        tail = shared[:, :8, :]
        lane = lax.broadcasted_iota(jnp.int32, tail.shape, 2)
        for k in range(1, per // 8):
            tail = jnp.where(lane >= k * 8 * LANES // per, shared[:, 8 * k : 8 * k + 8, :], tail)
        out_ref[to, 2 * NF // LANES * per :, :] = tail.astype(BF)
        return carry

    lax.fori_loop(0, pairs // step, body, 0)


def lags_kernel(parts, per, x_ref, high_ref, low_ref, out_ref):
    dests, length, _ = x_ref.shape
    blocks = 2 * NF // LANES
    total = jnp.sum(x_ref[...].astype(F32).reshape(dests // parts, parts, length, LANES), axis=1)
    scale = 1.0 / jnp.maximum(total[:, blocks * per :, :], 1.0)
    scale = jnp.concatenate(
        [scale[:, :, k * 8 * LANES // per :][:, :, :1] for k in range(per // 8)], axis=1
    )
    stacked = jnp.concatenate(
        [
            (total[:, k * per : (k + 1) * per, :] * scale).reshape(-1, LANES)
            for k in range(blocks)
        ],
        axis=1,
    )
    coarse, fine = halves(stacked)
    traces = dot(coarse, high_ref[...]) + dot(fine, high_ref[...]) + dot(coarse, low_ref[...])
    out_ref[...] = traces.reshape(out_ref.shape)


def call(kernel, shape, args, specs, scratch=(), mib=24, cost=None):
    return pl.pallas_call(
        kernel,
        out_shape=shape,
        in_specs=specs,
        out_specs=[VMEM] * len(shape),
        scratch_shapes=list(scratch),
        compiler_params=pltpu.CompilerParams(vmem_limit_bytes=mib << 20),
        cost_estimate=cost,
    )(*args)


def local(records, gap_mask, pair_list, pair_counts):
    rows, segs, span = records.shape
    owners, slots = pair_list.shape[2:]
    chan, nbr = lax.axis_size("chan"), lax.axis_size("nbr")
    per = slots // nbr
    pairs = owners * slots
    step = min(STEP, pairs)
    width = 2 * NF
    back = [(i, i - 1) for i in range(1, chan)]
    shape = jax.ShapeDtypeStruct
    tables = jnp.asarray(forward_tables(span))
    early, rest, marks, tables, window = call(
        first_kernel,
        [
            shape((FIRST, rows, width), BF),
            shape((segs - FIRST, rows, span), F32),
            shape((segs, rows), jnp.int32),
            shape(tables.shape, BF),
            shape((1, width), F32),
        ],
        [pltpu.with_memory_space_constraint(v, pltpu.HBM) for v in (jnp.transpose(records, (1, 0, 2)), gap_mask.T, tables, jnp.asarray(taper()))],
        [HBM] * 4,
        [pltpu.VMEM((FIRST, rows, span), F32), pltpu.SemaphoreType.DMA((6,))],
    )
    next_early = lax.ppermute(early, "chan", back)
    late, marks = call(
        second_kernel,
        [shape((segs - FIRST, rows, width), BF), shape((segs, rows), jnp.int32)],
        (rest, marks, tables, window),
        [VMEM] * 4,
        cost=pl.CostEstimate(flops=1000, bytes_accessed=1000, transcendentals=0),
    )
    next_late = lax.ppermute(late, "chan", back)
    next_marks = lax.ppermute(marks, "chan", back)
    source, sums, hot, source_marks, own_marks = call(
        functools.partial(sources_kernel, step),
        [
            shape((segs, pairs, width), BF),
            shape((pairs, width), F32),
            shape((pairs, rows), BF),
            shape((pairs, segs), F32),
            shape((pairs, segs), F32),
        ],
        (early, late, marks, pair_list, pair_counts),
        [VMEM] * 4 + [SMEM],
        [pltpu.VMEM((pairs, rows), BF), pltpu.VMEM((pairs, rows), BF)],
        mib=40,
        cost=pl.CostEstimate(flops=1000, bytes_accessed=1000, transcendentals=0),
    )
    (sums,) = call(
        functools.partial(early_kernel, step),
        [shape((pairs, width), F32)],
        (next_early, source, hot, sums),
        [VMEM] * 4,
        mib=40,
    )
    (cross,) = call(
        functools.partial(late_kernel, step, FIRST),
        [shape((chan * nbr, width // LANES * per + 8, LANES), BF)],
        (next_late, source, hot, sums, source_marks, own_marks, next_marks),
        [VMEM] * 7,
        mib=40,
    )
    arrived = lax.all_to_all(cross, ("chan", "nbr"), split_axis=0, concat_axis=0, tiled=True)
    high, low = inverse_tables(span)
    (traces,) = call(
        functools.partial(lags_kernel, nbr, per),
        [shape((chan, per, NLAG), F32)],
        (arrived, jnp.asarray(high), jnp.asarray(low)),
        [VMEM] * 3,
    )
    return traces[None]


def solution(mesh):
    return jax.shard_map(
        local,
        mesh=mesh,
        in_specs=(
            P("chan", "nbr", None),
            P("chan", "nbr"),
            P("chan", None, None, None),
            P("chan", None),
        ),
        out_specs=P("chan", None, "nbr", None),
        check_vma=False,
    )
```

time: 46.9 us -> 43.3 us (0.923)
  waiting for transfers between devices: 8.04 us -> 2.78 us
  local copies, waits for them, and re-layouts: 4.52 us -> 0.03 us
  Pallas kernels: 8.01 us -> 12.1 us
  starting transfers between devices: 3.88 us -> 5.8 us
    ppermute x1, waiting for transfers between devices: 8.04 us -> 0.01 us  [local(): next_marks = lax.ppermute(marks, 'chan', back)]
    unnamed x16 -> x8, local copies, waits for them, and re-layouts: 4.52 us -> 0.03 us
    pallas_call x3 -> x6, Pallas kernels: 8.01 us -> 12.1 us  [call(): pl.pallas_call(kernel, out_shape=shape, in_specs=specs, out_specs=[VMEM]...]
    ppermute x1 -> x2, waiting for transfers between devices: 0.01 us -> 2.77 us  [the longest x1 2.77 us: local(): next_early = lax.ppermute(early, 'chan', back)]
    ppermute x1 -> x2, starting transfers between devices: 1.96 us -> 3.88 us  [the longest x1 1.96 us: local(): next_late = lax.ppermute(late, 'chan', back)]
  transfers between devices with their start and end apart: 2 -> 3, of which waited for: 1 -> 1; matrix products, arithmetic and copies ran while one was open for 0% -> 0% of each run, Pallas kernels for 0% -> 10%
where the time goes in v2:
time: 43.3 us; the launch traced here: 43 us
  blocking collectives  22.3 us (52%)
  Pallas kernels  12.1 us (28%)
  starting transfers between devices  5.8 us (13%)
  waiting for transfers between devices  2.78 us (6%)
    all_to_all x1, blocking collectives, local(): lax.all_to_all(cross, ('chan', 'nbr'), split_axis=0, concat_axis=0, tiled...  22.3 us
    pallas_call x6, Pallas kernels, call(): pl.pallas_call(kernel, out_shape=shape, in_specs=specs, out_specs=[VMEM]...  12.1 us
    ppermute x1, waiting for transfers between devices, local(): next_early = lax.ppermute(early, 'chan', back)  2.77 us
    ppermute x1, starting transfers between devices, local(): next_late = lax.ppermute(late, 'chan', back)  1.96 us
    ppermute x1, starting transfers between devices, local(): next_early = lax.ppermute(early, 'chan', back)  1.92 us
    ppermute x1, starting transfers between devices, local(): next_marks = lax.ppermute(marks, 'chan', back)  1.92 us
  transfers between devices with their start and end apart: 3, of which 1 were waited for; matrix products, arithmetic and copies ran while one was open for 0% of the time, Pallas kernels for 10%

profile of v2, /device:TPU:1, one launch (start us, length us, event | category | flops | bytes accessed | tf_op | source)
XLA Modules:
  0.0 43.0 jit_solution(3421384130759722453)
XLA Ops:
  0.0 3.3 %shard_map.82 = (bf16[3,80,512]{2,1,0:T(8,128)(2,1)S(1)}, f32[4,80,1280]{2,1,0:T(8,128)S(1)}, s32[7,80]{1,0:T(8,128)S(1)}, bf16[4,640,256]{2,1,0:T(8,128)(2,1)S(1)}, f32[1,512]{1,0:T(1,128)S(1)}) custom-call(f32[7,80,1280]{2,1,0:T(8,128)} %bitcast.3, s32[7,80]{1,0:T(8,128)} %bitcast.4, bf16[4,640,256]{2,1,0:T(8,128)(2,1)} %constant.8.clone.table_hbm, ...), custom_call_target="tpu_custom_call" | custom-call | tf_op jit(solution)/shard_map/pallas_call | solution.py:244
  3.3 0.0 copy-start.2
  3.3 0.0 copy-start.3
  3.3 1.1 %shard_map.83 = (bf16[4,80,512]{2,1,0:T(8,128)(2,1)S(1)}, s32[7,80]{1,0:T(8,128)S(1)}) custom-call(f32[4,80,1280]{2,1,0:T(8,128)S(1)} %get-tuple-element.17.x_ref, s32[7,80]{1,0:T(8,128)S(1)} %get-tuple-element.18.mark_ref, bf16[4,640,256]{2,1,0:T(8,128)(2,1)S(1)} %get-tuple-element.19.table_ref, f32[1,512]{1,0:T(1,128)S(1)} %get-tuple-element.20.taper_ref), custom_call_target="tpu_custom_call" | custom-call | flops 1000 | bytes 1000 | tf_op jit(solution)/shard_map/pallas_call | solution.py:244
  4.5 2.0 %collective-permute-start = (bf16[4,80,512]{2,1,0:T(8,128)(2,1)S(1)}, bf16[4,80,512]{2,1,0:T(8,128)(2,1)S(1)}, u32[]{:S(2)}, u32[]{:S(2)}) collective-permute-start(bf16[4,80,512]{2,1,0:T(8,128)(2,1)S(1)} %get-tuple-element.21.late_ref), channel_id=1, source_target_pairs={{4,0},{8,4},{12,8},{16,12},{20,16},{24,20},{28,24},{5,1},{9,5},{13... | collective-permute-start | bytes 983048 | tf_op jit(solution)/shard_map/ppermute | solution.py:287
  6.4 1.9 %collective-permute-start.1 = (bf16[3,80,512]{2,1,0:T(8,128)(2,1)S(1)}, bf16[3,80,512]{2,1,0:T(8,128)(2,1)S(1)}, u32[]{:S(2)}, u32[]{:S(2)}) collective-permute-start(bf16[3,80,512]{2,1,0:T(8,128)(2,1)S(1)} %get-tuple-element.22.early_ref), channel_id=1, source_target_pairs={{4,0},{8,4},{12,8},{16,12},{20,16},{24,20},{28,24},{5,1},{9,5},{13... | collective-permute-start | bytes 737288 | tf_op jit(solution)/shard_map/ppermute | solution.py:279
  8.4 1.9 %collective-permute-start.2 = (s32[7,80]{1,0:T(8,128)S(1)}, s32[7,80]{1,0:T(8,128)S(1)}, u32[]{:S(2)}, u32[]{:S(2)}) collective-permute-start(s32[7,80]{1,0:T(8,128)S(1)} %get-tuple-element.23.mark_ref), channel_id=1, source_target_pairs={{4,0},{8,4},{12,8},{16,12},{20,16},{24,20},{28,24},{5,1},{9,5},{13... | collective-permute-start | bytes 6728 | tf_op jit(solution)/shard_map/ppermute | solution.py:288
  10.3 0.0 copy-done.2
  10.3 0.0 copy-done.3
  10.3 3.3 %shard_map.84 = (bf16[7,512,512]{2,1,0:T(8,128)(2,1)S(1)}, f32[512,512]{1,0:T(8,128)S(1)}, bf16[512,80]{1,0:T(8,128)(2,1)S(1)}, f32[512,7]{1,0:T(8,128)S(1)}, f32[512,7]{1,0:T(8,128)S(1)}) custom-call(bf16[3,80,512]{2,1,0:T(8,128)(2,1)S(1)} %get-tuple-element.22.early_ref, bf16[4,80,512]{2,1,0:T(8,128)(2,1)S(1)} %get-tuple-element.21.late_ref, ...), custom_call_target="tpu_custom_call" | custom-call | flops 1000 | bytes 1000 | tf_op jit(solution)/shard_map/pallas_call | solution.py:244
  13.6 2.8 %collective-permute-done.1.white_ref = bf16[3,80,512]{2,1,0:T(8,128)(2,1)S(1)} collective-permute-done((bf16[3,80,512]{2,1,0:T(8,128)(2,1)S(1)}, bf16[3,80,512]{2,1,0:T(8,128)(2,1)S(1)}, u32[]{:S(2)}, u32[]{:S(2)}) %collective-permute-start.1) | collective-permute-done | bytes 245792 | tf_op jit(solution)/shard_map/ppermute | solution.py:279
  16.4 1.1 %shard_map.85.sum_ref = f32[512,512]{1,0:T(8,128)S(1)} custom-call(bf16[3,80,512]{2,1,0:T(8,128)(2,1)S(1)} %collective-permute-done.1.white_ref, bf16[7,512,512]{2,1,0:T(8,128)(2,1)S(1)} %get-tuple-element.24.source_ref, bf16[512,80]{1,0:T(8,128)(2,1)S(1)} %get-tuple-element.25.next_ref, f32[512,512]{1,0:T(8,128)S(1)} %get-tuple-element.26.sum_ref), custom_call_target="tpu_custom_call" | custom-call | tf_op jit(solution)/shard_map/pallas_call | solution.py:244
  17.5 0.0 collective-permute-done.2.next_mark_ref
  17.5 0.0 collective-permute-done.white_ref
  17.5 0.0 copy-start.1
  17.5 1.7 %shard_map.86 = bf16[32,72,128]{2,1,0:T(8,128)(2,1)S(1)} custom-call(bf16[4,80,512]{2,1,0:T(8,128)(2,1)S(1)} %collective-permute-done.white_ref, bf16[7,512,512]{2,1,0:T(8,128)(2,1)S(1)} %get-tuple-element.24.source_ref, bf16[512,80]{1,0:T(8,128)(2,1)S(1)} %get-tuple-element.25.next_ref, f32[512,512]{1,0:T(8,128)S(1)} %shard_map.85.sum_ref, ...), custom_call_target="tpu_custom_call" | custom-call | tf_op jit(solution)/shard_map/pallas_call | solution.py:244
  19.3 0.0 copy-start
  19.3 22.3 %all_to_all.5.x_ref = bf16[32,72,128]{2,1,0:T(8,128)(2,1)S(1)} all-to-all(bf16[32,72,128]{2,1,0:T(8,128)(2,1)S(1)} %shard_map.86), channel_id=1, replica_groups=mesh['chan'=8,'nbr'=4] {'chan','nbr'}, dimensions={0} | all-to-all | bytes 1179648 | tf_op jit(solution)/shard_map/all_to_all | solution.py:318
  41.5 0.0 copy-done.1
  41.5 0.0 copy-done
  41.5 1.5 %shard_map.87 = f32[8,16,1024]{2,1,0:T(8,128)} custom-call(bf16[32,72,128]{2,1,0:T(8,128)(2,1)S(1)} %all_to_all.5.x_ref, bf16[512,1024]{1,0:T(8,128)(2,1)S(1)} %copy-done.1, bf16[512,1024]{1,0:T(8,128)(2,1)S(1)} %copy-done), custom_call_target="tpu_custom_call" | custom-call | tf_op jit(solution)/shard_map/pallas_call | solution.py:244
Async XLA Ops:
  3.3 7.0 %copy-start.2 = (s32[1,2,8,64]{3,2,1,0:T(8,128)S(1)}, s32[1,2,8,64]{3,2,1,0:T(8,128)}, u32[]{:S(2)}) copy-start(s32[1,2,8,64]{3,2,1,0:T(8,128)} %list_ref.1) | copy-start | bytes 12292
  3.3 7.0 %copy-start.3 = (s32[1,8]{1,0:T(1,128)S(1)}, s32[1,8]{1,0:T(1,128)}, u32[]{:S(2)}) copy-start(s32[1,8]{1,0:T(1,128)} %count_ref.1) | copy-start | bytes 100
  4.5 13.0 %collective-permute-start = (bf16[4,80,512]{2,1,0:T(8,128)(2,1)S(1)}, bf16[4,80,512]{2,1,0:T(8,128)(2,1)S(1)}, u32[]{:S(2)}, u32[]{:S(2)}) collective-permute-start(bf16[4,80,512]{2,1,0:T(8,128)(2,1)S(1)} %get-tuple-element.21.late_ref), channel_id=1, source_target_pairs={{4,0},{8,4},{12,8},{16,12},{20,16},{24,20},{28,24},{5,1},{9,5},{13... | collective-permute-start | bytes 983048 | tf_op jit(solution)/shard_map/ppermute | solution.py:287
  6.4 9.9 %collective-permute-start.1 = (bf16[3,80,512]{2,1,0:T(8,128)(2,1)S(1)}, bf16[3,80,512]{2,1,0:T(8,128)(2,1)S(1)}, u32[]{:S(2)}, u32[]{:S(2)}) collective-permute-start(bf16[3,80,512]{2,1,0:T(8,128)(2,1)S(1)} %get-tuple-element.22.early_ref), channel_id=1, source_target_pairs={{4,0},{8,4},{12,8},{16,12},{20,16},{24,20},{28,24},{5,1},{9,5},{13... | collective-permute-start | bytes 737288 | tf_op jit(solution)/shard_map/ppermute | solution.py:279
  8.4 9.1 %collective-permute-start.2 = (s32[7,80]{1,0:T(8,128)S(1)}, s32[7,80]{1,0:T(8,128)S(1)}, u32[]{:S(2)}, u32[]{:S(2)}) collective-permute-start(s32[7,80]{1,0:T(8,128)S(1)} %get-tuple-element.23.mark_ref), channel_id=1, source_target_pairs={{4,0},{8,4},{12,8},{16,12},{20,16},{24,20},{28,24},{5,1},{9,5},{13... | collective-permute-start | bytes 6728 | tf_op jit(solution)/shard_map/ppermute | solution.py:288
  17.5 24.0 %copy-start.1 = (bf16[512,1024]{1,0:T(8,128)(2,1)S(1)}, bf16[512,1024]{1,0:T(8,128)(2,1)}, u32[]{:S(2)}) copy-start(bf16[512,1024]{1,0:T(8,128)(2,1)} %constant.10.clone.high_ref) | copy-start | bytes 3145732
  19.3 22.3 %copy-start = (bf16[512,1024]{1,0:T(8,128)(2,1)S(1)}, bf16[512,1024]{1,0:T(8,128)(2,1)}, u32[]{:S(2)}) copy-start(bf16[512,1024]{1,0:T(8,128)(2,1)} %constant.11.clone.low_ref) | copy-start | bytes 3145732

commit v3 on v2

v3 whole, which is shorter than its diff:
```python
import functools
import math

import jax
import jax.numpy as jnp
import ml_dtypes
import numpy as np
from jax import lax
from jax.experimental import pallas as pl
from jax.experimental.pallas import tpu as pltpu
from jax.sharding import PartitionSpec as P

NF = 256
NLAG = 1024
LANES = 128
BF = jnp.bfloat16
F32 = jnp.float32
VMEM = pl.BlockSpec(memory_space=pltpu.VMEM)
HBM = pl.BlockSpec(memory_space=pltpu.HBM)
SMEM = pl.BlockSpec(memory_space=pltpu.SMEM)

EVEN, ODD = np.arange(2, NF + 1, 2), np.arange(1, NF + 1, 2)
FIRST = 5
GROUP = 3
STEP = 128


def two_parts(table):
    high = table.astype(ml_dtypes.bfloat16)
    return high, (table - high.astype(np.float64)).astype(ml_dtypes.bfloat16)


def forward_tables(span):
    clock = np.arange(span // 2)[:, None]
    parts = []
    for bins in (EVEN, ODD):
        angle = (clock * bins[None, :] % span) * (2.0 * math.pi / span)
        parts += two_parts(np.concatenate([np.cos(angle), -np.sin(angle)], axis=1))
    return np.stack(parts)


def inverse_tables(span):
    lag = np.arange(NLAG)[None, :] - NLAG // 2
    rows = []
    for bins in (EVEN, ODD):
        angle = (bins[:, None] * lag % span) * (2.0 * math.pi / span)
        rows += [np.cos(angle), -np.sin(angle)]
    return two_parts(np.concatenate(rows, axis=0))


def taper():
    window = np.sin(math.pi * np.concatenate([EVEN, EVEN, ODD, ODD]) / (NF + 1.0))
    return window[None, :].astype(np.float32)


def halves(value):
    high = value.astype(BF)
    return high, (value - high.astype(F32)).astype(BF)


def dot(a, b):
    return jnp.dot(a, b, preferred_element_type=F32)


def dot_across(a, b):
    return lax.dot_general(a, b, (((1,), (1,)), ((), ())), preferred_element_type=F32)


def as_column(row):
    size = row.shape[1]
    shape = (size, size)
    same = lax.broadcasted_iota(jnp.int32, shape, 0) == lax.broadcasted_iota(jnp.int32, shape, 1)
    return jnp.sum(jnp.where(same, row, 0.0), axis=1, keepdims=True)


def whiten(x_ref, flags, table_ref, taper_ref, ready):
    segs, rows, span = x_ref.shape
    half = span // 2
    low = x_ref[:, :, :half].reshape(segs * rows, half)
    high = x_ref[:, :, half:].reshape(segs * rows, half)
    found = []
    for i, folded in enumerate((low + high, low - high)):
        coarse, fine = halves(folded)
        ready(i)
        found.append(
            dot(coarse, table_ref[2 * i]) + dot(fine, table_ref[2 * i]) + dot(coarse, table_ref[2 * i + 1])
        )
    even, odd = found
    energy = jnp.sum(even * even + odd * odd, axis=1, keepdims=True) * (0.5 / NF)
    factor = flags / jnp.sqrt(energy + 1e-05)
    return [
        (part * factor * taper_ref[:, i * NF : (i + 1) * NF]).astype(BF) for i, part in enumerate(found)
    ]


def whiten_kernel(x_hbm, mark_hbm, table_hbm, taper_hbm, early_ref, late_ref, x, mark, table, window, row, sem):
    total, rows, _ = x_hbm.shape
    early = early_ref.shape[0] // rows
    copies = [
        pltpu.make_async_copy(mark_hbm, mark, sem.at[0]),
        pltpu.make_async_copy(taper_hbm, window, sem.at[1]),
        pltpu.make_async_copy(x_hbm.at[pl.ds(0, GROUP)], x.at[pl.ds(0, GROUP)], sem.at[2]),
        pltpu.make_async_copy(table_hbm.at[pl.ds(0, 2)], table.at[pl.ds(0, 2)], sem.at[3]),
        pltpu.make_async_copy(table_hbm.at[pl.ds(2, 2)], table.at[pl.ds(2, 2)], sem.at[4]),
        pltpu.make_async_copy(
            x_hbm.at[pl.ds(GROUP, total - GROUP)], x.at[pl.ds(GROUP, total - GROUP)], sem.at[5]
        ),
    ]
    for copy in copies:
        copy.start()
    copies[0].wait()
    copies[1].wait()
    flags = [as_column(mark[s : s + 1, :].astype(F32)) for s in range(total)]
    row[...] = jnp.zeros(row.shape, F32)
    row[:total, :rows] = mark[...].astype(F32)
    early_ref[early * rows :, :] = row[...].astype(BF)
    copies[2].wait()
    for start, stop in ((0, GROUP), (GROUP, total)):
        column = jnp.concatenate(flags[start:stop], axis=0)
        if start == 0:
            ready = lambda i: copies[3 + i].wait()
        else:
            copies[5].wait()
            ready = lambda i: None
        for i, white in enumerate(whiten(x.at[start:stop], column, table, window, ready)):
            columns = slice(i * NF, (i + 1) * NF)
            split = min(max(early - start, 0), stop - start) * rows
            if split:
                early_ref[start * rows : start * rows + split, columns] = white[:split]
            if split < white.shape[0]:
                base = max(start - early, 0) * rows
                late_ref[base : base + white.shape[0] - split, columns] = white[split:]


def add_products(real, imag, a, b):
    quad = NF // 2
    ar, ai, br, bi = a[:, :quad], a[:, quad:], b[:, :quad], b[:, quad:]
    return real + (ar * br + ai * bi), imag + (ai * br - ar * bi)


def sources_kernel(
    step, early_ref, late_ref, mark_ref, list_ref, count_ref,
    source_ref, sum_ref, next_ref, source_mark_ref, own_mark_ref, first, own,
):
    segs, rows = mark_ref.shape
    owners, slots = list_ref.shape[2:]
    quad = NF // 2
    anchor = lax.axis_index("chan") * rows
    spots = lax.broadcasted_iota(jnp.int32, (slots, rows), 1).astype(F32)
    for o in range(owners):
        live = lax.broadcasted_iota(jnp.int32, (1, slots), 1) < count_ref[0, o]
        where = slice(o * slots, (o + 1) * slots)
        column = as_column(jnp.where(live, list_ref[0, 0, o : o + 1, :] - anchor, -1).astype(F32))
        first[where, :] = (spots == column).astype(BF)
        column = as_column((list_ref[0, 1, o : o + 1, :] - anchor).astype(F32))
        own[where, :] = (spots == column).astype(BF)
        next_ref[where, :] = (spots == column - rows).astype(BF)
    marks = mark_ref[...].astype(BF)

    def body(i, carry):
        at = pl.ds(pl.multiple_of(i * step, step), step)
        a_hot, b_hot = first[at, :], own[at, :]
        source_mark_ref[at, :] = dot_across(a_hot, marks)
        own_mark_ref[at, :] = dot_across(b_hot, marks)
        for h in range(2):
            columns = slice(h * NF, (h + 1) * NF)
            real = imag = jnp.zeros((step, quad), F32)
            for s in range(segs):
                ref, base = (early_ref, s) if s < FIRST else (late_ref, s - FIRST)
                white = ref[base * rows : (base + 1) * rows, columns]
                a = dot(a_hot, white)
                source_ref[s, at, columns] = a.astype(BF)
                real, imag = add_products(real, imag, a, dot(b_hot, white))
            sum_ref[at, h * NF : h * NF + quad] = real
            sum_ref[at, h * NF + quad : (h + 1) * NF] = imag
        return carry

    lax.fori_loop(0, owners * slots // step, body, 0)


def add_segments(at, segs, base, white_ref, source_ref, hot, sums):
    quad = NF // 2
    rows = hot.shape[1]
    result = []
    for h in range(2):
        columns = slice(h * NF, (h + 1) * NF)
        real, imag = sums[at, h * NF : h * NF + quad], sums[at, h * NF + quad : (h + 1) * NF]
        for s in range(segs):
            a = source_ref[base + s, at, columns].astype(F32)
            real, imag = add_products(real, imag, a, dot(hot, white_ref[s * rows : (s + 1) * rows, columns]))
        result += [real, imag]
    return result


def early_kernel(
    step, white_ref, source_ref, next_ref, sum_ref, source_mark_ref, own_mark_ref, out_ref, tail_ref
):
    pairs, rows = next_ref.shape
    segs = source_mark_ref.shape[1]
    per = pairs // tail_ref.shape[0]
    quad = NF // 2
    next_marks = white_ref[FIRST * rows :, :LANES].astype(F32)[:segs, :rows].astype(BF)

    def body(i, carry):
        at = pl.ds(pl.multiple_of(i * step, step), step)
        to = pl.ds(i * (step // per), step // per)
        hot = next_ref[at, :]
        for k, part in enumerate(add_segments(at, FIRST, 0, white_ref, source_ref, hot, sum_ref)):
            out_ref[at, k * quad : (k + 1) * quad] = part
        both = source_mark_ref[at, :] * (own_mark_ref[at, :] + dot_across(hot, next_marks))
        shared = jnp.broadcast_to(jnp.sum(both, axis=1, keepdims=True), (step, LANES)).reshape(-1, per, LANES)
        tail = shared[:, :8, :]
        lane = lax.broadcasted_iota(jnp.int32, tail.shape, 2)
        for k in range(1, per // 8):
            tail = jnp.where(lane >= k * 8 * LANES // per, shared[:, 8 * k : 8 * k + 8, :], tail)
        tail_ref[to, :, :] = tail
        return carry

    lax.fori_loop(0, pairs // step, body, 0)


def late_kernel(step, white_ref, source_ref, next_ref, sum_ref, tail_ref, out_ref):
    pairs = sum_ref.shape[0]
    per = pairs // out_ref.shape[0]
    late = source_ref.shape[0] - FIRST
    out_ref[:, 2 * NF // LANES * per :, :] = tail_ref[...].astype(BF)

    def body(i, carry):
        at = pl.ds(pl.multiple_of(i * step, step), step)
        to = pl.ds(i * (step // per), step // per)
        for k, part in enumerate(
            add_segments(at, late, FIRST, white_ref, source_ref, next_ref[at, :], sum_ref)
        ):
            out_ref[to, k * per : (k + 1) * per, :] = part.astype(BF).reshape(-1, per, LANES)
        return carry

    lax.fori_loop(0, pairs // step, body, 0)


def lags_kernel(parts, per, x_ref, high_ref, low_ref, out_ref):
    dests, length, _ = x_ref.shape
    blocks = 2 * NF // LANES
    total = jnp.sum(x_ref[...].astype(F32).reshape(dests // parts, parts, length, LANES), axis=1)
    scale = 1.0 / jnp.maximum(total[:, blocks * per :, :], 1.0)
    scale = jnp.concatenate(
        [scale[:, :, k * 8 * LANES // per :][:, :, :1] for k in range(per // 8)], axis=1
    )
    stacked = jnp.concatenate(
        [
            (total[:, k * per : (k + 1) * per, :] * scale).reshape(-1, LANES)
            for k in range(blocks)
        ],
        axis=1,
    )
    coarse, fine = halves(stacked)
    traces = dot(coarse, high_ref[...]) + dot(fine, high_ref[...]) + dot(coarse, low_ref[...])
    out_ref[...] = traces.reshape(out_ref.shape)


def call(kernel, shape, args, specs, scratch=(), mib=24):
    return pl.pallas_call(
        kernel,
        out_shape=shape,
        in_specs=specs,
        out_specs=[VMEM] * len(shape),
        scratch_shapes=list(scratch),
        compiler_params=pltpu.CompilerParams(vmem_limit_bytes=mib << 20),
    )(*args)


def local(records, gap_mask, pair_list, pair_counts):
    rows, segs, span = records.shape
    owners, slots = pair_list.shape[2:]
    chan, nbr = lax.axis_size("chan"), lax.axis_size("nbr")
    per = slots // nbr
    pairs = owners * slots
    step = min(STEP, pairs)
    width = 2 * NF
    back = [(i, i - 1) for i in range(1, chan)]
    shape = jax.ShapeDtypeStruct
    tables = forward_tables(span)
    inputs = (jnp.transpose(records, (1, 0, 2)), gap_mask.T, jnp.asarray(tables), jnp.asarray(taper()))
    extra = -(-segs // 16) * 16
    early, late = call(
        whiten_kernel,
        [shape((FIRST * rows + extra, width), BF), shape(((segs - FIRST) * rows, width), BF)],
        [pltpu.with_memory_space_constraint(v, pltpu.HBM) for v in inputs],
        [HBM] * 4,
        [
            pltpu.VMEM((segs, rows, span), F32),
            pltpu.VMEM((segs, rows), jnp.int32),
            pltpu.VMEM(tables.shape, BF),
            pltpu.VMEM((1, width), F32),
            pltpu.VMEM((extra, width), F32),
            pltpu.SemaphoreType.DMA((6,)),
        ],
        mib=32,
    )
    next_early = lax.ppermute(early, "chan", back)
    next_late = lax.ppermute(late, "chan", back)
    source, sums, hot, source_marks, own_marks = call(
        functools.partial(sources_kernel, step),
        [
            shape((segs, pairs, width), BF),
            shape((pairs, width), F32),
            shape((pairs, rows), BF),
            shape((pairs, segs), F32),
            shape((pairs, segs), F32),
        ],
        (early, late, gap_mask.T, pair_list, pair_counts),
        [VMEM] * 4 + [SMEM],
        [pltpu.VMEM((pairs, rows), BF), pltpu.VMEM((pairs, rows), BF)],
        mib=40,
    )
    sums, tail = call(
        functools.partial(early_kernel, step),
        [shape((pairs, width), F32), shape((chan * nbr, 8, LANES), F32)],
        (next_early, source, hot, sums, source_marks, own_marks),
        [VMEM] * 6,
        mib=40,
    )
    (cross,) = call(
        functools.partial(late_kernel, step),
        [shape((chan * nbr, width // LANES * per + 8, LANES), BF)],
        (next_late, source, hot, sums, tail),
        [VMEM] * 5,
        mib=40,
    )
    arrived = lax.all_to_all(cross, ("chan", "nbr"), split_axis=0, concat_axis=0, tiled=True)
    high, low = inverse_tables(span)
    (traces,) = call(
        functools.partial(lags_kernel, nbr, per),
        [shape((chan, per, NLAG), F32)],
        (arrived, jnp.asarray(high), jnp.asarray(low)),
        [VMEM] * 3,
    )
    return traces[None]


def solution(mesh):
    return jax.shard_map(
        local,
        mesh=mesh,
        in_specs=(
            P("chan", "nbr", None),
            P("chan", "nbr"),
            P("chan", None, None, None),
            P("chan", None),
        ),
        out_specs=P("chan", None, "nbr", None),
        check_vma=False,
    )
```

time: 43.3 us -> 41.3 us (0.954)
  starting transfers between devices: 5.8 us -> 3.89 us
    ppermute x1 -> x0, starting transfers between devices: 1.92 us -> none  [local(): next_marks = lax.ppermute(marks, 'chan', back)]
    pallas_call x6 -> x5, Pallas kernels: 12.1 us -> 11.9 us  [call(): pl.pallas_call(kernel, out_shape=shape, in_specs=specs, out_specs=[VMEM]...]
  transfers between devices with their start and end apart: 3 -> 2, of which waited for: 1 -> 1; matrix products, arithmetic and copies ran while one was open for 0% -> 0% of each run, Pallas kernels for 10% -> 12%
where the time goes in v3:
time: 41.3 us; the launch traced here: 41.1 us
  blocking collectives  22.1 us (54%)
  Pallas kernels  11.9 us (29%)
  starting transfers between devices  3.89 us (9%)
  waiting for transfers between devices  3.09 us (7%)
    all_to_all x1, blocking collectives, local(): lax.all_to_all(cross, ('chan', 'nbr'), split_axis=0, concat_axis=0, tiled...  22.1 us
    pallas_call x5, Pallas kernels, call(): pl.pallas_call(kernel, out_shape=shape, in_specs=specs, out_specs=[VMEM]...  11.9 us
    ppermute x1, waiting for transfers between devices, local(): next_early = lax.ppermute(early, 'chan', back)  3.09 us
    ppermute x1, starting transfers between devices, local(): next_early = lax.ppermute(early, 'chan', back)  1.96 us
    ppermute x1, starting transfers between devices, local(): next_late = lax.ppermute(late, 'chan', back)  1.92 us
  transfers between devices with their start and end apart: 2, of which 1 were waited for; matrix products, arithmetic and copies ran while one was open for 0% of the time, Pallas kernels for 12%

profile of v3, /device:TPU:1, one launch (start us, length us, event | category | flops | bytes accessed | tf_op | source)
XLA Modules:
  0.0 41.1 jit_solution(9579932242947142770)
XLA Ops:
  0.0 0.0 copy-start.2
  0.0 0.0 copy-start.4
  0.0 0.0 copy-start.3
  0.0 4.4 %shard_map.82 = (bf16[416,512]{1,0:T(8,128)(2,1)S(1)}, bf16[160,512]{1,0:T(8,128)(2,1)S(1)}) custom-call(f32[7,80,1280]{2,1,0:T(8,128)} %bitcast.5, s32[7,80]{1,0:T(8,128)} %bitcast.3, bf16[4,640,256]{2,1,0:T(8,128)(2,1)} %constant.8.clone.table_hbm, f32[1,512]{1,0:T(1,128)} %constant.9.clone.taper_hbm), custom_call_target="tpu_custom_call" | custom-call | tf_op jit(solution)/shard_map/pallas_call | solution.py:261
  4.4 2.0 %collective-permute-start.1 = (bf16[416,512]{1,0:T(8,128)(2,1)S(1)}, bf16[416,512]{1,0:T(8,128)(2,1)S(1)}, u32[]{:S(2)}, u32[]{:S(2)}) collective-permute-start(bf16[416,512]{1,0:T(8,128)(2,1)S(1)} %get-tuple-element.15.early_ref), channel_id=1, source_target_pairs={{4,0},{8,4},{12,8},{16,12},{20,16},{24,20},{28,24},{5,1},{9,5},{13... | collective-permute-start | bytes 1277960 | tf_op jit(solution)/shard_map/ppermute | solution.py:299
  6.3 1.9 %collective-permute-start = (bf16[160,512]{1,0:T(8,128)(2,1)S(1)}, bf16[160,512]{1,0:T(8,128)(2,1)S(1)}, u32[]{:S(2)}, u32[]{:S(2)}) collective-permute-start(bf16[160,512]{1,0:T(8,128)(2,1)S(1)} %get-tuple-element.14.late_ref), channel_id=1, source_target_pairs={{4,0},{8,4},{12,8},{16,12},{20,16},{24,20},{28,24},{5,1},{9,5},{13... | collective-permute-start | bytes 491528 | tf_op jit(solution)/shard_map/ppermute | solution.py:300
  8.3 0.0 copy-done.2
  8.3 0.0 copy-done.4
  8.3 0.0 copy-done.3
  8.3 3.3 %shard_map.83 = (bf16[7,512,512]{2,1,0:T(8,128)(2,1)S(1)}, f32[512,512]{1,0:T(8,128)S(1)}, bf16[512,80]{1,0:T(8,128)(2,1)S(1)}, f32[512,7]{1,0:T(8,128)S(1)}, f32[512,7]{1,0:T(8,128)S(1)}) custom-call(bf16[416,512]{1,0:T(8,128)(2,1)S(1)} %get-tuple-element.15.early_ref, bf16[160,512]{1,0:T(8,128)(2,1)S(1)} %get-tuple-element.14.late_ref, ...), custom_call_target="tpu_custom_call" | custom-call | tf_op jit(solution)/shard_map/pallas_call | solution.py:261
  11.6 3.1 %collective-permute-done.1.white_ref = bf16[416,512]{1,0:T(8,128)(2,1)S(1)} collective-permute-done((bf16[416,512]{1,0:T(8,128)(2,1)S(1)}, bf16[416,512]{1,0:T(8,128)(2,1)S(1)}, u32[]{:S(2)}, u32[]{:S(2)}) %collective-permute-start.1) | collective-permute-done | bytes 426016 | tf_op jit(solution)/shard_map/ppermute | solution.py:299
  14.7 1.8 %shard_map.84 = (f32[512,512]{1,0:T(8,128)S(1)}, f32[32,8,128]{2,1,0:T(8,128)S(1)}) custom-call(bf16[416,512]{1,0:T(8,128)(2,1)S(1)} %collective-permute-done.1.white_ref, bf16[7,512,512]{2,1,0:T(8,128)(2,1)S(1)} %get-tuple-element.16.source_ref, bf16[512,80]{1,0:T(8,128)(2,1)S(1)} %get-tuple-element.17.next_ref, f32[512,512]{1,0:T(8,128)S(1)} %get-tuple-element.18.sum_ref, ...), custom_call_target="tpu_custom_call" | custom-call | tf_op jit(solution)/shard_map/pallas_call | solution.py:261
  16.5 0.0 collective-permute-done.white_ref
  16.5 0.0 copy-start
  16.6 0.0 copy-start.1
  16.6 1.0 %shard_map.85 = bf16[32,72,128]{2,1,0:T(8,128)(2,1)S(1)} custom-call(bf16[160,512]{1,0:T(8,128)(2,1)S(1)} %collective-permute-done.white_ref, bf16[7,512,512]{2,1,0:T(8,128)(2,1)S(1)} %get-tuple-element.16.source_ref, bf16[512,80]{1,0:T(8,128)(2,1)S(1)} %get-tuple-element.17.next_ref, f32[512,512]{1,0:T(8,128)S(1)} %get-tuple-element.21.sum_ref, ...), custom_call_target="tpu_custom_call" | custom-call | tf_op jit(solution)/shard_map/pallas_call | solution.py:261
  17.5 22.1 %all_to_all.5.x_ref = bf16[32,72,128]{2,1,0:T(8,128)(2,1)S(1)} all-to-all(bf16[32,72,128]{2,1,0:T(8,128)(2,1)S(1)} %shard_map.85), channel_id=1, replica_groups=mesh['chan'=8,'nbr'=4] {'chan','nbr'}, dimensions={0} | all-to-all | bytes 1179648 | tf_op jit(solution)/shard_map/all_to_all | solution.py:329
  39.6 0.0 copy-done
  39.6 0.0 copy-done.1
  39.6 1.5 %shard_map.86 = f32[8,16,1024]{2,1,0:T(8,128)} custom-call(bf16[32,72,128]{2,1,0:T(8,128)(2,1)S(1)} %all_to_all.5.x_ref, bf16[512,1024]{1,0:T(8,128)(2,1)S(1)} %copy-done.1, bf16[512,1024]{1,0:T(8,128)(2,1)S(1)} %copy-done), custom_call_target="tpu_custom_call" | custom-call | tf_op jit(solution)/shard_map/pallas_call | solution.py:261
Async XLA Ops:
  0.0 8.3 %copy-start.2 = (s32[80,7]{0,1:T(8,128)S(1)}, s32[80,7]{0,1:T(8,128)}, u32[]{:S(2)}) copy-start(s32[80,7]{0,1:T(8,128)} %param.9) | copy-start | bytes 6724
  0.0 8.3 %copy-start.4 = (s32[1,8]{1,0:T(1,128)S(1)}, s32[1,8]{1,0:T(1,128)}, u32[]{:S(2)}) copy-start(s32[1,8]{1,0:T(1,128)} %count_ref.1) | copy-start | bytes 100
  0.0 8.3 %copy-start.3 = (s32[1,2,8,64]{3,2,1,0:T(8,128)S(1)}, s32[1,2,8,64]{3,2,1,0:T(8,128)}, u32[]{:S(2)}) copy-start(s32[1,2,8,64]{3,2,1,0:T(8,128)} %list_ref.1) | copy-start | bytes 12292
  4.4 10.3 %collective-permute-start.1 = (bf16[416,512]{1,0:T(8,128)(2,1)S(1)}, bf16[416,512]{1,0:T(8,128)(2,1)S(1)}, u32[]{:S(2)}, u32[]{:S(2)}) collective-permute-start(bf16[416,512]{1,0:T(8,128)(2,1)S(1)} %get-tuple-element.15.early_ref), channel_id=1, source_target_pairs={{4,0},{8,4},{12,8},{16,12},{20,16},{24,20},{28,24},{5,1},{9,5},{13... | collective-permute-start | bytes 1277960 | tf_op jit(solution)/shard_map/ppermute | solution.py:299
  6.3 10.2 %collective-permute-start = (bf16[160,512]{1,0:T(8,128)(2,1)S(1)}, bf16[160,512]{1,0:T(8,128)(2,1)S(1)}, u32[]{:S(2)}, u32[]{:S(2)}) collective-permute-start(bf16[160,512]{1,0:T(8,128)(2,1)S(1)} %get-tuple-element.14.late_ref), channel_id=1, source_target_pairs={{4,0},{8,4},{12,8},{16,12},{20,16},{24,20},{28,24},{5,1},{9,5},{13... | collective-permute-start | bytes 491528 | tf_op jit(solution)/shard_map/ppermute | solution.py:300
  16.5 23.1 %copy-start = (bf16[512,1024]{1,0:T(8,128)(2,1)S(1)}, bf16[512,1024]{1,0:T(8,128)(2,1)}, u32[]{:S(2)}) copy-start(bf16[512,1024]{1,0:T(8,128)(2,1)} %constant.11.clone.low_ref) | copy-start | bytes 3145732
  16.6 23.1 %copy-start.1 = (bf16[512,1024]{1,0:T(8,128)(2,1)S(1)}, bf16[512,1024]{1,0:T(8,128)(2,1)}, u32[]{:S(2)}) copy-start(bf16[512,1024]{1,0:T(8,128)(2,1)} %constant.10.clone.high_ref) | copy-start | bytes 3145732

commit v4 on v3

--- a/solution.py
+++ b/solution.py
@@ -22,7 +22,7 @@
 EVEN, ODD = np.arange(2, NF + 1, 2), np.arange(1, NF + 1, 2)
 FIRST = 5
 GROUP = 3
-STEP = 128
+STEP = 512
 
 
 def two_parts(table):
@@ -35,7 +35,8 @@
     parts = []
     for bins in (EVEN, ODD):
         angle = (clock * bins[None, :] % span) * (2.0 * math.pi / span)
-        parts += two_parts(np.concatenate([np.cos(angle), -np.sin(angle)], axis=1))
+        table = np.concatenate([np.cos(angle), -np.sin(angle)], axis=1)
+        parts.append(np.concatenate(two_parts(table), axis=0))
     return np.stack(parts)
 
 
@@ -73,7 +74,7 @@
     return jnp.sum(jnp.where(same, row, 0.0), axis=1, keepdims=True)
 
 
-def whiten(x_ref, flags, table_ref, taper_ref, ready):
+def whiten(x_ref, flags, table_ref, taper_ref):
     segs, rows, span = x_ref.shape
     half = span // 2
     low = x_ref[:, :, :half].reshape(segs * rows, half)
@@ -81,9 +82,8 @@
     found = []
     for i, folded in enumerate((low + high, low - high)):
         coarse, fine = halves(folded)
-        ready(i)
         found.append(
-            dot(coarse, table_ref[2 * i]) + dot(fine, table_ref[2 * i]) + dot(coarse, table_ref[2 * i + 1])
+            dot(fine, table_ref[i, :half, :]) + dot(jnp.concatenate([coarse, coarse], axis=1), table_ref[i])
         )
     even, odd = found
     energy = jnp.sum(even * even + odd * odd, axis=1, keepdims=True) * (0.5 / NF)
@@ -96,33 +96,28 @@
 def whiten_kernel(x_hbm, mark_hbm, table_hbm, taper_hbm, early_ref, late_ref, x, mark, table, window, row, sem):
     total, rows, _ = x_hbm.shape
     early = early_ref.shape[0] // rows
-    copies = [
+    small = [
         pltpu.make_async_copy(mark_hbm, mark, sem.at[0]),
         pltpu.make_async_copy(taper_hbm, window, sem.at[1]),
-        pltpu.make_async_copy(x_hbm.at[pl.ds(0, GROUP)], x.at[pl.ds(0, GROUP)], sem.at[2]),
-        pltpu.make_async_copy(table_hbm.at[pl.ds(0, 2)], table.at[pl.ds(0, 2)], sem.at[3]),
-        pltpu.make_async_copy(table_hbm.at[pl.ds(2, 2)], table.at[pl.ds(2, 2)], sem.at[4]),
-        pltpu.make_async_copy(
-            x_hbm.at[pl.ds(GROUP, total - GROUP)], x.at[pl.ds(GROUP, total - GROUP)], sem.at[5]
-        ),
     ]
-    for copy in copies:
+    tables = pltpu.make_async_copy(table_hbm, table, sem.at[2])
+    groups = [
+        pltpu.make_async_copy(x_hbm.at[pl.ds(a, b - a)], x.at[pl.ds(a, b - a)], sem.at[3 + i])
+        for i, (a, b) in enumerate(((0, GROUP), (GROUP, total)))
+    ]
+    for copy in small + [tables] + groups:
         copy.start()
-    copies[0].wait()
-    copies[1].wait()
+    for copy in small:
+        copy.wait()
     flags = [as_column(mark[s : s + 1, :].astype(F32)) for s in range(total)]
     row[...] = jnp.zeros(row.shape, F32)
     row[:total, :rows] = mark[...].astype(F32)
     early_ref[early * rows :, :] = row[...].astype(BF)
-    copies[2].wait()
-    for start, stop in ((0, GROUP), (GROUP, total)):
+    tables.wait()
+    for group, (start, stop) in zip(groups, ((0, GROUP), (GROUP, total))):
+        group.wait()
         column = jnp.concatenate(flags[start:stop], axis=0)
-        if start == 0:
-            ready = lambda i: copies[3 + i].wait()
-        else:
-            copies[5].wait()
-            ready = lambda i: None
-        for i, white in enumerate(whiten(x.at[start:stop], column, table, window, ready)):
+        for i, white in enumerate(whiten(x.at[start:stop], column, table, window)):
             columns = slice(i * NF, (i + 1) * NF)
             split = min(max(early - start, 0), stop - start) * rows
             if split:
@@ -292,7 +287,7 @@
             pltpu.VMEM(tables.shape, BF),
             pltpu.VMEM((1, width), F32),
             pltpu.VMEM((extra, width), F32),
-            pltpu.SemaphoreType.DMA((6,)),
+            pltpu.SemaphoreType.DMA((5,)),
         ],
         mib=32,
     )

time: 41.3 us -> 40.1 us (0.971)
  Pallas kernels: 11.9 us -> 9.72 us
  waiting for transfers between devices: 3.09 us -> 4.08 us
    pallas_call x5, Pallas kernels: 11.9 us -> 9.72 us  [call(): pl.pallas_call(kernel, out_shape=shape, in_specs=specs, out_specs=[VMEM]...]
    ppermute x1, waiting for transfers between devices: 0.01 us -> 0.57 us  [local(): next_late = lax.ppermute(late, 'chan', back)]
    ppermute x1, waiting for transfers between devices: 3.09 us -> 3.51 us  [local(): next_early = lax.ppermute(early, 'chan', back)]
  transfers between devices with their start and end apart: 2 -> 2, of which waited for: 1 -> 2; matrix products, arithmetic and copies ran while one was open for 0% -> 0% of each run, Pallas kernels for 12% -> 10%
where the time goes in v4:
time: 40.1 us; the launch traced here: 39.9 us
  blocking collectives  22.1 us (55%)
  Pallas kernels  9.72 us (24%)
  waiting for transfers between devices  4.08 us (10%)
  starting transfers between devices  3.88 us (10%)
    all_to_all x1, blocking collectives, local(): lax.all_to_all(cross, ('chan', 'nbr'), split_axis=0, concat_axis=0, tiled...  22.1 us
    pallas_call x5, Pallas kernels, call(): pl.pallas_call(kernel, out_shape=shape, in_specs=specs, out_specs=[VMEM]...  9.72 us
    ppermute x1, waiting for transfers between devices, local(): next_early = lax.ppermute(early, 'chan', back)  3.51 us
    ppermute x1, starting transfers between devices, local(): next_early = lax.ppermute(early, 'chan', back)  1.96 us
    ppermute x1, starting transfers between devices, local(): next_late = lax.ppermute(late, 'chan', back)  1.92 us
  transfers between devices with their start and end apart: 2, of which 2 were waited for; matrix products, arithmetic and copies ran while one was open for 0% of the time, Pallas kernels for 10%

profile of v4, /device:TPU:1, one launch (start us, length us, event | category | flops | bytes accessed | tf_op | source)
XLA Modules:
  0.0 39.9 jit_solution(9045696899007467739)
XLA Ops:
  0.0 0.0 copy-start.2
  0.0 0.0 copy-start.4
  0.0 0.0 copy-start.3
  0.0 3.7 %shard_map.82 = (bf16[416,512]{1,0:T(8,128)(2,1)S(1)}, bf16[160,512]{1,0:T(8,128)(2,1)S(1)}) custom-call(f32[7,80,1280]{2,1,0:T(8,128)} %bitcast.5, s32[7,80]{1,0:T(8,128)} %bitcast.3, bf16[2,1280,256]{2,1,0:T(8,128)(2,1)} %constant.8.clone.table_hbm, f32[1,512]{1,0:T(1,128)} %constant.9.clone.taper_hbm), custom_call_target="tpu_custom_call" | custom-call | tf_op jit(solution)/shard_map/pallas_call | solution.py:256
  3.7 2.0 %collective-permute-start.1 = (bf16[416,512]{1,0:T(8,128)(2,1)S(1)}, bf16[416,512]{1,0:T(8,128)(2,1)S(1)}, u32[]{:S(2)}, u32[]{:S(2)}) collective-permute-start(bf16[416,512]{1,0:T(8,128)(2,1)S(1)} %get-tuple-element.15.early_ref), channel_id=1, source_target_pairs={{4,0},{8,4},{12,8},{16,12},{20,16},{24,20},{28,24},{5,1},{9,5},{13... | collective-permute-start | bytes 1277960 | tf_op jit(solution)/shard_map/ppermute | solution.py:294
  5.7 1.9 %collective-permute-start = (bf16[160,512]{1,0:T(8,128)(2,1)S(1)}, bf16[160,512]{1,0:T(8,128)(2,1)S(1)}, u32[]{:S(2)}, u32[]{:S(2)}) collective-permute-start(bf16[160,512]{1,0:T(8,128)(2,1)S(1)} %get-tuple-element.14.late_ref), channel_id=1, source_target_pairs={{4,0},{8,4},{12,8},{16,12},{20,16},{24,20},{28,24},{5,1},{9,5},{13... | collective-permute-start | bytes 491528 | tf_op jit(solution)/shard_map/ppermute | solution.py:295
  7.6 0.0 copy-done.2
  7.6 0.0 copy-done.4
  7.6 0.0 copy-done.3
  7.6 2.9 %shard_map.83 = (bf16[7,512,512]{2,1,0:T(8,128)(2,1)S(1)}, f32[512,512]{1,0:T(8,128)S(1)}, bf16[512,80]{1,0:T(8,128)(2,1)S(1)}, f32[512,7]{1,0:T(8,128)S(1)}, f32[512,7]{1,0:T(8,128)S(1)}) custom-call(bf16[416,512]{1,0:T(8,128)(2,1)S(1)} %get-tuple-element.15.early_ref, bf16[160,512]{1,0:T(8,128)(2,1)S(1)} %get-tuple-element.14.late_ref, ...), custom_call_target="tpu_custom_call" | custom-call | tf_op jit(solution)/shard_map/pallas_call | solution.py:256
  10.5 3.5 %collective-permute-done.1.white_ref = bf16[416,512]{1,0:T(8,128)(2,1)S(1)} collective-permute-done((bf16[416,512]{1,0:T(8,128)(2,1)S(1)}, bf16[416,512]{1,0:T(8,128)(2,1)S(1)}, u32[]{:S(2)}, u32[]{:S(2)}) %collective-permute-start.1) | collective-permute-done | bytes 426016 | tf_op jit(solution)/shard_map/ppermute | solution.py:294
  14.0 1.2 %shard_map.84 = (f32[512,512]{1,0:T(8,128)S(1)}, f32[32,8,128]{2,1,0:T(8,128)S(1)}) custom-call(bf16[416,512]{1,0:T(8,128)(2,1)S(1)} %collective-permute-done.1.white_ref, bf16[7,512,512]{2,1,0:T(8,128)(2,1)S(1)} %get-tuple-element.16.source_ref, bf16[512,80]{1,0:T(8,128)(2,1)S(1)} %get-tuple-element.17.next_ref, f32[512,512]{1,0:T(8,128)S(1)} %get-tuple-element.18.sum_ref, ...), custom_call_target="tpu_custom_call" | custom-call | tf_op jit(solution)/shard_map/pallas_call | solution.py:256
  15.2 0.6 %collective-permute-done.white_ref = bf16[160,512]{1,0:T(8,128)(2,1)S(1)} collective-permute-done((bf16[160,512]{1,0:T(8,128)(2,1)S(1)}, bf16[160,512]{1,0:T(8,128)(2,1)S(1)}, u32[]{:S(2)}, u32[]{:S(2)}) %collective-permute-start) | collective-permute-done | bytes 163872 | tf_op jit(solution)/shard_map/ppermute | solution.py:295
  15.8 0.0 copy-start
  15.8 0.0 copy-start.1
  15.8 0.5 %shard_map.85 = bf16[32,72,128]{2,1,0:T(8,128)(2,1)S(1)} custom-call(bf16[160,512]{1,0:T(8,128)(2,1)S(1)} %collective-permute-done.white_ref, bf16[7,512,512]{2,1,0:T(8,128)(2,1)S(1)} %get-tuple-element.16.source_ref, bf16[512,80]{1,0:T(8,128)(2,1)S(1)} %get-tuple-element.17.next_ref, f32[512,512]{1,0:T(8,128)S(1)} %get-tuple-element.21.sum_ref, ...), custom_call_target="tpu_custom_call" | custom-call | tf_op jit(solution)/shard_map/pallas_call | solution.py:256
  16.3 22.1 %all_to_all.5.x_ref = bf16[32,72,128]{2,1,0:T(8,128)(2,1)S(1)} all-to-all(bf16[32,72,128]{2,1,0:T(8,128)(2,1)S(1)} %shard_map.85), channel_id=1, replica_groups=mesh['chan'=8,'nbr'=4] {'chan','nbr'}, dimensions={0} | all-to-all | bytes 1179648 | tf_op jit(solution)/shard_map/all_to_all | solution.py:324
  38.4 0.0 copy-done
  38.4 0.0 copy-done.1
  38.4 1.5 %shard_map.86 = f32[8,16,1024]{2,1,0:T(8,128)} custom-call(bf16[32,72,128]{2,1,0:T(8,128)(2,1)S(1)} %all_to_all.5.x_ref, bf16[512,1024]{1,0:T(8,128)(2,1)S(1)} %copy-done.1, bf16[512,1024]{1,0:T(8,128)(2,1)S(1)} %copy-done), custom_call_target="tpu_custom_call" | custom-call | tf_op jit(solution)/shard_map/pallas_call | solution.py:256
Async XLA Ops:
  0.0 7.6 %copy-start.2 = (s32[80,7]{0,1:T(8,128)S(1)}, s32[80,7]{0,1:T(8,128)}, u32[]{:S(2)}) copy-start(s32[80,7]{0,1:T(8,128)} %param.9) | copy-start | bytes 6724
  0.0 7.6 %copy-start.4 = (s32[1,8]{1,0:T(1,128)S(1)}, s32[1,8]{1,0:T(1,128)}, u32[]{:S(2)}) copy-start(s32[1,8]{1,0:T(1,128)} %count_ref.1) | copy-start | bytes 100
  0.0 7.6 %copy-start.3 = (s32[1,2,8,64]{3,2,1,0:T(8,128)S(1)}, s32[1,2,8,64]{3,2,1,0:T(8,128)}, u32[]{:S(2)}) copy-start(s32[1,2,8,64]{3,2,1,0:T(8,128)} %list_ref.1) | copy-start | bytes 12292
  3.7 10.3 %collective-permute-start.1 = (bf16[416,512]{1,0:T(8,128)(2,1)S(1)}, bf16[416,512]{1,0:T(8,128)(2,1)S(1)}, u32[]{:S(2)}, u32[]{:S(2)}) collective-permute-start(bf16[416,512]{1,0:T(8,128)(2,1)S(1)} %get-tuple-element.15.early_ref), channel_id=1, source_target_pairs={{4,0},{8,4},{12,8},{16,12},{20,16},{24,20},{28,24},{5,1},{9,5},{13... | collective-permute-start | bytes 1277960 | tf_op jit(solution)/shard_map/ppermute | solution.py:294
  5.7 10.1 %collective-permute-start = (bf16[160,512]{1,0:T(8,128)(2,1)S(1)}, bf16[160,512]{1,0:T(8,128)(2,1)S(1)}, u32[]{:S(2)}, u32[]{:S(2)}) collective-permute-start(bf16[160,512]{1,0:T(8,128)(2,1)S(1)} %get-tuple-element.14.late_ref), channel_id=1, source_target_pairs={{4,0},{8,4},{12,8},{16,12},{20,16},{24,20},{28,24},{5,1},{9,5},{13... | collective-permute-start | bytes 491528 | tf_op jit(solution)/shard_map/ppermute | solution.py:295
  15.8 22.6 %copy-start = (bf16[512,1024]{1,0:T(8,128)(2,1)S(1)}, bf16[512,1024]{1,0:T(8,128)(2,1)}, u32[]{:S(2)}) copy-start(bf16[512,1024]{1,0:T(8,128)(2,1)} %constant.11.clone.low_ref) | copy-start | bytes 3145732
  15.8 22.6 %copy-start.1 = (bf16[512,1024]{1,0:T(8,128)(2,1)S(1)}, bf16[512,1024]{1,0:T(8,128)(2,1)}, u32[]{:S(2)}) copy-start(bf16[512,1024]{1,0:T(8,128)(2,1)} %constant.10.clone.high_ref) | copy-start | bytes 3145732

commit v5 on v4

--- a/solution.py
+++ b/solution.py
@@ -20,8 +20,7 @@
 SMEM = pl.BlockSpec(memory_space=pltpu.SMEM)
 
 EVEN, ODD = np.arange(2, NF + 1, 2), np.arange(1, NF + 1, 2)
-FIRST = 5
-GROUP = 3
+FIRST = 4
 STEP = 512
 
 
@@ -93,38 +92,38 @@
     ]
 
 
-def whiten_kernel(x_hbm, mark_hbm, table_hbm, taper_hbm, early_ref, late_ref, x, mark, table, window, row, sem):
+def first_kernel(x_hbm, mark_hbm, table_hbm, taper_hbm, early_ref, rest, table, window, factors, x, mark, row, sem):
     total, rows, _ = x_hbm.shape
-    early = early_ref.shape[0] // rows
+    early = x.shape[0]
     small = [
         pltpu.make_async_copy(mark_hbm, mark, sem.at[0]),
         pltpu.make_async_copy(taper_hbm, window, sem.at[1]),
     ]
-    tables = pltpu.make_async_copy(table_hbm, table, sem.at[2])
-    groups = [
-        pltpu.make_async_copy(x_hbm.at[pl.ds(a, b - a)], x.at[pl.ds(a, b - a)], sem.at[3 + i])
-        for i, (a, b) in enumerate(((0, GROUP), (GROUP, total)))
+    large = [
+        pltpu.make_async_copy(table_hbm, table, sem.at[2]),
+        pltpu.make_async_copy(x_hbm.at[pl.ds(0, early)], x, sem.at[3]),
+        pltpu.make_async_copy(x_hbm.at[pl.ds(early, total - early)], rest, sem.at[4]),
     ]
-    for copy in small + [tables] + groups:
+    for copy in small + large[:2]:
         copy.start()
     for copy in small:
         copy.wait()
+    large[2].start()
     flags = [as_column(mark[s : s + 1, :].astype(F32)) for s in range(total)]
+    factors[...] = jnp.concatenate(flags[early:], axis=0)
     row[...] = jnp.zeros(row.shape, F32)
     row[:total, :rows] = mark[...].astype(F32)
     early_ref[early * rows :, :] = row[...].astype(BF)
-    tables.wait()
-    for group, (start, stop) in zip(groups, ((0, GROUP), (GROUP, total))):
-        group.wait()
-        column = jnp.concatenate(flags[start:stop], axis=0)
-        for i, white in enumerate(whiten(x.at[start:stop], column, table, window)):
-            columns = slice(i * NF, (i + 1) * NF)
-            split = min(max(early - start, 0), stop - start) * rows
-            if split:
-                early_ref[start * rows : start * rows + split, columns] = white[:split]
-            if split < white.shape[0]:
-                base = max(start - early, 0) * rows
-                late_ref[base : base + white.shape[0] - split, columns] = white[split:]
+    large[0].wait()
+    large[1].wait()
+    for i, white in enumerate(whiten(x, jnp.concatenate(flags[:early], axis=0), table, window)):
+        early_ref[: early * rows, i * NF : (i + 1) * NF] = white
+    large[2].wait()
+
+
+def second_kernel(x_ref, table_ref, window_ref, factor_ref, late_ref):
+    for i, white in enumerate(whiten(x_ref, factor_ref[...], table_ref, window_ref)):
+        late_ref[:, i * NF : (i + 1) * NF] = white
 
 
 def add_products(real, imag, a, b):
@@ -276,20 +275,30 @@
     tables = forward_tables(span)
     inputs = (jnp.transpose(records, (1, 0, 2)), gap_mask.T, jnp.asarray(tables), jnp.asarray(taper()))
     extra = -(-segs // 16) * 16
-    early, late = call(
-        whiten_kernel,
-        [shape((FIRST * rows + extra, width), BF), shape(((segs - FIRST) * rows, width), BF)],
+    early, rest, table, window, factors = call(
+        first_kernel,
+        [
+            shape((FIRST * rows + extra, width), BF),
+            shape((segs - FIRST, rows, span), F32),
+            shape(tables.shape, BF),
+            shape((1, width), F32),
+            shape(((segs - FIRST) * rows, 1), F32),
+        ],
         [pltpu.with_memory_space_constraint(v, pltpu.HBM) for v in inputs],
         [HBM] * 4,
         [
-            pltpu.VMEM((segs, rows, span), F32),
+            pltpu.VMEM((FIRST, rows, span), F32),
             pltpu.VMEM((segs, rows), jnp.int32),
-            pltpu.VMEM(tables.shape, BF),
-            pltpu.VMEM((1, width), F32),
             pltpu.VMEM((extra, width), F32),
             pltpu.SemaphoreType.DMA((5,)),
         ],
         mib=32,
+    )
+    (late,) = call(
+        second_kernel,
+        [shape(((segs - FIRST) * rows, width), BF)],
+        (rest, table, window, factors),
+        [VMEM] * 4,
     )
     next_early = lax.ppermute(early, "chan", back)
     next_late = lax.ppermute(late, "chan", back)

time: 40.1 us -> 39.6 us (0.988)
  waiting for transfers between devices: 4.08 us -> 3.4 us
    ppermute x1, waiting for transfers between devices: 3.51 us -> 1.75 us  [local(): next_early = lax.ppermute(early, 'chan', back)]
    ppermute x1, waiting for transfers between devices: 0.57 us -> 1.65 us  [local(): next_late = lax.ppermute(late, 'chan', back)]
    pallas_call x5 -> x6, Pallas kernels: 9.72 us -> 9.86 us  [call(): pl.pallas_call(kernel, out_shape=shape, in_specs=specs, out_specs=[VMEM]...]
  transfers between devices with their start and end apart: 2 -> 2, of which waited for: 2 -> 2; matrix products, arithmetic and copies ran while one was open for 0% -> 0% of each run, Pallas kernels for 10% -> 12%
where the time goes in v5:
time: 39.6 us; the launch traced here: 39.4 us
  blocking collectives  22.1 us (56%)
  Pallas kernels  9.86 us (25%)
  starting transfers between devices  3.89 us (10%)
  waiting for transfers between devices  3.4 us (9%)
    all_to_all x1, blocking collectives, local(): lax.all_to_all(cross, ('chan', 'nbr'), split_axis=0, concat_axis=0, tiled...  22.1 us
    pallas_call x6, Pallas kernels, call(): pl.pallas_call(kernel, out_shape=shape, in_specs=specs, out_specs=[VMEM]...  9.86 us
    ppermute x1, starting transfers between devices, local(): next_early = lax.ppermute(early, 'chan', back)  1.97 us
    ppermute x1, starting transfers between devices, local(): next_late = lax.ppermute(late, 'chan', back)  1.92 us
    ppermute x1, waiting for transfers between devices, local(): next_early = lax.ppermute(early, 'chan', back)  1.75 us
    ppermute x1, waiting for transfers between devices, local(): next_late = lax.ppermute(late, 'chan', back)  1.65 us
  transfers between devices with their start and end apart: 2, of which 2 were waited for; matrix products, arithmetic and copies ran while one was open for 0% of the time, Pallas kernels for 12%

profile of v5, /device:TPU:1, one launch (start us, length us, event | category | flops | bytes accessed | tf_op | source)
XLA Modules:
  0.0 39.4 jit_solution(11819396734533637968)
XLA Ops:
  0.0 2.9 %shard_map.82 = (bf16[336,512]{1,0:T(8,128)(2,1)S(1)}, f32[3,80,1280]{2,1,0:T(8,128)S(1)}, bf16[2,1280,256]{2,1,0:T(8,128)(2,1)S(1)}, f32[1,512]{1,0:T(1,128)S(1)}, f32[240,1]{1,0:T(8,128)S(1)}) custom-call(f32[7,80,1280]{2,1,0:T(8,128)} %bitcast.5, s32[7,80]{1,0:T(8,128)} %bitcast.3, bf16[2,1280,256]{2,1,0:T(8,128)(2,1)} %constant.8.clone.table_hbm, ...), custom_call_target="tpu_custom_call" | custom-call | tf_op jit(solution)/shard_map/pallas_call | solution.py:255
  2.9 2.0 %collective-permute-start.1 = (bf16[336,512]{1,0:T(8,128)(2,1)S(1)}, bf16[336,512]{1,0:T(8,128)(2,1)S(1)}, u32[]{:S(2)}, u32[]{:S(2)}) collective-permute-start(bf16[336,512]{1,0:T(8,128)(2,1)S(1)} %get-tuple-element.21.early_ref), channel_id=1, source_target_pairs={{4,0},{8,4},{12,8},{16,12},{20,16},{24,20},{28,24},{5,1},{9,5},{13... | collective-permute-start | bytes 1032200 | tf_op jit(solution)/shard_map/ppermute | solution.py:303
  4.9 0.0 copy-start.2
  4.9 0.0 copy-start.3
  4.9 0.0 copy-start.4
  4.9 0.8 %shard_map.83.late_ref = bf16[240,512]{1,0:T(8,128)(2,1)S(1)} custom-call(f32[3,80,1280]{2,1,0:T(8,128)S(1)} %get-tuple-element.17.x_ref, bf16[2,1280,256]{2,1,0:T(8,128)(2,1)S(1)} %get-tuple-element.18.table_ref, f32[1,512]{1,0:T(1,128)S(1)} %get-tuple-element.19.window_ref, f32[240,1]{1,0:T(8,128)S(1)} %get-tuple-element.20.factor_ref), custom_call_target="tpu_custom_call" | custom-call | tf_op jit(solution)/shard_map/pallas_call | solution.py:255
  5.8 1.9 %collective-permute-start = (bf16[240,512]{1,0:T(8,128)(2,1)S(1)}, bf16[240,512]{1,0:T(8,128)(2,1)S(1)}, u32[]{:S(2)}, u32[]{:S(2)}) collective-permute-start(bf16[240,512]{1,0:T(8,128)(2,1)S(1)} %shard_map.83.late_ref), channel_id=1, source_target_pairs={{4,0},{8,4},{12,8},{16,12},{20,16},{24,20},{28,24},{5,1},{9,5},{13... | collective-permute-start | bytes 737288 | tf_op jit(solution)/shard_map/ppermute | solution.py:304
  7.7 0.0 copy-done.2
  7.7 0.0 copy-done.3
  7.7 0.0 copy-done.4
  7.7 2.9 %shard_map.84 = (bf16[7,512,512]{2,1,0:T(8,128)(2,1)S(1)}, f32[512,512]{1,0:T(8,128)S(1)}, bf16[512,80]{1,0:T(8,128)(2,1)S(1)}, f32[512,7]{1,0:T(8,128)S(1)}, f32[512,7]{1,0:T(8,128)S(1)}) custom-call(bf16[336,512]{1,0:T(8,128)(2,1)S(1)} %get-tuple-element.21.early_ref, bf16[240,512]{1,0:T(8,128)(2,1)S(1)} %shard_map.83.late_ref, s32[7,80]{1,0:T(8,128)S(1)} %bitcast.4, ...), custom_call_target="tpu_custom_call" | custom-call | tf_op jit(solution)/shard_map/pallas_call | solution.py:255
  10.6 1.8 %collective-permute-done.1.white_ref = bf16[336,512]{1,0:T(8,128)(2,1)S(1)} collective-permute-done((bf16[336,512]{1,0:T(8,128)(2,1)S(1)}, bf16[336,512]{1,0:T(8,128)(2,1)S(1)}, u32[]{:S(2)}, u32[]{:S(2)}) %collective-permute-start.1) | collective-permute-done | bytes 344096 | tf_op jit(solution)/shard_map/ppermute | solution.py:303
  12.4 1.0 %shard_map.85 = (f32[512,512]{1,0:T(8,128)S(1)}, f32[32,8,128]{2,1,0:T(8,128)S(1)}) custom-call(bf16[336,512]{1,0:T(8,128)(2,1)S(1)} %collective-permute-done.1.white_ref, bf16[7,512,512]{2,1,0:T(8,128)(2,1)S(1)} %get-tuple-element.22.source_ref, bf16[512,80]{1,0:T(8,128)(2,1)S(1)} %get-tuple-element.23.next_ref, f32[512,512]{1,0:T(8,128)S(1)} %get-tuple-element.24.sum_ref, ...), custom_call_target="tpu_custom_call" | custom-call | tf_op jit(solution)/shard_map/pallas_call | solution.py:255
  13.3 1.7 %collective-permute-done.white_ref = bf16[240,512]{1,0:T(8,128)(2,1)S(1)} collective-permute-done((bf16[240,512]{1,0:T(8,128)(2,1)S(1)}, bf16[240,512]{1,0:T(8,128)(2,1)S(1)}, u32[]{:S(2)}, u32[]{:S(2)}) %collective-permute-start) | collective-permute-done | bytes 245792 | tf_op jit(solution)/shard_map/ppermute | solution.py:304
  15.0 0.0 copy-start.1
  15.0 0.8 %shard_map.86 = bf16[32,72,128]{2,1,0:T(8,128)(2,1)S(1)} custom-call(bf16[240,512]{1,0:T(8,128)(2,1)S(1)} %collective-permute-done.white_ref, bf16[7,512,512]{2,1,0:T(8,128)(2,1)S(1)} %get-tuple-element.22.source_ref, bf16[512,80]{1,0:T(8,128)(2,1)S(1)} %get-tuple-element.23.next_ref, f32[512,512]{1,0:T(8,128)S(1)} %get-tuple-element.27.sum_ref, ...), custom_call_target="tpu_custom_call" | custom-call | tf_op jit(solution)/shard_map/pallas_call | solution.py:255
  15.8 0.0 copy-start
  15.8 22.1 %all_to_all.5.x_ref = bf16[32,72,128]{2,1,0:T(8,128)(2,1)S(1)} all-to-all(bf16[32,72,128]{2,1,0:T(8,128)(2,1)S(1)} %shard_map.86), channel_id=1, replica_groups=mesh['chan'=8,'nbr'=4] {'chan','nbr'}, dimensions={0} | all-to-all | bytes 1179648 | tf_op jit(solution)/shard_map/all_to_all | solution.py:333
  37.9 0.0 copy-done.1
  37.9 0.0 copy-done
  37.9 1.5 %shard_map.87 = f32[8,16,1024]{2,1,0:T(8,128)} custom-call(bf16[32,72,128]{2,1,0:T(8,128)(2,1)S(1)} %all_to_all.5.x_ref, bf16[512,1024]{1,0:T(8,128)(2,1)S(1)} %copy-done.1, bf16[512,1024]{1,0:T(8,128)(2,1)S(1)} %copy-done), custom_call_target="tpu_custom_call" | custom-call | tf_op jit(solution)/shard_map/pallas_call | solution.py:255
Async XLA Ops:
  2.9 9.4 %collective-permute-start.1 = (bf16[336,512]{1,0:T(8,128)(2,1)S(1)}, bf16[336,512]{1,0:T(8,128)(2,1)S(1)}, u32[]{:S(2)}, u32[]{:S(2)}) collective-permute-start(bf16[336,512]{1,0:T(8,128)(2,1)S(1)} %get-tuple-element.21.early_ref), channel_id=1, source_target_pairs={{4,0},{8,4},{12,8},{16,12},{20,16},{24,20},{28,24},{5,1},{9,5},{13... | collective-permute-start | bytes 1032200 | tf_op jit(solution)/shard_map/ppermute | solution.py:303
  4.9 2.8 %copy-start.2 = (s32[80,7]{0,1:T(8,128)S(1)}, s32[80,7]{0,1:T(8,128)}, u32[]{:S(2)}) copy-start(s32[80,7]{0,1:T(8,128)} %param.9) | copy-start | bytes 6724
  4.9 2.8 %copy-start.3 = (s32[1,2,8,64]{3,2,1,0:T(8,128)S(1)}, s32[1,2,8,64]{3,2,1,0:T(8,128)}, u32[]{:S(2)}) copy-start(s32[1,2,8,64]{3,2,1,0:T(8,128)} %list_ref.1) | copy-start | bytes 12292
  4.9 2.8 %copy-start.4 = (s32[1,8]{1,0:T(1,128)S(1)}, s32[1,8]{1,0:T(1,128)}, u32[]{:S(2)}) copy-start(s32[1,8]{1,0:T(1,128)} %count_ref.1) | copy-start | bytes 100
  5.8 9.2 %collective-permute-start = (bf16[240,512]{1,0:T(8,128)(2,1)S(1)}, bf16[240,512]{1,0:T(8,128)(2,1)S(1)}, u32[]{:S(2)}, u32[]{:S(2)}) collective-permute-start(bf16[240,512]{1,0:T(8,128)(2,1)S(1)} %shard_map.83.late_ref), channel_id=1, source_target_pairs={{4,0},{8,4},{12,8},{16,12},{20,16},{24,20},{28,24},{5,1},{9,5},{13... | collective-permute-start | bytes 737288 | tf_op jit(solution)/shard_map/ppermute | solution.py:304
  15.0 22.9 %copy-start.1 = (bf16[512,1024]{1,0:T(8,128)(2,1)S(1)}, bf16[512,1024]{1,0:T(8,128)(2,1)}, u32[]{:S(2)}) copy-start(bf16[512,1024]{1,0:T(8,128)(2,1)} %constant.10.clone.high_ref) | copy-start | bytes 3145732
  15.8 22.1 %copy-start = (bf16[512,1024]{1,0:T(8,128)(2,1)S(1)}, bf16[512,1024]{1,0:T(8,128)(2,1)}, u32[]{:S(2)}) copy-start(bf16[512,1024]{1,0:T(8,128)(2,1)} %constant.11.clone.low_ref) | copy-start | bytes 3145732

commit v6 on v5

--- a/solution.py
+++ b/solution.py
@@ -22,6 +22,7 @@
 EVEN, ODD = np.arange(2, NF + 1, 2), np.arange(1, NF + 1, 2)
 FIRST = 4
 STEP = 512
+HALVES = 2
 
 
 def two_parts(table):
@@ -163,7 +164,7 @@
                 ref, base = (early_ref, s) if s < FIRST else (late_ref, s - FIRST)
                 white = ref[base * rows : (base + 1) * rows, columns]
                 a = dot(a_hot, white)
-                source_ref[s, at, columns] = a.astype(BF)
+                source_ref[s, at, columns] = a
                 real, imag = add_products(real, imag, a, dot(b_hot, white))
             sum_ref[at, h * NF : h * NF + quad] = real
             sum_ref[at, h * NF + quad : (h + 1) * NF] = imag
@@ -180,7 +181,7 @@
         columns = slice(h * NF, (h + 1) * NF)
         real, imag = sums[at, h * NF : h * NF + quad], sums[at, h * NF + quad : (h + 1) * NF]
         for s in range(segs):
-            a = source_ref[base + s, at, columns].astype(F32)
+            a = source_ref[base + s, at, columns]
             real, imag = add_products(real, imag, a, dot(hot, white_ref[s * rows : (s + 1) * rows, columns]))
         result += [real, imag]
     return result
@@ -231,7 +232,7 @@
     lax.fori_loop(0, pairs // step, body, 0)
 
 
-def lags_kernel(parts, per, x_ref, high_ref, low_ref, out_ref):
+def lags_kernel(parts, per, x_ref, high_ref, low_ref, out_hbm, held, sem):
     dests, length, _ = x_ref.shape
     blocks = 2 * NF // LANES
     total = jnp.sum(x_ref[...].astype(F32).reshape(dests // parts, parts, length, LANES), axis=1)
@@ -247,16 +248,27 @@
         axis=1,
     )
     coarse, fine = halves(stacked)
-    traces = dot(coarse, high_ref[...]) + dot(fine, high_ref[...]) + dot(coarse, low_ref[...])
-    out_ref[...] = traces.reshape(out_ref.shape)
-
-
-def call(kernel, shape, args, specs, scratch=(), mib=24):
+    both = jnp.concatenate([coarse, fine], axis=0)
+    count = stacked.shape[0]
+    copies = []
+    for k in range(HALVES):
+        columns = slice(k * NLAG // HALVES, (k + 1) * NLAG // HALVES)
+        product = dot(both, high_ref[:, columns])
+        traces = product[:count] + product[count:] + dot(coarse, low_ref[:, columns])
+        held[:, :, columns] = traces.reshape(held.shape[0], held.shape[1], -1)
+        part = pl.ds(k * NLAG // HALVES, NLAG // HALVES)
+        copies.append(pltpu.make_async_copy(held.at[:, :, part], out_hbm.at[:, :, part], sem.at[k]))
+        copies[-1].start()
+    for copy in copies:
+        copy.wait()
+
+
+def call(kernel, shape, args, specs, scratch=(), mib=24, out=VMEM):
     return pl.pallas_call(
         kernel,
         out_shape=shape,
         in_specs=specs,
-        out_specs=[VMEM] * len(shape),
+        out_specs=[out] * len(shape),
         scratch_shapes=list(scratch),
         compiler_params=pltpu.CompilerParams(vmem_limit_bytes=mib << 20),
     )(*args)
@@ -305,7 +317,7 @@
     source, sums, hot, source_marks, own_marks = call(
         functools.partial(sources_kernel, step),
         [
-            shape((segs, pairs, width), BF),
+            shape((segs, pairs, width), F32),
             shape((pairs, width), F32),
             shape((pairs, rows), BF),
             shape((pairs, segs), F32),
@@ -337,6 +349,8 @@
         [shape((chan, per, NLAG), F32)],
         (arrived, jnp.asarray(high), jnp.asarray(low)),
         [VMEM] * 3,
+        [pltpu.VMEM((chan, per, NLAG), F32), pltpu.SemaphoreType.DMA((HALVES,))],
+        out=HBM,
     )
     return traces[None]
 

time: 39.6 us -> 39.4 us (level)
  no operation moved by 1% of the time
where the time goes in v6:
time: 39.4 us; the launch traced here: 39.2 us
  blocking collectives  22.1 us (56%)
  Pallas kernels  9.5 us (24%)
  starting transfers between devices  3.89 us (10%)
  waiting for transfers between devices  3.54 us (9%)
    all_to_all x1, blocking collectives, local(): lax.all_to_all(cross, ('chan', 'nbr'), split_axis=0, concat_axis=0, tiled...  22.1 us
    pallas_call x6, Pallas kernels, call(): pl.pallas_call(kernel, out_shape=shape, in_specs=specs, out_specs=[out] *...  9.5 us
    ppermute x1, starting transfers between devices, local(): next_early = lax.ppermute(early, 'chan', back)  1.97 us
    ppermute x1, starting transfers between devices, local(): next_late = lax.ppermute(late, 'chan', back)  1.92 us
    ppermute x1, waiting for transfers between devices, local(): next_late = lax.ppermute(late, 'chan', back)  1.79 us
    ppermute x1, waiting for transfers between devices, local(): next_early = lax.ppermute(early, 'chan', back)  1.75 us
  transfers between devices with their start and end apart: 2, of which 2 were waited for; matrix products, arithmetic and copies ran while one was open for 0% of the time, Pallas kernels for 12%

profile of v6, /device:TPU:1, one launch (start us, length us, event | category | flops | bytes accessed | tf_op | source)
XLA Modules:
  0.0 39.2 jit_solution(441424925345214532)
XLA Ops:
  0.0 2.9 %shard_map.82 = (bf16[336,512]{1,0:T(8,128)(2,1)S(1)}, f32[3,80,1280]{2,1,0:T(8,128)S(1)}, bf16[2,1280,256]{2,1,0:T(8,128)(2,1)S(1)}, f32[1,512]{1,0:T(1,128)S(1)}, f32[240,1]{1,0:T(8,128)S(1)}) custom-call(f32[7,80,1280]{2,1,0:T(8,128)} %bitcast.5, s32[7,80]{1,0:T(8,128)} %bitcast.3, bf16[2,1280,256]{2,1,0:T(8,128)(2,1)} %constant.8.clone.table_hbm, ...), custom_call_target="tpu_custom_call" | custom-call | tf_op jit(solution)/shard_map/pallas_call | solution.py:267
  2.9 2.0 %collective-permute-start.1 = (bf16[336,512]{1,0:T(8,128)(2,1)S(1)}, bf16[336,512]{1,0:T(8,128)(2,1)S(1)}, u32[]{:S(2)}, u32[]{:S(2)}) collective-permute-start(bf16[336,512]{1,0:T(8,128)(2,1)S(1)} %get-tuple-element.21.early_ref), channel_id=1, source_target_pairs={{4,0},{8,4},{12,8},{16,12},{20,16},{24,20},{28,24},{5,1},{9,5},{13... | collective-permute-start | bytes 1032200 | tf_op jit(solution)/shard_map/ppermute | solution.py:315
  4.9 0.0 copy-start.2
  4.9 0.0 copy-start.3
  4.9 0.0 copy-start.4
  4.9 0.8 %shard_map.83.late_ref = bf16[240,512]{1,0:T(8,128)(2,1)S(1)} custom-call(f32[3,80,1280]{2,1,0:T(8,128)S(1)} %get-tuple-element.17.x_ref, bf16[2,1280,256]{2,1,0:T(8,128)(2,1)S(1)} %get-tuple-element.18.table_ref, f32[1,512]{1,0:T(1,128)S(1)} %get-tuple-element.19.window_ref, f32[240,1]{1,0:T(8,128)S(1)} %get-tuple-element.20.factor_ref), custom_call_target="tpu_custom_call" | custom-call | tf_op jit(solution)/shard_map/pallas_call | solution.py:267
  5.8 1.9 %collective-permute-start = (bf16[240,512]{1,0:T(8,128)(2,1)S(1)}, bf16[240,512]{1,0:T(8,128)(2,1)S(1)}, u32[]{:S(2)}, u32[]{:S(2)}) collective-permute-start(bf16[240,512]{1,0:T(8,128)(2,1)S(1)} %shard_map.83.late_ref), channel_id=1, source_target_pairs={{4,0},{8,4},{12,8},{16,12},{20,16},{24,20},{28,24},{5,1},{9,5},{13... | collective-permute-start | bytes 737288 | tf_op jit(solution)/shard_map/ppermute | solution.py:316
  7.7 0.0 copy-done.2
  7.7 0.0 copy-done.3
  7.7 0.0 copy-done.4
  7.7 2.9 %shard_map.84 = (f32[7,512,512]{2,1,0:T(8,128)S(1)}, f32[512,512]{1,0:T(8,128)S(1)}, bf16[512,80]{1,0:T(8,128)(2,1)S(1)}, f32[512,7]{1,0:T(8,128)S(1)}, f32[512,7]{1,0:T(8,128)S(1)}) custom-call(bf16[336,512]{1,0:T(8,128)(2,1)S(1)} %get-tuple-element.21.early_ref, bf16[240,512]{1,0:T(8,128)(2,1)S(1)} %shard_map.83.late_ref, s32[7,80]{1,0:T(8,128)S(1)} %bitcast.4, ...), custom_call_target="tpu_custom_call" | custom-call | tf_op jit(solution)/shard_map/pallas_call | solution.py:267
  10.6 1.8 %collective-permute-done.1.white_ref = bf16[336,512]{1,0:T(8,128)(2,1)S(1)} collective-permute-done((bf16[336,512]{1,0:T(8,128)(2,1)S(1)}, bf16[336,512]{1,0:T(8,128)(2,1)S(1)}, u32[]{:S(2)}, u32[]{:S(2)}) %collective-permute-start.1) | collective-permute-done | bytes 344096 | tf_op jit(solution)/shard_map/ppermute | solution.py:315
  12.4 0.8 %shard_map.85 = (f32[512,512]{1,0:T(8,128)S(1)}, f32[32,8,128]{2,1,0:T(8,128)S(1)}) custom-call(bf16[336,512]{1,0:T(8,128)(2,1)S(1)} %collective-permute-done.1.white_ref, f32[7,512,512]{2,1,0:T(8,128)S(1)} %get-tuple-element.22.source_ref, bf16[512,80]{1,0:T(8,128)(2,1)S(1)} %get-tuple-element.23.next_ref, f32[512,512]{1,0:T(8,128)S(1)} %get-tuple-element.24.sum_ref, ...), custom_call_target="tpu_custom_call" | custom-call | tf_op jit(solution)/shard_map/pallas_call | solution.py:267
  13.2 1.8 %collective-permute-done.white_ref = bf16[240,512]{1,0:T(8,128)(2,1)S(1)} collective-permute-done((bf16[240,512]{1,0:T(8,128)(2,1)S(1)}, bf16[240,512]{1,0:T(8,128)(2,1)S(1)}, u32[]{:S(2)}, u32[]{:S(2)}) %collective-permute-start) | collective-permute-done | bytes 245792 | tf_op jit(solution)/shard_map/ppermute | solution.py:316
  15.0 0.0 copy-start.1
  15.0 0.6 %shard_map.86 = bf16[32,72,128]{2,1,0:T(8,128)(2,1)S(1)} custom-call(bf16[240,512]{1,0:T(8,128)(2,1)S(1)} %collective-permute-done.white_ref, f32[7,512,512]{2,1,0:T(8,128)S(1)} %get-tuple-element.22.source_ref, bf16[512,80]{1,0:T(8,128)(2,1)S(1)} %get-tuple-element.23.next_ref, f32[512,512]{1,0:T(8,128)S(1)} %get-tuple-element.27.sum_ref, ...), custom_call_target="tpu_custom_call" | custom-call | tf_op jit(solution)/shard_map/pallas_call | solution.py:267
  15.6 0.0 copy-start
  15.6 22.1 %all_to_all.5.x_ref = bf16[32,72,128]{2,1,0:T(8,128)(2,1)S(1)} all-to-all(bf16[32,72,128]{2,1,0:T(8,128)(2,1)S(1)} %shard_map.86), channel_id=1, replica_groups=mesh['chan'=8,'nbr'=4] {'chan','nbr'}, dimensions={0} | all-to-all | bytes 1179648 | tf_op jit(solution)/shard_map/all_to_all | solution.py:345
  37.7 0.0 copy-done.1
  37.7 0.0 copy-done
  37.8 1.4 %shard_map.87 = f32[8,16,1024]{2,1,0:T(8,128)} custom-call(bf16[32,72,128]{2,1,0:T(8,128)(2,1)S(1)} %all_to_all.5.x_ref, bf16[512,1024]{1,0:T(8,128)(2,1)S(1)} %copy-done.1, bf16[512,1024]{1,0:T(8,128)(2,1)S(1)} %copy-done), custom_call_target="tpu_custom_call" | custom-call | tf_op jit(solution)/shard_map/pallas_call | solution.py:267
Async XLA Ops:
  2.9 9.4 %collective-permute-start.1 = (bf16[336,512]{1,0:T(8,128)(2,1)S(1)}, bf16[336,512]{1,0:T(8,128)(2,1)S(1)}, u32[]{:S(2)}, u32[]{:S(2)}) collective-permute-start(bf16[336,512]{1,0:T(8,128)(2,1)S(1)} %get-tuple-element.21.early_ref), channel_id=1, source_target_pairs={{4,0},{8,4},{12,8},{16,12},{20,16},{24,20},{28,24},{5,1},{9,5},{13... | collective-permute-start | bytes 1032200 | tf_op jit(solution)/shard_map/ppermute | solution.py:315
  4.9 2.8 %copy-start.2 = (s32[80,7]{0,1:T(8,128)S(1)}, s32[80,7]{0,1:T(8,128)}, u32[]{:S(2)}) copy-start(s32[80,7]{0,1:T(8,128)} %param.9) | copy-start | bytes 6724
  4.9 2.8 %copy-start.3 = (s32[1,2,8,64]{3,2,1,0:T(8,128)S(1)}, s32[1,2,8,64]{3,2,1,0:T(8,128)}, u32[]{:S(2)}) copy-start(s32[1,2,8,64]{3,2,1,0:T(8,128)} %list_ref.1) | copy-start | bytes 12292
  4.9 2.8 %copy-start.4 = (s32[1,8]{1,0:T(1,128)S(1)}, s32[1,8]{1,0:T(1,128)}, u32[]{:S(2)}) copy-start(s32[1,8]{1,0:T(1,128)} %count_ref.1) | copy-start | bytes 100
  5.8 9.2 %collective-permute-start = (bf16[240,512]{1,0:T(8,128)(2,1)S(1)}, bf16[240,512]{1,0:T(8,128)(2,1)S(1)}, u32[]{:S(2)}, u32[]{:S(2)}) collective-permute-start(bf16[240,512]{1,0:T(8,128)(2,1)S(1)} %shard_map.83.late_ref), channel_id=1, source_target_pairs={{4,0},{8,4},{12,8},{16,12},{20,16},{24,20},{28,24},{5,1},{9,5},{13... | collective-permute-start | bytes 737288 | tf_op jit(solution)/shard_map/ppermute | solution.py:316
  15.0 22.8 %copy-start.1 = (bf16[512,1024]{1,0:T(8,128)(2,1)S(1)}, bf16[512,1024]{1,0:T(8,128)(2,1)}, u32[]{:S(2)}) copy-start(bf16[512,1024]{1,0:T(8,128)(2,1)} %constant.10.clone.high_ref) | copy-start | bytes 3145732
  15.6 22.1 %copy-start = (bf16[512,1024]{1,0:T(8,128)(2,1)S(1)}, bf16[512,1024]{1,0:T(8,128)(2,1)}, u32[]{:S(2)}) copy-start(bf16[512,1024]{1,0:T(8,128)(2,1)} %constant.11.clone.low_ref) | copy-start | bytes 3145732

commit v7 on v6

--- a/solution.py
+++ b/solution.py
@@ -89,11 +89,21 @@
     energy = jnp.sum(even * even + odd * odd, axis=1, keepdims=True) * (0.5 / NF)
     factor = flags / jnp.sqrt(energy + 1e-05)
     return [
-        (part * factor * taper_ref[:, i * NF : (i + 1) * NF]).astype(BF) for i, part in enumerate(found)
+        part * factor * taper_ref[:, i * NF : (i + 1) * NF] for i, part in enumerate(found)
     ]
 
 
-def first_kernel(x_hbm, mark_hbm, table_hbm, taper_hbm, early_ref, rest, table, window, factors, x, mark, row, sem):
+def share(found, keep_ref, give_ref, base):
+    odd = lax.axis_index("nbr") % 2 == 1
+    even_bins, odd_bins = found
+    rows = even_bins.shape[0]
+    keep_ref[base : base + rows, :] = jnp.where(odd, odd_bins, even_bins).astype(BF)
+    give_ref[...] = jnp.where(odd, even_bins, odd_bins).astype(BF)
+
+
+def first_kernel(
+    x_hbm, mark_hbm, table_hbm, taper_hbm, keep_ref, give_ref, rest, table, window, factors, mark_rows, x, mark, row, sem
+):
     total, rows, _ = x_hbm.shape
     early = x.shape[0]
     small = [
@@ -114,17 +124,20 @@
     factors[...] = jnp.concatenate(flags[early:], axis=0)
     row[...] = jnp.zeros(row.shape, F32)
     row[:total, :rows] = mark[...].astype(F32)
-    early_ref[early * rows :, :] = row[...].astype(BF)
+    mark_rows[...] = row[...].astype(BF)
     large[0].wait()
     large[1].wait()
-    for i, white in enumerate(whiten(x, jnp.concatenate(flags[:early], axis=0), table, window)):
-        early_ref[: early * rows, i * NF : (i + 1) * NF] = white
+    found = whiten(x, jnp.concatenate(flags[:early], axis=0), table, window)
+    share(found, keep_ref, give_ref, 0)
     large[2].wait()
 
 
-def second_kernel(x_ref, table_ref, window_ref, factor_ref, late_ref):
-    for i, white in enumerate(whiten(x_ref, factor_ref[...], table_ref, window_ref)):
-        late_ref[:, i * NF : (i + 1) * NF] = white
+def second_kernel(x_ref, table_ref, window_ref, factor_ref, early_ref, mark_rows, keep_ref, give_ref):
+    found = whiten(x_ref, factor_ref[...], table_ref, window_ref)
+    count = early_ref.shape[0]
+    keep_ref[:count, :] = early_ref[...]
+    share(found, keep_ref, give_ref, count)
+    keep_ref[count + give_ref.shape[0] :, :] = mark_rows[...]
 
 
 def add_products(real, imag, a, b):
@@ -133,13 +146,47 @@
     return real + (ar * br + ai * bi), imag + (ai * br - ar * bi)
 
 
+def first_terms(at, white_ref, segs, base, a_hot, b_hot, source_ref, real, imag):
+    rows = a_hot.shape[1]
+    for s in range(segs):
+        white = white_ref[s * rows : (s + 1) * rows, :]
+        a = dot(a_hot, white)
+        source_ref[base + s, at, :] = a
+        real, imag = add_products(real, imag, a, dot(b_hot, white))
+    return real, imag
+
+
+def more_terms(at, white_ref, segs, base, hot, source_ref, real, imag):
+    rows = hot.shape[1]
+    for s in range(segs):
+        b = dot(hot, white_ref[s * rows : (s + 1) * rows, :])
+        real, imag = add_products(real, imag, source_ref[base + s, at, :], b)
+    return real, imag
+
+
+def load_sums(sum_ref, at):
+    return sum_ref[at, : NF // 2], sum_ref[at, NF // 2 :]
+
+
+def store_sums(sum_ref, at, real, imag):
+    sum_ref[at, : NF // 2] = real
+    sum_ref[at, NF // 2 :] = imag
+
+
+def in_steps(step, pairs, body):
+    def run(i, carry):
+        body(i, pl.ds(pl.multiple_of(i * step, step), step))
+        return carry
+
+    lax.fori_loop(0, pairs // step, run, 0)
+
+
 def sources_kernel(
-    step, early_ref, late_ref, mark_ref, list_ref, count_ref,
-    source_ref, sum_ref, next_ref, source_mark_ref, own_mark_ref, first, own,
+    step, white_ref, mark_ref, list_ref, count_ref,
+    source_ref, sum_ref, first, own, next_ref, source_mark_ref, own_mark_ref,
 ):
     segs, rows = mark_ref.shape
     owners, slots = list_ref.shape[2:]
-    quad = NF // 2
     anchor = lax.axis_index("chan") * rows
     spots = lax.broadcasted_iota(jnp.int32, (slots, rows), 1).astype(F32)
     for o in range(owners):
@@ -152,56 +199,41 @@
         next_ref[where, :] = (spots == column - rows).astype(BF)
     marks = mark_ref[...].astype(BF)
 
-    def body(i, carry):
-        at = pl.ds(pl.multiple_of(i * step, step), step)
+    def body(i, at):
         a_hot, b_hot = first[at, :], own[at, :]
         source_mark_ref[at, :] = dot_across(a_hot, marks)
         own_mark_ref[at, :] = dot_across(b_hot, marks)
-        for h in range(2):
-            columns = slice(h * NF, (h + 1) * NF)
-            real = imag = jnp.zeros((step, quad), F32)
-            for s in range(segs):
-                ref, base = (early_ref, s) if s < FIRST else (late_ref, s - FIRST)
-                white = ref[base * rows : (base + 1) * rows, columns]
-                a = dot(a_hot, white)
-                source_ref[s, at, columns] = a
-                real, imag = add_products(real, imag, a, dot(b_hot, white))
-            sum_ref[at, h * NF : h * NF + quad] = real
-            sum_ref[at, h * NF + quad : (h + 1) * NF] = imag
-        return carry
-
-    lax.fori_loop(0, owners * slots // step, body, 0)
-
-
-def add_segments(at, segs, base, white_ref, source_ref, hot, sums):
-    quad = NF // 2
-    rows = hot.shape[1]
-    result = []
-    for h in range(2):
-        columns = slice(h * NF, (h + 1) * NF)
-        real, imag = sums[at, h * NF : h * NF + quad], sums[at, h * NF + quad : (h + 1) * NF]
-        for s in range(segs):
-            a = source_ref[base + s, at, columns]
-            real, imag = add_products(real, imag, a, dot(hot, white_ref[s * rows : (s + 1) * rows, columns]))
-        result += [real, imag]
-    return result
+        zero = jnp.zeros((step, NF // 2), F32)
+        store_sums(sum_ref, at, *first_terms(at, white_ref, segs, 0, a_hot, b_hot, source_ref, zero, zero))
+
+    in_steps(step, owners * slots, body)
+
+
+def given_kernel(step, early_ref, late_ref, first, own, sum_ref, source_ref, out_ref):
+    rows = first.shape[1]
+
+    def body(i, at):
+        sums = load_sums(sum_ref, at)
+        for ref, base in ((early_ref, 0), (late_ref, FIRST)):
+            sums = first_terms(at, ref, ref.shape[0] // rows, base, first[at, :], own[at, :], source_ref, *sums)
+        store_sums(out_ref, at, *sums)
+
+    in_steps(step, sum_ref.shape[0], body)
 
 
 def early_kernel(
-    step, white_ref, source_ref, next_ref, sum_ref, source_mark_ref, own_mark_ref, out_ref, tail_ref
+    step, white_ref, given_ref, source_ref, other_ref, next_ref, sum_ref, source_mark_ref, own_mark_ref, out_ref, tail_ref
 ):
     pairs, rows = next_ref.shape
     segs = source_mark_ref.shape[1]
     per = pairs // tail_ref.shape[0]
-    quad = NF // 2
-    next_marks = white_ref[FIRST * rows :, :LANES].astype(F32)[:segs, :rows].astype(BF)
-
-    def body(i, carry):
-        at = pl.ds(pl.multiple_of(i * step, step), step)
+    next_marks = white_ref[segs * rows :, :LANES].astype(F32)[:segs, :rows].astype(BF)
+
+    def body(i, at):
         to = pl.ds(i * (step // per), step // per)
         hot = next_ref[at, :]
-        for k, part in enumerate(add_segments(at, FIRST, 0, white_ref, source_ref, hot, sum_ref)):
-            out_ref[at, k * quad : (k + 1) * quad] = part
+        sums = more_terms(at, white_ref, segs, 0, hot, source_ref, *load_sums(sum_ref, at))
+        store_sums(out_ref, at, *more_terms(at, given_ref, FIRST, 0, hot, other_ref, *sums))
         both = source_mark_ref[at, :] * (own_mark_ref[at, :] + dot_across(hot, next_marks))
         shared = jnp.broadcast_to(jnp.sum(both, axis=1, keepdims=True), (step, LANES)).reshape(-1, per, LANES)
         tail = shared[:, :8, :]
@@ -209,41 +241,36 @@
         for k in range(1, per // 8):
             tail = jnp.where(lane >= k * 8 * LANES // per, shared[:, 8 * k : 8 * k + 8, :], tail)
         tail_ref[to, :, :] = tail
-        return carry
-
-    lax.fori_loop(0, pairs // step, body, 0)
-
-
-def late_kernel(step, white_ref, source_ref, next_ref, sum_ref, tail_ref, out_ref):
+
+    in_steps(step, pairs, body)
+
+
+def late_kernel(step, given_ref, other_ref, next_ref, sum_ref, tail_ref, out_ref):
     pairs = sum_ref.shape[0]
     per = pairs // out_ref.shape[0]
-    late = source_ref.shape[0] - FIRST
-    out_ref[:, 2 * NF // LANES * per :, :] = tail_ref[...].astype(BF)
-
-    def body(i, carry):
-        at = pl.ds(pl.multiple_of(i * step, step), step)
+    late = other_ref.shape[0] - FIRST
+    out_ref[:, 2 * per :, :] = tail_ref[...].astype(BF)
+
+    def body(i, at):
         to = pl.ds(i * (step // per), step // per)
-        for k, part in enumerate(
-            add_segments(at, late, FIRST, white_ref, source_ref, next_ref[at, :], sum_ref)
-        ):
+        sums = more_terms(at, given_ref, late, FIRST, next_ref[at, :], other_ref, *load_sums(sum_ref, at))
+        for k, part in enumerate(sums):
             out_ref[to, k * per : (k + 1) * per, :] = part.astype(BF).reshape(-1, per, LANES)
-        return carry
-
-    lax.fori_loop(0, pairs // step, body, 0)
+
+    in_steps(step, pairs, body)
 
 
 def lags_kernel(parts, per, x_ref, high_ref, low_ref, out_hbm, held, sem):
     dests, length, _ = x_ref.shape
-    blocks = 2 * NF // LANES
-    total = jnp.sum(x_ref[...].astype(F32).reshape(dests // parts, parts, length, LANES), axis=1)
-    scale = 1.0 / jnp.maximum(total[:, blocks * per :, :], 1.0)
+    total = jnp.sum(x_ref[...].astype(F32).reshape(dests // parts, parts // 2, 2, length, LANES), axis=1)
+    scale = 1.0 / jnp.maximum(total[:, 0, 2 * per :, :] + total[:, 1, 2 * per :, :], 1.0)
     scale = jnp.concatenate(
         [scale[:, :, k * 8 * LANES // per :][:, :, :1] for k in range(per // 8)], axis=1
     )
     stacked = jnp.concatenate(
         [
-            (total[:, k * per : (k + 1) * per, :] * scale).reshape(-1, LANES)
-            for k in range(blocks)
+            (total[:, k // 2, k % 2 * per : (k % 2 + 1) * per, :] * scale).reshape(-1, LANES)
+            for k in range(4)
         ],
         axis=1,
     )
@@ -281,66 +308,73 @@
     per = slots // nbr
     pairs = owners * slots
     step = min(STEP, pairs)
-    width = 2 * NF
     back = [(i, i - 1) for i in range(1, chan)]
+    swap = [(i, i ^ 1) for i in range(nbr)]
+    late = segs - FIRST
     shape = jax.ShapeDtypeStruct
     tables = forward_tables(span)
     inputs = (jnp.transpose(records, (1, 0, 2)), gap_mask.T, jnp.asarray(tables), jnp.asarray(taper()))
     extra = -(-segs // 16) * 16
-    early, rest, table, window, factors = call(
+    keep, give_early, rest, table, window, factors, mark_rows = call(
         first_kernel,
         [
-            shape((FIRST * rows + extra, width), BF),
-            shape((segs - FIRST, rows, span), F32),
+            shape((FIRST * rows, NF), BF),
+            shape((FIRST * rows, NF), BF),
+            shape((late, rows, span), F32),
             shape(tables.shape, BF),
-            shape((1, width), F32),
-            shape(((segs - FIRST) * rows, 1), F32),
+            shape((1, 2 * NF), F32),
+            shape((late * rows, 1), F32),
+            shape((extra, NF), BF),
         ],
         [pltpu.with_memory_space_constraint(v, pltpu.HBM) for v in inputs],
         [HBM] * 4,
         [
             pltpu.VMEM((FIRST, rows, span), F32),
             pltpu.VMEM((segs, rows), jnp.int32),
-            pltpu.VMEM((extra, width), F32),
+            pltpu.VMEM((extra, NF), F32),
             pltpu.SemaphoreType.DMA((5,)),
         ],
         mib=32,
     )
-    (late,) = call(
+    got_early = lax.ppermute(give_early, "nbr", swap)
+    keep, give_late = call(
         second_kernel,
-        [shape(((segs - FIRST) * rows, width), BF)],
-        (rest, table, window, factors),
-        [VMEM] * 4,
-    )
-    next_early = lax.ppermute(early, "chan", back)
-    next_late = lax.ppermute(late, "chan", back)
-    source, sums, hot, source_marks, own_marks = call(
+        [shape((segs * rows + extra, NF), BF), shape((late * rows, NF), BF)],
+        (rest, table, window, factors, keep, mark_rows),
+        [VMEM] * 6,
+    )
+    got_late = lax.ppermute(give_late, "nbr", swap)
+    next_keep = lax.ppermute(keep, "chan", back)
+    next_got_early = lax.ppermute(got_early, "chan", back)
+    next_got_late = lax.ppermute(got_late, "chan", back)
+    hots = [shape((pairs, rows), BF)] * 3
+    source, sums, first, own, hot, source_marks, own_marks = call(
         functools.partial(sources_kernel, step),
-        [
-            shape((segs, pairs, width), F32),
-            shape((pairs, width), F32),
-            shape((pairs, rows), BF),
-            shape((pairs, segs), F32),
-            shape((pairs, segs), F32),
-        ],
-        (early, late, gap_mask.T, pair_list, pair_counts),
-        [VMEM] * 4 + [SMEM],
-        [pltpu.VMEM((pairs, rows), BF), pltpu.VMEM((pairs, rows), BF)],
-        mib=40,
+        [shape((segs, pairs, NF), F32), shape((pairs, NF), F32)] + hots + [shape((pairs, segs), F32)] * 2,
+        (keep, gap_mask.T, pair_list, pair_counts),
+        [VMEM] * 3 + [SMEM],
+        mib=32,
+    )
+    other, sums = call(
+        functools.partial(given_kernel, step),
+        [shape((segs, pairs, NF), F32), shape((pairs, NF), F32)],
+        (got_early, got_late, first, own, sums),
+        [VMEM] * 5,
+        mib=32,
     )
     sums, tail = call(
         functools.partial(early_kernel, step),
-        [shape((pairs, width), F32), shape((chan * nbr, 8, LANES), F32)],
-        (next_early, source, hot, sums, source_marks, own_marks),
-        [VMEM] * 6,
-        mib=40,
+        [shape((pairs, NF), F32), shape((chan * nbr, 8, LANES), F32)],
+        (next_keep, next_got_early, source, other, hot, sums, source_marks, own_marks),
+        [VMEM] * 8,
+        mib=32,
     )
     (cross,) = call(
         functools.partial(late_kernel, step),
-        [shape((chan * nbr, width // LANES * per + 8, LANES), BF)],
-        (next_late, source, hot, sums, tail),
+        [shape((chan * nbr, 2 * per + 8, LANES), BF)],
+        (next_got_late, other, hot, sums, tail),
         [VMEM] * 5,
-        mib=40,
+        mib=32,
     )
     arrived = lax.all_to_all(cross, ("chan", "nbr"), split_axis=0, concat_axis=0, tiled=True)
     high, low = inverse_tables(span)

time: 39.4 us -> 38.9 us (0.987)
  starting transfers between devices: 3.89 us -> 10.5 us
  blocking collectives: 22.1 us -> 16.4 us
  waiting for transfers between devices: 3.54 us -> 1.89 us
    ppermute x2 -> x5, starting transfers between devices: 3.89 us -> 10.5 us  [the longest x1 3.13 us: local(): next_got_early = lax.ppermute(got_early, 'chan', back)]
    all_to_all x1, blocking collectives: 22.1 us -> 16.4 us  [local(): lax.all_to_all(cross, ('chan', 'nbr'), split_axis=0, concat_axis=0, tiled...]
    ppermute x2 -> x5, waiting for transfers between devices: 3.54 us -> 1.89 us  [the longest x1 1.75 us: local(): got_late = lax.ppermute(give_late, 'nbr', swap)]
    pallas_call x6 -> x7, Pallas kernels: 9.5 us -> 9.7 us  [call(): pl.pallas_call(kernel, out_shape=shape, in_specs=specs, out_specs=[out] *...]
  transfers between devices with their start and end apart: 2 -> 5, of which waited for: 2 -> 2; matrix products, arithmetic and copies ran while one was open for 0% -> 0% of each run, Pallas kernels for 12% -> 13%
where the time goes in v7:
time: 38.9 us; the launch traced here: 38.7 us
  blocking collectives  16.4 us (42%)
  starting transfers between devices  10.5 us (27%)
  Pallas kernels  9.7 us (25%)
  waiting for transfers between devices  1.89 us (5%)
    all_to_all x1, blocking collectives, local(): lax.all_to_all(cross, ('chan', 'nbr'), split_axis=0, concat_axis=0, tiled...  16.4 us
    pallas_call x7, Pallas kernels, call(): pl.pallas_call(kernel, out_shape=shape, in_specs=specs, out_specs=[out] *...  9.7 us
    ppermute x1, starting transfers between devices, local(): next_got_early = lax.ppermute(got_early, 'chan', back)  3.13 us
    ppermute x1, starting transfers between devices, local(): next_keep = lax.ppermute(keep, 'chan', back)  2.86 us
    ppermute x1, starting transfers between devices, local(): next_got_late = lax.ppermute(got_late, 'chan', back)  2.29 us
    ppermute x1, starting transfers between devices, local(): got_early = lax.ppermute(give_early, 'nbr', swap)  2.19 us
    ppermute x1, waiting for transfers between devices, local(): got_late = lax.ppermute(give_late, 'nbr', swap)  1.75 us
  transfers between devices with their start and end apart: 5, of which 2 were waited for; matrix products, arithmetic and copies ran while one was open for 0% of the time, Pallas kernels for 13%

profile of v7, /device:TPU:1, one launch (start us, length us, event | category | flops | bytes accessed | tf_op | source)
XLA Modules:
  0.0 38.7 jit_solution(7854575281294904589)
XLA Ops:
  0.0 0.0 copy-start.2
  0.0 0.0 copy-start.3
  0.0 0.0 copy-start.4
  0.0 3.0 %shard_map.82 = (bf16[320,256]{1,0:T(8,128)(2,1)S(1)}, bf16[320,256]{1,0:T(8,128)(2,1)S(1)}, f32[3,80,1280]{2,1,0:T(8,128)S(1)}, bf16[2,1280,256]{2,1,0:T(8,128)...) custom-call(f32[7,80,1280]{2,1,0:T(8,128)} %bitcast.5, s32[7,80]{1,0:T(8,128)} %bitcast.3, ...), custom_call_target="tpu_custom_call" | custom-call | tf_op jit(solution)/shard_map/pallas_call | solution.py:294
  3.0 2.2 %collective-permute-start.2 = (bf16[320,256]{1,0:T(8,128)(2,1)S(1)}, bf16[320,256]{1,0:T(8,128)(2,1)S(1)}, u32[]{:S(2)}, u32[]{:S(2)}) collective-permute-start(bf16[320,256]{1,0:T(8,128)(2,1)S(1)} %get-tuple-element.32), channel_id=1, source_target_pairs={{0,1},{1,0},{2,3},{3,2},{4,5},{5,4},{6,7},{7,6},{8,9},{9,8},{10,11... | collective-permute-start | bytes 491528 | tf_op jit(solution)/shard_map/ppermute | solution.py:339
  5.2 0.8 %shard_map.83 = (bf16[576,256]{1,0:T(8,128)(2,1)S(1)}, bf16[240,256]{1,0:T(8,128)(2,1)S(1)}) custom-call(f32[3,80,1280]{2,1,0:T(8,128)S(1)} %get-tuple-element.25.x_ref, bf16[2,1280,256]{2,1,0:T(8,128)(2,1)S(1)} %get-tuple-element.26.table_ref, f32[1,512]{1,0:T(1,128)S(1)} %get-tuple-element.27.window_ref, f32[240,1]{1,0:T(8,128)S(1)} %get-tuple-element.28.factor_ref, ...), custom_call_target="tpu_custom_call" | custom-call | tf_op jit(solution)/shard_map/pallas_call | solution.py:294
  6.0 2.9 %collective-permute-start.3 = (bf16[576,256]{1,0:T(8,128)(2,1)S(1)}, bf16[576,256]{1,0:T(8,128)(2,1)S(1)}, u32[]{:S(2)}, u32[]{:S(2)}) collective-permute-start(bf16[576,256]{1,0:T(8,128)(2,1)S(1)} %get-tuple-element.33.white_ref), channel_id=1, source_target_pairs={{4,0},{8,4},{12,8},{16,12},{20,16},{24,20},{28,24},{5,1},{9,5},{13... | collective-permute-start | bytes 884744 | tf_op jit(solution)/shard_map/ppermute | solution.py:347
  8.9 0.1 collective-permute-start
  9.0 0.1 collective-permute-done.2.early_ref
  9.1 3.1 %collective-permute-start.4 = (bf16[320,256]{1,0:T(8,128)(2,1)S(1)}, bf16[320,256]{1,0:T(8,128)(2,1)S(1)}, u32[]{:S(2)}, u32[]{:S(2)}) collective-permute-start(bf16[320,256]{1,0:T(8,128)(2,1)S(1)} %collective-permute-done.2.early_ref), channel_id=1, source_target_pairs={{4,0},{8,4},{12,8},{16,12},{20,16},{24,20},{28,24},{5,1},{9,5},{13... | collective-permute-start | bytes 491528 | tf_op jit(solution)/shard_map/ppermute | solution.py:348
  12.2 1.8 %collective-permute-done.late_ref = bf16[240,256]{1,0:T(8,128)(2,1)S(1)} collective-permute-done((bf16[240,256]{1,0:T(8,128)(2,1)S(1)}, bf16[240,256]{1,0:T(8,128)(2,1)S(1)}, u32[]{:S(2)}, u32[]{:S(2)}) %collective-permute-start) | collective-permute-done | bytes 122912 | tf_op jit(solution)/shard_map/ppermute | solution.py:346
  14.0 2.3 %collective-permute-start.1 = (bf16[240,256]{1,0:T(8,128)(2,1)S(1)}, bf16[240,256]{1,0:T(8,128)(2,1)S(1)}, u32[]{:S(2)}, u32[]{:S(2)}) collective-permute-start(bf16[240,256]{1,0:T(8,128)(2,1)S(1)} %collective-permute-done.late_ref), channel_id=1, source_target_pairs={{4,0},{8,4},{12,8},{16,12},{20,16},{24,20},{28,24},{5,1},{9,5},{13... | collective-permute-start | bytes 368648 | tf_op jit(solution)/shard_map/ppermute | solution.py:349
  16.3 0.0 copy-done.2
  16.3 0.0 copy-done.3
  16.3 0.0 copy-done.4
  16.3 1.9 %shard_map.84 = (f32[7,512,256]{2,1,0:T(8,128)S(1)}, f32[512,256]{1,0:T(8,128)S(1)}, bf16[512,80]{1,0:T(8,128)(2,1)S(1)}, bf16[512,80]{1,0:T(8,128)(2,1)S(1)}, b...) custom-call(bf16[576,256]{1,0:T(8,128)(2,1)S(1)} %get-tuple-element.33.white_ref, ...), custom_call_target="tpu_custom_call" | custom-call | tf_op jit(solution)/shard_map/pallas_call | solution.py:294
  18.2 1.1 %shard_map.85 = (f32[7,512,256]{2,1,0:T(8,128)S(1)}, f32[512,256]{1,0:T(8,128)S(1)}) custom-call(bf16[320,256]{1,0:T(8,128)(2,1)S(1)} %collective-permute-done.2.early_ref, bf16[240,256]{1,0:T(8,128)(2,1)S(1)} %collective-permute-done.late_ref, bf16[512,80]{1,0:T(8,128)(2,1)S(1)} %get-tuple-element.34.first, bf16[512,80]{1,0:T(8,128)(2,1)S(1)} %get-tuple-element.35.own, ...), custom_call_target="tpu_custom_call" | custom-call | tf_op jit(solution)/shard_map/pallas_call | solution.py:294
  19.3 0.0 collective-permute-done.3.white_ref
  19.3 0.0 collective-permute-done.4.given_ref
  19.4 1.1 %shard_map.86 = (f32[512,256]{1,0:T(8,128)S(1)}, f32[32,8,128]{2,1,0:T(8,128)S(1)}) custom-call(bf16[576,256]{1,0:T(8,128)(2,1)S(1)} %collective-permute-done.3.white_ref, bf16[320,256]{1,0:T(8,128)(2,1)S(1)} %collective-permute-done.4.given_ref, f32[7,512,256]{2,1,0:T(8,128)S(1)} %get-tuple-element.39.source_ref, ...), custom_call_target="tpu_custom_call" | custom-call | tf_op jit(solution)/shard_map/pallas_call | solution.py:294
  20.5 0.0 copy-start
  20.5 0.0 copy-start.1
  20.5 0.0 collective-permute-done.1.given_ref
  20.5 0.4 shard_map.87
  20.9 16.4 %all_to_all.5.x_ref = bf16[32,40,128]{2,1,0:T(8,128)(2,1)S(1)} all-to-all(bf16[32,40,128]{2,1,0:T(8,128)(2,1)S(1)} %shard_map.87), channel_id=1, replica_groups=mesh['chan'=8,'nbr'=4] {'chan','nbr'}, dimensions={0} | all-to-all | bytes 655360 | tf_op jit(solution)/shard_map/all_to_all | solution.py:379
  37.3 0.0 copy-done
  37.3 0.0 copy-done.1
  37.3 1.4 %shard_map.88 = f32[8,16,1024]{2,1,0:T(8,128)} custom-call(bf16[32,40,128]{2,1,0:T(8,128)(2,1)S(1)} %all_to_all.5.x_ref, bf16[512,1024]{1,0:T(8,128)(2,1)S(1)} %copy-done, bf16[512,1024]{1,0:T(8,128)(2,1)S(1)} %copy-done.1), custom_call_target="tpu_custom_call" | custom-call | tf_op jit(solution)/shard_map/pallas_call | solution.py:294
Async XLA Ops:
  0.0 16.3 %copy-start.2 = (s32[80,7]{0,1:T(8,128)S(1)}, s32[80,7]{0,1:T(8,128)}, u32[]{:S(2)}) copy-start(s32[80,7]{0,1:T(8,128)} %param.9) | copy-start | bytes 6724
  0.0 16.3 %copy-start.3 = (s32[1,2,8,64]{3,2,1,0:T(8,128)S(1)}, s32[1,2,8,64]{3,2,1,0:T(8,128)}, u32[]{:S(2)}) copy-start(s32[1,2,8,64]{3,2,1,0:T(8,128)} %list_ref.1) | copy-start | bytes 12292
  0.0 16.3 %copy-start.4 = (s32[1,8]{1,0:T(1,128)S(1)}, s32[1,8]{1,0:T(1,128)}, u32[]{:S(2)}) copy-start(s32[1,8]{1,0:T(1,128)} %count_ref.1) | copy-start | bytes 100
  3.0 6.1 %collective-permute-start.2 = (bf16[320,256]{1,0:T(8,128)(2,1)S(1)}, bf16[320,256]{1,0:T(8,128)(2,1)S(1)}, u32[]{:S(2)}, u32[]{:S(2)}) collective-permute-start(bf16[320,256]{1,0:T(8,128)(2,1)S(1)} %get-tuple-element.32), channel_id=1, source_target_pairs={{0,1},{1,0},{2,3},{3,2},{4,5},{5,4},{6,7},{7,6},{8,9},{9,8},{10,11... | collective-permute-start | bytes 491528 | tf_op jit(solution)/shard_map/ppermute | solution.py:339
  6.0 13.3 %collective-permute-start.3 = (bf16[576,256]{1,0:T(8,128)(2,1)S(1)}, bf16[576,256]{1,0:T(8,128)(2,1)S(1)}, u32[]{:S(2)}, u32[]{:S(2)}) collective-permute-start(bf16[576,256]{1,0:T(8,128)(2,1)S(1)} %get-tuple-element.33.white_ref), channel_id=1, source_target_pairs={{4,0},{8,4},{12,8},{16,12},{20,16},{24,20},{28,24},{5,1},{9,5},{13... | collective-permute-start | bytes 884744 | tf_op jit(solution)/shard_map/ppermute | solution.py:347
  8.9 5.1 %collective-permute-start = (bf16[240,256]{1,0:T(8,128)(2,1)S(1)}, bf16[240,256]{1,0:T(8,128)(2,1)S(1)}, u32[]{:S(2)}, u32[]{:S(2)}) collective-permute-start(bf16[240,256]{1,0:T(8,128)(2,1)S(1)} %get-tuple-element.31), channel_id=1, source_target_pairs={{0,1},{1,0},{2,3},{3,2},{4,5},{5,4},{6,7},{7,6},{8,9},{9,8},{10,11... | collective-permute-start | bytes 368648 | tf_op jit(solution)/shard_map/ppermute | solution.py:346
  9.1 10.3 %collective-permute-start.4 = (bf16[320,256]{1,0:T(8,128)(2,1)S(1)}, bf16[320,256]{1,0:T(8,128)(2,1)S(1)}, u32[]{:S(2)}, u32[]{:S(2)}) collective-permute-start(bf16[320,256]{1,0:T(8,128)(2,1)S(1)} %collective-permute-done.2.early_ref), channel_id=1, source_target_pairs={{4,0},{8,4},{12,8},{16,12},{20,16},{24,20},{28,24},{5,1},{9,5},{13... | collective-permute-start | bytes 491528 | tf_op jit(solution)/shard_map/ppermute | solution.py:348
  14.0 6.5 %collective-permute-start.1 = (bf16[240,256]{1,0:T(8,128)(2,1)S(1)}, bf16[240,256]{1,0:T(8,128)(2,1)S(1)}, u32[]{:S(2)}, u32[]{:S(2)}) collective-permute-start(bf16[240,256]{1,0:T(8,128)(2,1)S(1)} %collective-permute-done.late_ref), channel_id=1, source_target_pairs={{4,0},{8,4},{12,8},{16,12},{20,16},{24,20},{28,24},{5,1},{9,5},{13... | collective-permute-start | bytes 368648 | tf_op jit(solution)/shard_map/ppermute | solution.py:349
  20.5 16.8 %copy-start = (bf16[512,1024]{1,0:T(8,128)(2,1)S(1)}, bf16[512,1024]{1,0:T(8,128)(2,1)}, u32[]{:S(2)}) copy-start(bf16[512,1024]{1,0:T(8,128)(2,1)} %constant.10.clone.high_ref) | copy-start | bytes 3145732
  20.5 16.8 %copy-start.1 = (bf16[512,1024]{1,0:T(8,128)(2,1)S(1)}, bf16[512,1024]{1,0:T(8,128)(2,1)}, u32[]{:S(2)}) copy-start(bf16[512,1024]{1,0:T(8,128)(2,1)} %constant.11.clone.low_ref) | copy-start | bytes 3145732

commit v8 on v7

--- a/solution.py
+++ b/solution.py
@@ -290,7 +290,7 @@
         copy.wait()
 
 
-def call(kernel, shape, args, specs, scratch=(), mib=24, out=VMEM):
+def call(kernel, shape, args, specs, scratch=(), mib=24, out=VMEM, us=0):
     return pl.pallas_call(
         kernel,
         out_shape=shape,
@@ -298,6 +298,7 @@
         out_specs=[out] * len(shape),
         scratch_shapes=list(scratch),
         compiler_params=pltpu.CompilerParams(vmem_limit_bytes=mib << 20),
+        cost_estimate=pl.CostEstimate(flops=us * 10**9, bytes_accessed=us * 10**6, transcendentals=0) if us else None,
     )(*args)
 
 
@@ -342,11 +343,13 @@
         [shape((segs * rows + extra, NF), BF), shape((late * rows, NF), BF)],
         (rest, table, window, factors, keep, mark_rows),
         [VMEM] * 6,
+        us=10,
     )
     got_late = lax.ppermute(give_late, "nbr", swap)
     next_keep = lax.ppermute(keep, "chan", back)
     next_got_early = lax.ppermute(got_early, "chan", back)
-    next_got_late = lax.ppermute(got_late, "chan", back)
+    cross_over = [(i * nbr + k, (i - 1) * nbr + (k ^ 1)) for i in range(1, chan) for k in range(nbr)]
+    next_got_late = lax.ppermute(give_late, ("chan", "nbr"), cross_over)
     hots = [shape((pairs, rows), BF)] * 3
     source, sums, first, own, hot, source_marks, own_marks = call(
         functools.partial(sources_kernel, step),
@@ -361,6 +364,7 @@
         (got_early, got_late, first, own, sums),
         [VMEM] * 5,
         mib=32,
+        us=1,
     )
     sums, tail = call(
         functools.partial(early_kernel, step),

time: 38.9 us -> 38.5 us (0.990)
  waiting for transfers between devices: 1.89 us -> 1.2 us
  starting transfers between devices: 10.5 us -> 10.9 us
    ppermute x1, waiting for transfers between devices: 1.75 us -> 0.01 us  [local(): got_late = lax.ppermute(give_late, 'nbr', swap)]
    ppermute x1, waiting for transfers between devices: 0.01 us -> 1.08 us  [local(): next_got_late = lax.ppermute(give_late, ('chan', 'nbr'), cross_over)]
where the time goes in v8:
time: 38.5 us; the launch traced here: 38.3 us
  blocking collectives  16.4 us (43%)
  starting transfers between devices  10.9 us (28%)
  Pallas kernels  9.66 us (25%)
  waiting for transfers between devices  1.2 us (3%)
    all_to_all x1, blocking collectives, local(): lax.all_to_all(cross, ('chan', 'nbr'), split_axis=0, concat_axis=0, tiled...  16.4 us
    pallas_call x7, Pallas kernels, call(): pl.pallas_call(kernel, out_shape=shape, in_specs=specs, out_specs=[out] *...  9.66 us
    ppermute x1, starting transfers between devices, local(): next_got_early = lax.ppermute(got_early, 'chan', back)  3.13 us
    ppermute x1, starting transfers between devices, local(): next_keep = lax.ppermute(keep, 'chan', back)  2.86 us
    ppermute x1, starting transfers between devices, local(): next_got_late = lax.ppermute(give_late, ('chan', 'nbr'), cross_over)  2.64 us
    ppermute x1, starting transfers between devices, local(): got_early = lax.ppermute(give_early, 'nbr', swap)  2.19 us
    ppermute x1, waiting for transfers between devices, local(): next_got_late = lax.ppermute(give_late, ('chan', 'nbr'), cross_over)  1.08 us
  transfers between devices with their start and end apart: 5, of which 2 were waited for; matrix products, arithmetic and copies ran while one was open for 0% of the time, Pallas kernels for 13%

profile of v8, /device:TPU:1, one launch (start us, length us, event | category | flops | bytes accessed | tf_op | source)
XLA Modules:
  0.0 38.3 jit_solution(5674427276271507330)
XLA Ops:
  0.0 2.9 %shard_map.82 = (bf16[320,256]{1,0:T(8,128)(2,1)S(1)}, bf16[320,256]{1,0:T(8,128)(2,1)S(1)}, f32[3,80,1280]{2,1,0:T(8,128)S(1)}, bf16[2,1280,256]{2,1,0:T(8,128)...) custom-call(f32[7,80,1280]{2,1,0:T(8,128)} %bitcast.5, s32[7,80]{1,0:T(8,128)} %bitcast.3, ...), custom_call_target="tpu_custom_call" | custom-call | tf_op jit(solution)/shard_map/pallas_call | solution.py:294
  2.9 2.2 %collective-permute-start.1 = (bf16[320,256]{1,0:T(8,128)(2,1)S(1)}, bf16[320,256]{1,0:T(8,128)(2,1)S(1)}, u32[]{:S(2)}, u32[]{:S(2)}) collective-permute-start(bf16[320,256]{1,0:T(8,128)(2,1)S(1)} %get-tuple-element.32), channel_id=1, source_target_pairs={{0,1},{1,0},{2,3},{3,2},{4,5},{5,4},{6,7},{7,6},{8,9},{9,8},{10,11... | collective-permute-start | bytes 491528 | tf_op jit(solution)/shard_map/ppermute | solution.py:340
  5.1 0.0 copy-start.2
  5.1 0.0 copy-start.3
  5.1 0.0 copy-start.4
  5.1 0.8 %shard_map.83 = (bf16[576,256]{1,0:T(8,128)(2,1)S(1)}, bf16[240,256]{1,0:T(8,128)(2,1)S(1)}) custom-call(f32[3,80,1280]{2,1,0:T(8,128)S(1)} %get-tuple-element.25.x_ref, bf16[2,1280,256]{2,1,0:T(8,128)(2,1)S(1)} %get-tuple-element.26.table_ref, f32[1,512]{1,0:T(1,128)S(1)} %get-tuple-element.27.window_ref, f32[240,1]{1,0:T(8,128)S(1)} %get-tuple-element.28.factor_ref, ...), custom_call_target="tpu_custom_call" | custom-call | flops 10000000000 | bytes 10000000 | tf_op jit(solution)/shard_map/pallas_call | solution.py:294
  6.0 2.9 %collective-permute-start.3 = (bf16[576,256]{1,0:T(8,128)(2,1)S(1)}, bf16[576,256]{1,0:T(8,128)(2,1)S(1)}, u32[]{:S(2)}, u32[]{:S(2)}) collective-permute-start(bf16[576,256]{1,0:T(8,128)(2,1)S(1)} %get-tuple-element.33.white_ref), channel_id=1, source_target_pairs={{4,0},{8,4},{12,8},{16,12},{20,16},{24,20},{28,24},{5,1},{9,5},{13... | collective-permute-start | bytes 884744 | tf_op jit(solution)/shard_map/ppermute | solution.py:349
  8.9 0.1 collective-permute-start.2
  8.9 0.1 collective-permute-done.1.early_ref
  9.0 3.1 %collective-permute-start.4 = (bf16[320,256]{1,0:T(8,128)(2,1)S(1)}, bf16[320,256]{1,0:T(8,128)(2,1)S(1)}, u32[]{:S(2)}, u32[]{:S(2)}) collective-permute-start(bf16[320,256]{1,0:T(8,128)(2,1)S(1)} %collective-permute-done.1.early_ref), channel_id=1, source_target_pairs={{4,0},{8,4},{12,8},{16,12},{20,16},{24,20},{28,24},{5,1},{9,5},{13... | collective-permute-start | bytes 491528 | tf_op jit(solution)/shard_map/ppermute | solution.py:350
  12.2 2.6 %collective-permute-start = (bf16[240,256]{1,0:T(8,128)(2,1)S(1)}, bf16[240,256]{1,0:T(8,128)(2,1)S(1)}, u32[]{:S(2)}, u32[]{:S(2)}) collective-permute-start(bf16[240,256]{1,0:T(8,128)(2,1)S(1)} %get-tuple-element.31), channel_id=1, source_target_pairs={{4,1},{5,0},{6,3},{7,2},{8,5},{9,4},{10,7},{11,6},{12,9},{13,8},{1... | collective-permute-start | bytes 368648 | tf_op jit(solution)/shard_map/ppermute | solution.py:352
  14.8 0.0 copy-done.2
  14.8 0.0 copy-done.3
  14.8 0.0 copy-done.4
  14.9 1.9 %shard_map.84 = (f32[7,512,256]{2,1,0:T(8,128)S(1)}, f32[512,256]{1,0:T(8,128)S(1)}, bf16[512,80]{1,0:T(8,128)(2,1)S(1)}, bf16[512,80]{1,0:T(8,128)(2,1)S(1)}, b...) custom-call(bf16[576,256]{1,0:T(8,128)(2,1)S(1)} %get-tuple-element.33.white_ref, ...), custom_call_target="tpu_custom_call" | custom-call | tf_op jit(solution)/shard_map/pallas_call | solution.py:294
  16.8 0.0 collective-permute-done.2.late_ref
  16.8 1.1 %shard_map.85 = (f32[7,512,256]{2,1,0:T(8,128)S(1)}, f32[512,256]{1,0:T(8,128)S(1)}) custom-call(bf16[320,256]{1,0:T(8,128)(2,1)S(1)} %collective-permute-done.1.early_ref, bf16[240,256]{1,0:T(8,128)(2,1)S(1)} %collective-permute-done.2.late_ref, bf16[512,80]{1,0:T(8,128)(2,1)S(1)} %get-tuple-element.34.first, bf16[512,80]{1,0:T(8,128)(2,1)S(1)} %get-tuple-element.35.own, ...), custom_call_target="tpu_custom_call" | custom-call | flops 1000000000 | bytes 1000000 | tf_op jit(solution)/shard_map/pallas_call | solution.py:294
  17.9 0.0 collective-permute-done.3.white_ref
  17.9 0.0 collective-permute-done.4.given_ref
  17.9 1.1 %shard_map.86 = (f32[512,256]{1,0:T(8,128)S(1)}, f32[32,8,128]{2,1,0:T(8,128)S(1)}) custom-call(bf16[576,256]{1,0:T(8,128)(2,1)S(1)} %collective-permute-done.3.white_ref, bf16[320,256]{1,0:T(8,128)(2,1)S(1)} %collective-permute-done.4.given_ref, f32[7,512,256]{2,1,0:T(8,128)S(1)} %get-tuple-element.39.source_ref, ...), custom_call_target="tpu_custom_call" | custom-call | tf_op jit(solution)/shard_map/pallas_call | solution.py:294
  19.0 0.0 copy-start
  19.0 0.0 copy-start.1
  19.0 1.1 %collective-permute-done.given_ref = bf16[240,256]{1,0:T(8,128)(2,1)S(1)} collective-permute-done((bf16[240,256]{1,0:T(8,128)(2,1)S(1)}, bf16[240,256]{1,0:T(8,128)(2,1)S(1)}, u32[]{:S(2)}, u32[]{:S(2)}) %collective-permute-start) | collective-permute-done | bytes 122912 | tf_op jit(solution)/shard_map/ppermute | solution.py:352
  20.1 0.4 shard_map.87
  20.5 16.4 %all_to_all.5.x_ref = bf16[32,40,128]{2,1,0:T(8,128)(2,1)S(1)} all-to-all(bf16[32,40,128]{2,1,0:T(8,128)(2,1)S(1)} %shard_map.87), channel_id=1, replica_groups=mesh['chan'=8,'nbr'=4] {'chan','nbr'}, dimensions={0} | all-to-all | bytes 655360 | tf_op jit(solution)/shard_map/all_to_all | solution.py:383
  36.8 0.0 copy-done
  36.8 0.0 copy-done.1
  36.8 1.4 %shard_map.88 = f32[8,16,1024]{2,1,0:T(8,128)} custom-call(bf16[32,40,128]{2,1,0:T(8,128)(2,1)S(1)} %all_to_all.5.x_ref, bf16[512,1024]{1,0:T(8,128)(2,1)S(1)} %copy-done, bf16[512,1024]{1,0:T(8,128)(2,1)S(1)} %copy-done.1), custom_call_target="tpu_custom_call" | custom-call | tf_op jit(solution)/shard_map/pallas_call | solution.py:294
Async XLA Ops:
  2.9 6.1 %collective-permute-start.1 = (bf16[320,256]{1,0:T(8,128)(2,1)S(1)}, bf16[320,256]{1,0:T(8,128)(2,1)S(1)}, u32[]{:S(2)}, u32[]{:S(2)}) collective-permute-start(bf16[320,256]{1,0:T(8,128)(2,1)S(1)} %get-tuple-element.32), channel_id=1, source_target_pairs={{0,1},{1,0},{2,3},{3,2},{4,5},{5,4},{6,7},{7,6},{8,9},{9,8},{10,11... | collective-permute-start | bytes 491528 | tf_op jit(solution)/shard_map/ppermute | solution.py:340
  5.1 9.7 %copy-start.2 = (s32[80,7]{0,1:T(8,128)S(1)}, s32[80,7]{0,1:T(8,128)}, u32[]{:S(2)}) copy-start(s32[80,7]{0,1:T(8,128)} %param.9) | copy-start | bytes 6724
  5.1 9.7 %copy-start.3 = (s32[1,2,8,64]{3,2,1,0:T(8,128)S(1)}, s32[1,2,8,64]{3,2,1,0:T(8,128)}, u32[]{:S(2)}) copy-start(s32[1,2,8,64]{3,2,1,0:T(8,128)} %list_ref.1) | copy-start | bytes 12292
  5.1 9.7 %copy-start.4 = (s32[1,8]{1,0:T(1,128)S(1)}, s32[1,8]{1,0:T(1,128)}, u32[]{:S(2)}) copy-start(s32[1,8]{1,0:T(1,128)} %count_ref.1) | copy-start | bytes 100
  6.0 11.9 %collective-permute-start.3 = (bf16[576,256]{1,0:T(8,128)(2,1)S(1)}, bf16[576,256]{1,0:T(8,128)(2,1)S(1)}, u32[]{:S(2)}, u32[]{:S(2)}) collective-permute-start(bf16[576,256]{1,0:T(8,128)(2,1)S(1)} %get-tuple-element.33.white_ref), channel_id=1, source_target_pairs={{4,0},{8,4},{12,8},{16,12},{20,16},{24,20},{28,24},{5,1},{9,5},{13... | collective-permute-start | bytes 884744 | tf_op jit(solution)/shard_map/ppermute | solution.py:349
  8.9 7.9 %collective-permute-start.2 = (bf16[240,256]{1,0:T(8,128)(2,1)S(1)}, bf16[240,256]{1,0:T(8,128)(2,1)S(1)}, u32[]{:S(2)}, u32[]{:S(2)}) collective-permute-start(bf16[240,256]{1,0:T(8,128)(2,1)S(1)} %get-tuple-element.31), channel_id=1, source_target_pairs={{0,1},{1,0},{2,3},{3,2},{4,5},{5,4},{6,7},{7,6},{8,9},{9,8},{10,11... | collective-permute-start | bytes 368648 | tf_op jit(solution)/shard_map/ppermute | solution.py:348
  9.0 8.9 %collective-permute-start.4 = (bf16[320,256]{1,0:T(8,128)(2,1)S(1)}, bf16[320,256]{1,0:T(8,128)(2,1)S(1)}, u32[]{:S(2)}, u32[]{:S(2)}) collective-permute-start(bf16[320,256]{1,0:T(8,128)(2,1)S(1)} %collective-permute-done.1.early_ref), channel_id=1, source_target_pairs={{4,0},{8,4},{12,8},{16,12},{20,16},{24,20},{28,24},{5,1},{9,5},{13... | collective-permute-start | bytes 491528 | tf_op jit(solution)/shard_map/ppermute | solution.py:350
  12.2 7.9 %collective-permute-start = (bf16[240,256]{1,0:T(8,128)(2,1)S(1)}, bf16[240,256]{1,0:T(8,128)(2,1)S(1)}, u32[]{:S(2)}, u32[]{:S(2)}) collective-permute-start(bf16[240,256]{1,0:T(8,128)(2,1)S(1)} %get-tuple-element.31), channel_id=1, source_target_pairs={{4,1},{5,0},{6,3},{7,2},{8,5},{9,4},{10,7},{11,6},{12,9},{13,8},{1... | collective-permute-start | bytes 368648 | tf_op jit(solution)/shard_map/ppermute | solution.py:352
  19.0 17.8 %copy-start = (bf16[512,1024]{1,0:T(8,128)(2,1)S(1)}, bf16[512,1024]{1,0:T(8,128)(2,1)}, u32[]{:S(2)}) copy-start(bf16[512,1024]{1,0:T(8,128)(2,1)} %constant.10.clone.high_ref) | copy-start | bytes 3145732
  19.0 17.8 %copy-start.1 = (bf16[512,1024]{1,0:T(8,128)(2,1)S(1)}, bf16[512,1024]{1,0:T(8,128)(2,1)}, u32[]{:S(2)}) copy-start(bf16[512,1024]{1,0:T(8,128)(2,1)} %constant.11.clone.low_ref) | copy-start | bytes 3145732

commit v9 on v8

--- a/solution.py
+++ b/solution.py
@@ -274,14 +274,11 @@
         ],
         axis=1,
     )
-    coarse, fine = halves(stacked)
-    both = jnp.concatenate([coarse, fine], axis=0)
-    count = stacked.shape[0]
+    coarse = stacked.astype(BF)
     copies = []
     for k in range(HALVES):
         columns = slice(k * NLAG // HALVES, (k + 1) * NLAG // HALVES)
-        product = dot(both, high_ref[:, columns])
-        traces = product[:count] + product[count:] + dot(coarse, low_ref[:, columns])
+        traces = dot(coarse, high_ref[:, columns]) + dot(coarse, low_ref[:, columns])
         held[:, :, columns] = traces.reshape(held.shape[0], held.shape[1], -1)
         part = pl.ds(k * NLAG // HALVES, NLAG // HALVES)
         copies.append(pltpu.make_async_copy(held.at[:, :, part], out_hbm.at[:, :, part], sem.at[k]))

time: 38.5 us -> 38.4 us (level)
  no operation moved by 1% of the time
where the time goes in v9:
time: 38.4 us; the launch traced here: 38.1 us
  blocking collectives  16.4 us (43%)
  starting transfers between devices  10.9 us (28%)
  Pallas kernels  9.53 us (25%)
  waiting for transfers between devices  1.2 us (3%)
    all_to_all x1, blocking collectives, local(): lax.all_to_all(cross, ('chan', 'nbr'), split_axis=0, concat_axis=0, tiled...  16.4 us
    pallas_call x7, Pallas kernels, call(): pl.pallas_call(kernel, out_shape=shape, in_specs=specs, out_specs=[out] *...  9.53 us
    ppermute x1, starting transfers between devices, local(): next_got_early = lax.ppermute(got_early, 'chan', back)  3.13 us
    ppermute x1, starting transfers between devices, local(): next_keep = lax.ppermute(keep, 'chan', back)  2.86 us
    ppermute x1, starting transfers between devices, local(): next_got_late = lax.ppermute(give_late, ('chan', 'nbr'), cross_over)  2.64 us
    ppermute x1, starting transfers between devices, local(): got_early = lax.ppermute(give_early, 'nbr', swap)  2.19 us
    ppermute x1, waiting for transfers between devices, local(): next_got_late = lax.ppermute(give_late, ('chan', 'nbr'), cross_over)  1.08 us
  transfers between devices with their start and end apart: 5, of which 2 were waited for; matrix products, arithmetic and copies ran while one was open for 0% of the time, Pallas kernels for 13%

profile of v9, /device:TPU:1, one launch (start us, length us, event | category | flops | bytes accessed | tf_op | source)
XLA Modules:
  0.0 38.1 jit_solution(3967035134802840447)
XLA Ops:
  0.0 2.9 %shard_map.82 = (bf16[320,256]{1,0:T(8,128)(2,1)S(1)}, bf16[320,256]{1,0:T(8,128)(2,1)S(1)}, f32[3,80,1280]{2,1,0:T(8,128)S(1)}, bf16[2,1280,256]{2,1,0:T(8,128)...) custom-call(f32[7,80,1280]{2,1,0:T(8,128)} %bitcast.5, s32[7,80]{1,0:T(8,128)} %bitcast.3, ...), custom_call_target="tpu_custom_call" | custom-call | tf_op jit(solution)/shard_map/pallas_call | solution.py:291
  2.9 2.2 %collective-permute-start.1 = (bf16[320,256]{1,0:T(8,128)(2,1)S(1)}, bf16[320,256]{1,0:T(8,128)(2,1)S(1)}, u32[]{:S(2)}, u32[]{:S(2)}) collective-permute-start(bf16[320,256]{1,0:T(8,128)(2,1)S(1)} %get-tuple-element.32), channel_id=1, source_target_pairs={{0,1},{1,0},{2,3},{3,2},{4,5},{5,4},{6,7},{7,6},{8,9},{9,8},{10,11... | collective-permute-start | bytes 491528 | tf_op jit(solution)/shard_map/ppermute | solution.py:337
  5.1 0.0 copy-start.2
  5.1 0.0 copy-start.3
  5.1 0.0 copy-start.4
  5.1 0.8 %shard_map.83 = (bf16[576,256]{1,0:T(8,128)(2,1)S(1)}, bf16[240,256]{1,0:T(8,128)(2,1)S(1)}) custom-call(f32[3,80,1280]{2,1,0:T(8,128)S(1)} %get-tuple-element.25.x_ref, bf16[2,1280,256]{2,1,0:T(8,128)(2,1)S(1)} %get-tuple-element.26.table_ref, f32[1,512]{1,0:T(1,128)S(1)} %get-tuple-element.27.window_ref, f32[240,1]{1,0:T(8,128)S(1)} %get-tuple-element.28.factor_ref, ...), custom_call_target="tpu_custom_call" | custom-call | flops 10000000000 | bytes 10000000 | tf_op jit(solution)/shard_map/pallas_call | solution.py:291
  6.0 2.9 %collective-permute-start.3 = (bf16[576,256]{1,0:T(8,128)(2,1)S(1)}, bf16[576,256]{1,0:T(8,128)(2,1)S(1)}, u32[]{:S(2)}, u32[]{:S(2)}) collective-permute-start(bf16[576,256]{1,0:T(8,128)(2,1)S(1)} %get-tuple-element.33.white_ref), channel_id=1, source_target_pairs={{4,0},{8,4},{12,8},{16,12},{20,16},{24,20},{28,24},{5,1},{9,5},{13... | collective-permute-start | bytes 884744 | tf_op jit(solution)/shard_map/ppermute | solution.py:346
  8.9 0.1 collective-permute-start.2
  8.9 0.1 collective-permute-done.1.early_ref
  9.0 3.1 %collective-permute-start.4 = (bf16[320,256]{1,0:T(8,128)(2,1)S(1)}, bf16[320,256]{1,0:T(8,128)(2,1)S(1)}, u32[]{:S(2)}, u32[]{:S(2)}) collective-permute-start(bf16[320,256]{1,0:T(8,128)(2,1)S(1)} %collective-permute-done.1.early_ref), channel_id=1, source_target_pairs={{4,0},{8,4},{12,8},{16,12},{20,16},{24,20},{28,24},{5,1},{9,5},{13... | collective-permute-start | bytes 491528 | tf_op jit(solution)/shard_map/ppermute | solution.py:347
  12.2 2.6 %collective-permute-start = (bf16[240,256]{1,0:T(8,128)(2,1)S(1)}, bf16[240,256]{1,0:T(8,128)(2,1)S(1)}, u32[]{:S(2)}, u32[]{:S(2)}) collective-permute-start(bf16[240,256]{1,0:T(8,128)(2,1)S(1)} %get-tuple-element.31), channel_id=1, source_target_pairs={{4,1},{5,0},{6,3},{7,2},{8,5},{9,4},{10,7},{11,6},{12,9},{13,8},{1... | collective-permute-start | bytes 368648 | tf_op jit(solution)/shard_map/ppermute | solution.py:349
  14.8 0.0 copy-done.2
  14.8 0.0 copy-done.3
  14.8 0.0 copy-done.4
  14.9 1.9 %shard_map.84 = (f32[7,512,256]{2,1,0:T(8,128)S(1)}, f32[512,256]{1,0:T(8,128)S(1)}, bf16[512,80]{1,0:T(8,128)(2,1)S(1)}, bf16[512,80]{1,0:T(8,128)(2,1)S(1)}, b...) custom-call(bf16[576,256]{1,0:T(8,128)(2,1)S(1)} %get-tuple-element.33.white_ref, ...), custom_call_target="tpu_custom_call" | custom-call | tf_op jit(solution)/shard_map/pallas_call | solution.py:291
  16.8 0.0 collective-permute-done.2.late_ref
  16.8 1.1 %shard_map.85 = (f32[7,512,256]{2,1,0:T(8,128)S(1)}, f32[512,256]{1,0:T(8,128)S(1)}) custom-call(bf16[320,256]{1,0:T(8,128)(2,1)S(1)} %collective-permute-done.1.early_ref, bf16[240,256]{1,0:T(8,128)(2,1)S(1)} %collective-permute-done.2.late_ref, bf16[512,80]{1,0:T(8,128)(2,1)S(1)} %get-tuple-element.34.first, bf16[512,80]{1,0:T(8,128)(2,1)S(1)} %get-tuple-element.35.own, ...), custom_call_target="tpu_custom_call" | custom-call | flops 1000000000 | bytes 1000000 | tf_op jit(solution)/shard_map/pallas_call | solution.py:291
  17.9 0.0 collective-permute-done.3.white_ref
  17.9 0.0 collective-permute-done.4.given_ref
  17.9 1.1 %shard_map.86 = (f32[512,256]{1,0:T(8,128)S(1)}, f32[32,8,128]{2,1,0:T(8,128)S(1)}) custom-call(bf16[576,256]{1,0:T(8,128)(2,1)S(1)} %collective-permute-done.3.white_ref, bf16[320,256]{1,0:T(8,128)(2,1)S(1)} %collective-permute-done.4.given_ref, f32[7,512,256]{2,1,0:T(8,128)S(1)} %get-tuple-element.39.source_ref, ...), custom_call_target="tpu_custom_call" | custom-call | tf_op jit(solution)/shard_map/pallas_call | solution.py:291
  19.0 0.0 copy-start
  19.0 0.0 copy-start.1
  19.0 1.1 %collective-permute-done.given_ref = bf16[240,256]{1,0:T(8,128)(2,1)S(1)} collective-permute-done((bf16[240,256]{1,0:T(8,128)(2,1)S(1)}, bf16[240,256]{1,0:T(8,128)(2,1)S(1)}, u32[]{:S(2)}, u32[]{:S(2)}) %collective-permute-start) | collective-permute-done | bytes 122912 | tf_op jit(solution)/shard_map/ppermute | solution.py:349
  20.1 0.4 shard_map.87
  20.5 16.4 %all_to_all.5.x_ref = bf16[32,40,128]{2,1,0:T(8,128)(2,1)S(1)} all-to-all(bf16[32,40,128]{2,1,0:T(8,128)(2,1)S(1)} %shard_map.87), channel_id=1, replica_groups=mesh['chan'=8,'nbr'=4] {'chan','nbr'}, dimensions={0} | all-to-all | bytes 655360 | tf_op jit(solution)/shard_map/all_to_all | solution.py:380
  36.8 0.0 copy-done
  36.8 0.0 copy-done.1
  36.8 1.3 %shard_map.88 = f32[8,16,1024]{2,1,0:T(8,128)} custom-call(bf16[32,40,128]{2,1,0:T(8,128)(2,1)S(1)} %all_to_all.5.x_ref, bf16[512,1024]{1,0:T(8,128)(2,1)S(1)} %copy-done, bf16[512,1024]{1,0:T(8,128)(2,1)S(1)} %copy-done.1), custom_call_target="tpu_custom_call" | custom-call | tf_op jit(solution)/shard_map/pallas_call | solution.py:291
Async XLA Ops:
  2.9 6.1 %collective-permute-start.1 = (bf16[320,256]{1,0:T(8,128)(2,1)S(1)}, bf16[320,256]{1,0:T(8,128)(2,1)S(1)}, u32[]{:S(2)}, u32[]{:S(2)}) collective-permute-start(bf16[320,256]{1,0:T(8,128)(2,1)S(1)} %get-tuple-element.32), channel_id=1, source_target_pairs={{0,1},{1,0},{2,3},{3,2},{4,5},{5,4},{6,7},{7,6},{8,9},{9,8},{10,11... | collective-permute-start | bytes 491528 | tf_op jit(solution)/shard_map/ppermute | solution.py:337
  5.1 9.7 %copy-start.2 = (s32[80,7]{0,1:T(8,128)S(1)}, s32[80,7]{0,1:T(8,128)}, u32[]{:S(2)}) copy-start(s32[80,7]{0,1:T(8,128)} %param.9) | copy-start | bytes 6724
  5.1 9.7 %copy-start.3 = (s32[1,2,8,64]{3,2,1,0:T(8,128)S(1)}, s32[1,2,8,64]{3,2,1,0:T(8,128)}, u32[]{:S(2)}) copy-start(s32[1,2,8,64]{3,2,1,0:T(8,128)} %list_ref.1) | copy-start | bytes 12292
  5.1 9.7 %copy-start.4 = (s32[1,8]{1,0:T(1,128)S(1)}, s32[1,8]{1,0:T(1,128)}, u32[]{:S(2)}) copy-start(s32[1,8]{1,0:T(1,128)} %count_ref.1) | copy-start | bytes 100
  6.0 11.9 %collective-permute-start.3 = (bf16[576,256]{1,0:T(8,128)(2,1)S(1)}, bf16[576,256]{1,0:T(8,128)(2,1)S(1)}, u32[]{:S(2)}, u32[]{:S(2)}) collective-permute-start(bf16[576,256]{1,0:T(8,128)(2,1)S(1)} %get-tuple-element.33.white_ref), channel_id=1, source_target_pairs={{4,0},{8,4},{12,8},{16,12},{20,16},{24,20},{28,24},{5,1},{9,5},{13... | collective-permute-start | bytes 884744 | tf_op jit(solution)/shard_map/ppermute | solution.py:346
  8.9 7.9 %collective-permute-start.2 = (bf16[240,256]{1,0:T(8,128)(2,1)S(1)}, bf16[240,256]{1,0:T(8,128)(2,1)S(1)}, u32[]{:S(2)}, u32[]{:S(2)}) collective-permute-start(bf16[240,256]{1,0:T(8,128)(2,1)S(1)} %get-tuple-element.31), channel_id=1, source_target_pairs={{0,1},{1,0},{2,3},{3,2},{4,5},{5,4},{6,7},{7,6},{8,9},{9,8},{10,11... | collective-permute-start | bytes 368648 | tf_op jit(solution)/shard_map/ppermute | solution.py:345
  9.0 8.9 %collective-permute-start.4 = (bf16[320,256]{1,0:T(8,128)(2,1)S(1)}, bf16[320,256]{1,0:T(8,128)(2,1)S(1)}, u32[]{:S(2)}, u32[]{:S(2)}) collective-permute-start(bf16[320,256]{1,0:T(8,128)(2,1)S(1)} %collective-permute-done.1.early_ref), channel_id=1, source_target_pairs={{4,0},{8,4},{12,8},{16,12},{20,16},{24,20},{28,24},{5,1},{9,5},{13... | collective-permute-start | bytes 491528 | tf_op jit(solution)/shard_map/ppermute | solution.py:347
  12.2 7.9 %collective-permute-start = (bf16[240,256]{1,0:T(8,128)(2,1)S(1)}, bf16[240,256]{1,0:T(8,128)(2,1)S(1)}, u32[]{:S(2)}, u32[]{:S(2)}) collective-permute-start(bf16[240,256]{1,0:T(8,128)(2,1)S(1)} %get-tuple-element.31), channel_id=1, source_target_pairs={{4,1},{5,0},{6,3},{7,2},{8,5},{9,4},{10,7},{11,6},{12,9},{13,8},{1... | collective-permute-start | bytes 368648 | tf_op jit(solution)/shard_map/ppermute | solution.py:349
  19.0 17.8 %copy-start = (bf16[512,1024]{1,0:T(8,128)(2,1)S(1)}, bf16[512,1024]{1,0:T(8,128)(2,1)}, u32[]{:S(2)}) copy-start(bf16[512,1024]{1,0:T(8,128)(2,1)} %constant.10.clone.high_ref) | copy-start | bytes 3145732
  19.0 17.8 %copy-start.1 = (bf16[512,1024]{1,0:T(8,128)(2,1)S(1)}, bf16[512,1024]{1,0:T(8,128)(2,1)}, u32[]{:S(2)}) copy-start(bf16[512,1024]{1,0:T(8,128)(2,1)} %constant.11.clone.low_ref) | copy-start | bytes 3145732
